TPU v7x, 32 devices: a whole 2x2x4 slice. The times are simulated.
32 devices in a mesh: sub: 4 (over y, x), tm: 8 (over z, core).
Axes of the slice: x: 2, y: 2, z: 4, core: 2. Of those that a mesh axis runs over, the one named last changes fastest.
Arguments:
- streams: bfloat16 [2, 2160, 32768], P(None, 'sub', 'tm'), may hold values from -6 to 6
- beam_weights: bfloat16 [2, 100, 2160], P(None, None, 'sub'), may hold values from -0.09375 to 0.09375
- code_signs: int32 [32, 16], replicated, may hold values from 0 to 1
- gate_map: int32 [256], replicated, may hold values from 0 to 127, as said below
Outputs:
- profiles: float32 [128, 100, 128], P('tm', 'sub')
Inputs may be any that keep to these rules, and one draw needn't show every extreme that they name: `gate_map`: each range gate is named by exactly 2 sections.
All inputs are finite; a program needn't handle non-finite values.
Results may differ from a plain program's by a relative error of at most 0.0041.
Values may be sent and summed in bfloat16 or wider, within the bound.
No kernel may reach another device: no remote copies, remote signals or barrier semaphores. Data moves between devices by JAX's collectives and lax.ppermute only.
A program may use at most 128 MiB of HBM per device.

v0:
```python
import math

import jax
import jax.numpy as jnp
from jax import lax
from jax.sharding import PartitionSpec as P

PKT = 32
IPP_LEN = 512
LAGS = 64
NCODES = 32
NBAUD = 16
BAUD_LEN = 8
SEC_LEN = 2
GATES = 128
NSEC = 256


def passed_along(block, axis, distance):
    devices = range(lax.axis_size(axis))
    route = [(i - distance, i) for i in devices if i - distance in devices]
    return lax.ppermute(block, axis, route)


def complex_block(weights, count):
    w_real = weights[0]
    w_imag = weights[1]
    upper_rows = jnp.concatenate([w_real, -w_imag], 1)
    lower_rows = jnp.concatenate([w_imag, w_real], 1)
    return jnp.stack([upper_rows, lower_rows], 1).reshape(2 * count, 2 * w_real.shape[1])


def form_beams(streams, beam_weights):
    flat_rows = streams.reshape(2 * streams.shape[1], streams.shape[2])
    rows_here = beam_weights.shape[1] // lax.axis_size("sub")
    product = jnp.dot(
        complex_block(beam_weights, rows_here * lax.axis_size("sub")),
        flat_rows,
        preferred_element_type=jnp.float32,
    )
    summed = lax.psum_scatter(
        product.reshape(rows_here * lax.axis_size("sub"), 2, flat_rows.shape[1]),
        "sub",
        scatter_dimension=0,
        tiled=True,
    )
    return summed.astype(jnp.bfloat16)


def split_time(series):
    groups = lax.axis_size("tm")
    repeats = series.shape[-1] // (groups * PKT)
    return series.reshape(series.shape[:-1] + (groups, repeats, 1, PKT))


def body(streams, beam_weights, code_signs, gate_map):
    early = form_beams(streams, beam_weights)
    moved = lax.all_to_all(split_time(early), "tm", split_axis=2, concat_axis=4, tiled=True)
    beams = moved.reshape(early.shape)
    edge_samples = passed_along(beams[:, :, :LAGS], "tm", -1)
    extended = jnp.concatenate([beams, edge_samples], 2).astype(jnp.float32)
    beams_here = beams.shape[0]
    samples_here = beams.shape[2]
    periods_here = samples_here // IPP_LEN
    positions = jnp.arange(IPP_LEN + LAGS)
    baud_hot = ((positions // BAUD_LEN % NBAUD)[:, None] == jnp.arange(NBAUD)[None, :]).astype(
        jnp.float32
    )
    sign_table = (2 * code_signs - 1).astype(jnp.float32)
    baud_seq = jnp.dot(sign_table, baud_hot.T, precision=lax.Precision.HIGHEST)
    first_period = lax.axis_index("tm") * periods_here
    codes = (first_period + jnp.arange(periods_here)) % NCODES
    code_hot = (codes[:, None] == jnp.arange(NCODES)[None, :]).astype(jnp.float32)
    period_signs = jnp.dot(code_hot, baud_seq, precision=lax.Precision.HIGHEST)
    base_sign = period_signs[:, :IPP_LEN]
    section_of = jnp.arange(IPP_LEN) // SEC_LEN
    position_gate = jnp.dot(
        (section_of[:, None] == jnp.arange(NSEC)[None, :]).astype(jnp.float32),
        (gate_map[:, None] == jnp.arange(GATES)[None, :]).astype(jnp.float32),
        precision=lax.Precision.HIGHEST,
    )
    base = extended[:, :, :samples_here]
    base_real = base[:, 0]
    base_imag = base[:, 1]

    def one_lag(shift_by):
        later = lax.dynamic_slice_in_dim(extended, shift_by, samples_here, 2)
        real_part = later[:, 0] * base_real + later[:, 1] * base_imag
        imag_part = later[:, 1] * base_real - later[:, 0] * base_imag
        decode = base_sign * lax.dynamic_slice_in_dim(period_signs, shift_by, IPP_LEN, 1)
        terms = jnp.stack([real_part, imag_part], 1).reshape(beams_here * 2, periods_here, IPP_LEN)
        folded = jnp.sum(terms * decode[None, :, :], axis=1)
        return jnp.dot(folded, position_gate, precision=lax.Precision.HIGHEST)

    def lag_block(block_index):
        outputs = [one_lag(block_index * 8 + offset + 1) for offset in range(8)]
        return jnp.stack(outputs, 0)

    per_lag = lax.map(lag_block, jnp.arange(LAGS // 8))
    per_lag = per_lag.reshape(LAGS, beams_here, 2, GATES)
    all_periods = periods_here * lax.axis_size("tm")
    scale = 1.0 / math.sqrt(all_periods * IPP_LEN / GATES)
    term = per_lag.transpose(3, 1, 2, 0).reshape(GATES, beams_here, 2 * LAGS) * scale
    return lax.psum_scatter(term, "tm", scatter_dimension=0, tiled=True)


def solution(mesh):
    placed = (P(None, "sub", "tm"), P(None, None, "sub"), P(), P())
    return jax.shard_map(
        body, mesh=mesh, in_specs=placed, out_specs=P("tm", "sub", None), check_vma=False
    )
```

profile of v0, /device:TPU:0, one launch (start us, length us, event | category | flops | bytes accessed | tf_op | source)
XLA Modules:
  0.0 673.9 jit_solution(8529845959562281891)
XLA Ops:
  8.1 13.4 %copy.84 = bf16[2,540,4096]{2,1,0:T(8,128)(2,1)} copy(bf16[2,540,4096]{2,0,1:T(2,128)(2,1)} %param.6) | data formatting | bytes 17694720 | tf_op args[0]
  21.5 8.7 %reshape.284 = bf16[1080,4096,1]{1,0,2:T(8,128)(2,1)} reshape(bf16[2,540,4096]{2,1,0:T(8,128)(2,1)} %copy.84) | data formatting | bytes 17694720 | tf_op jit(solution)/shard_map/reshape | solution.py:34
  30.3 6.0 fusion.25
  36.3 2.8 copy.85
  39.1 115.9 %all-reduce.2 = bf16[100,2,4096]{2,1,0:T(2,128)(2,1)} all-reduce(f32[100,2,4096]{2,1,0:T(2,128)S(1)} %copy.85), channel_id=2, replica_groups=mesh['sub'=4,'tm'=8] {'sub'}, use_global_device_ids=true, to_apply=%region_0.0.clone | all-reduce | flops 819200 | bytes 4915200
  160.6 4.9 all-to-all-start
  166.3 12.1 %all-to-all-done = bf16[8,2,12800]{2,1,0:T(2,128)(2,1)S(1)} async-done(((bf16[8,2,12800]{2,1,0:T(2,128)(2,1)}), bf16[8,2,12800]{2,1,0:T(2,128)(2,1)S(1)}, u32[]{:S(2)}, u32[]{:S(2)}) %all-to-all-start) | async-done | bytes 409632 | tf_op jit(solution)/shard_map/all_to_all | solution.py:58
  187.7 439.6 %while.14 = (s32[]{:T(128)}, f32[8,8,50,128]{3,1,0,2:T(8,128)}, s32[8]{0:T(128)S(1)}, f32[25,2,4160]{2,1,0:T(2,128)S(1)}, f32[25,4096]{1,0:T(8,128)}, /*index=5*...) while((s32[]{:T(128)}, f32[8,8,50,128]{3,1,0,2:T(8,128)}, ...), condition=%wide.region_10.11_spmd, body=%wide.region_1.10_spmd.sunk | while | flops 324231232 | bytes 78133984 | solution.py:99
  202.8 6.0 fusion.113
  221.7 2.7 reshape.299
  230.7 2.8 reshape.297
  237.4 2.7 reshape.298
  256.1 6.0 fusion.113
  275.0 2.7 reshape.299
  284.0 2.8 reshape.297
  309.3 6.0 fusion.113
  337.2 2.8 reshape.297
  343.9 2.7 reshape.298
  362.6 6.0 fusion.113
  381.5 2.7 reshape.299
  390.5 2.8 reshape.297
  397.2 2.7 reshape.298
  415.9 6.0 fusion.113
  434.8 2.7 reshape.299
  443.8 2.8 reshape.297
  469.1 6.0 fusion.113
  497.0 2.8 reshape.297
  522.4 6.0 fusion.113
  550.3 2.8 reshape.297
  575.6 6.0 fusion.113
  603.5 2.8 reshape.297
  631.0 34.0 %reduce-scatter.2.cloned.1.call-done = f32[16,25,128]{2,1,0:T(8,128)} async-done(((f32[128,25,128]{2,1,0:T(8,128)}), f32[16,25,128]{2,1,0:T(8,128)}) %reduce-scatter.2.cloned.1.call-update) | async-done | bytes 204816 | tf_op jit(solution)/shard_map/reduce_scatter | solution.py:104
  (504 shorter events, 351.2 us)
Async XLA Ops:
  39.1 115.9 %copy-start.12 = (u32[32]{0:T(128)S(1)}, u32[32]{0:T(128)}, u32[]{:S(2)}) copy-start(u32[32]{0:T(128)} %constant.222) | copy-start | bytes 388
  158.7 6.8 %copy-start.10 = (s32[32,16]{0,1:T(8,128)S(1)}, s32[32,16]{0,1:T(8,128)}, u32[]{:S(2)}) copy-start(s32[32,16]{0,1:T(8,128)} %param.8) | copy-start | bytes 6148
  158.7 7.2 %copy-start.11 = (s32[256]{0:T(256)S(1)}, s32[256]{0:T(256)}, u32[]{:S(2)}) copy-start(s32[256]{0:T(256)} %param.9) | copy-start | bytes 3076
  160.6 17.8 %all-to-all-start = ((bf16[8,2,12800]{2,1,0:T(2,128)(2,1)}), bf16[8,2,12800]{2,1,0:T(2,128)(2,1)S(1)}, u32[]{:S(2)}, u32[]{:S(2)}) async-start(bf16[8,2,12800]{2,1,0:T(2,128)(2,1)} %reshape.287), calls=%async_computation | async-start | bytes 819200 | tf_op jit(solution)/shard_map/all_to_all | solution.py:58
  165.5 499.6 %reduce-scatter.2.cloned.1.call-start = ((), (), s32[]{:S(2)}) async-start(), calls=%async_computation.2 | async-start | bytes 2359296 | tf_op jit(solution)/shard_map/reduce_scatter | solution.py:104
  181.8 3.1 collective-permute-start
  220.2 4.3 copy-start.8
  229.2 4.3 copy-start.7
  235.9 4.3 copy-start.6
  245.8 3.0 copy-start.4
  273.5 4.3 copy-start.8
  282.5 4.3 copy-start.7
  289.1 4.3 copy-start.6
  326.7 4.3 copy-start.8
  335.7 4.3 copy-start.7
  342.4 4.3 copy-start.6
  380.0 4.3 copy-start.8
  389.0 4.3 copy-start.7
  395.7 4.3 copy-start.6
  405.6 3.0 copy-start.4
  433.2 4.3 copy-start.8
  442.2 4.3 copy-start.7
  448.9 4.3 copy-start.6
  486.5 4.3 copy-start.8
  495.5 4.3 copy-start.7
  502.2 4.3 copy-start.6
  539.7 4.3 copy-start.8
  548.7 4.3 copy-start.7
  555.4 4.3 copy-start.6
  593.0 4.3 copy-start.8
  602.0 4.3 copy-start.7
  608.6 4.3 copy-start.6
  (54 other events, 96.3 us)
Sparse Core Ops, SparseCore 0:
  631.2 33.8 reduce-scatter.1
where the time goes:
time: 680 us; the launch traced here: 674 us
  local copies, waits for them, and re-layouts  234 us (34%)
  other arithmetic  179 us (26%)
  blocking collectives  116 us (17%)
  matrix products  55.6 us (8%)
  waiting for transfers between devices  47.1 us (7%)
  loops' own time  21.4 us (3%)
  between operations  14.4 us (2%)
    unnamed x1, blocking collectives  116 us
    reshape x64, local copies, waits for them, and re-layouts, one_lag(): jnp.stack([real_part, imag_part], 1)  111 us
    reduce_sum x64, other arithmetic, one_lag(): folded = jnp.sum(terms * decode[None, :, :], axis=1)  69.9 us
    another operation x64, local copies, waits for them, and re-layouts, one_lag(): jnp.stack([real_part, imag_part], 1)  69.4 us
    dot_general x64, matrix products, one_lag(): return jnp.dot(folded, position_gate, precision=lax.Precision.HIGHEST)  48.8 us
    add x8, other arithmetic, one_lag(): real_part = later[:, 0] * base_real + later[:, 1] * base_imag  47.8 us
    another operation x32, other arithmetic, one_lag(): jnp.stack([real_part, imag_part], 1)  47.6 us
    reduce_scatter x1, waiting for transfers between devices, body(): return lax.psum_scatter(term, 'tm', scatter_dimension=0, tiled=True)  34 us
  transfers between devices with their start and end apart: 3, of which 3 were waited for; matrix products, arithmetic and copies ran while one was open for 0% of the time, Pallas kernels for 0%

commit v1 on v0

v1 whole, which is shorter than its diff:
```python
import functools
import math

import jax
import jax.numpy as jnp
from jax import lax
from jax.experimental import pallas as pl
from jax.experimental.pallas import tpu as pltpu
from jax.sharding import PartitionSpec as P

PKT = 32
IPP_LEN = 512
LAGS = 64
NCODES = 32
BAUD_LEN = 8
SEC_LEN = 2
GATES = 128
LANES = 128
BLOCKS = IPP_LEN // LANES
PER_ROW = LANES // PKT
PKTS = IPP_LEN // PKT
STREAM_MAX = 6.0
WEIGHT_MAX = 0.09375
VMEM = 48 * 1024 * 1024
F32 = jnp.float32
BF16 = jnp.bfloat16


def beam_kernel(w_ref, x_ref, out_ref, first_ref, second_ref):
    beams = w_ref.shape[1]
    half = first_ref.shape[0] // 2

    @pl.when(pl.program_id(0) == 0)
    def _():
        first_ref[:beams] = w_ref[0]
        first_ref[half : half + beams] = w_ref[1]
        second_ref[:beams] = -w_ref[1]
        second_ref[half : half + beams] = w_ref[0]

    product = jnp.dot(first_ref[...], x_ref[0], preferred_element_type=F32)
    product += jnp.dot(second_ref[...], x_ref[1], preferred_element_type=F32)
    for row in range(out_ref.shape[2]):
        piece = product[:, row * LANES : (row + 1) * LANES]
        out_ref[0, :, row, :] = piece[:beams]
        out_ref[1, :, row, :] = piece[half : half + beams]


def partial_beams(streams, beam_weights):
    beams = beam_weights.shape[1]
    depth = streams.shape[1]
    samples = streams.shape[2]
    tile = 8 * LANES
    padded = (beams + 15) // 16 * 16
    return pl.pallas_call(
        beam_kernel,
        grid=(samples // tile,),
        in_specs=[
            pl.BlockSpec((2, beams, depth), lambda t: (0, 0, 0)),
            pl.BlockSpec((2, depth, tile), lambda t: (0, 0, t)),
        ],
        out_specs=pl.BlockSpec((2, beams, 8, LANES), lambda t: (0, 0, t, 0)),
        out_shape=jax.ShapeDtypeStruct((2, beams, samples // LANES, LANES), F32),
        scratch_shapes=[pltpu.VMEM((2 * padded, depth), BF16)] * 2,
        compiler_params=pltpu.CompilerParams(vmem_limit_bytes=VMEM),
        cost_estimate=pl.CostEstimate(
            flops=8 * beams * depth * samples,
            bytes_accessed=4 * depth * samples + 8 * beams * samples,
            transcendentals=0,
        ),
        name="partial_beams",
    )(beam_weights, streams)


def lag_kernel(scale, x_ref, sign_ref, gate_ref, out_ref):
    sources, slots, _, rows, _ = x_ref.shape
    row_groups = sign_ref.shape[0]
    depth = row_groups * rows
    lane = lax.broadcasted_iota(jnp.int32, (rows, LANES), 1)
    row = lax.broadcasted_iota(jnp.int32, (rows, LANES), 0)
    flip = (
        lax.broadcasted_iota(jnp.int32, (LANES, LANES), 0)
        + lax.broadcasted_iota(jnp.int32, (LANES, LANES), 1)
        == LANES - 1
    ).astype(F32).astype(BF16)
    real_lane = lax.broadcasted_iota(jnp.int32, (LANES, LANES), 1) < LAGS

    def columns_of(slot, part):
        pieces = [x_ref[d, slot, part].astype(F32) for d in range(sources)]
        raw = []
        for group in range(row_groups):
            blocks = []
            for block in range(BLOCKS):
                total = None
                for place in range(PER_ROW):
                    packet = group * PKTS + block * PER_ROW + place
                    shift = (place - packet // sources) * PKT % LANES
                    piece = pieces[packet % sources]
                    if shift:
                        piece = pltpu.roll(piece, shift, 1)
                    total = piece if total is None else jnp.where(lane >= place * PKT, piece, total)
                blocks.append(total)
            raw.append(blocks)
        last = jnp.where(row == rows - 1, 0.0, pltpu.roll(raw[0][0], rows - 1, 0))
        columns = []
        for block in range(BLOCKS):
            columns.append([raw[group][block] * sign_ref[group] for group in range(row_groups)])
        after = [raw[group + 1][0] for group in range(row_groups - 1)] + [last]
        columns.append([after[group] * sign_ref[group] for group in range(row_groups)])
        return [jnp.concatenate(column, 0).astype(BF16) for column in columns]

    for slot in range(slots):
        real = columns_of(slot, 0)
        imag = columns_of(slot, 1)
        both = [jnp.concatenate([a, b], 0) for a, b in zip(real, imag)]
        turned = [jnp.concatenate([b, -a], 0) for a, b in zip(real, imag)]
        total = jnp.zeros((GATES, LANES), F32)
        for block in range(BLOCKS):
            base = lax.dot_general(
                flip, both[block], (((1,), (1,)), ((), ())), preferred_element_type=F32
            ).astype(BF16)
            later = jnp.concatenate(
                [both[block], both[block + 1], turned[block], turned[block + 1]], 1
            )
            gram = jnp.dot(base, later, preferred_element_type=F32)
            real_lags = pltpu.roll(gram[:, : 2 * LANES], LANES, 1, stride=1, stride_axis=0)
            imag_lags = pltpu.roll(gram[:, 2 * LANES :], LANES + LAGS, 1, stride=1, stride_axis=0)
            lags = jnp.where(real_lane, real_lags[:, :LANES], imag_lags[:, :LANES])
            high = lags.astype(BF16)
            low = (lags - high.astype(F32)).astype(BF16)
            gate = gate_ref[:, block * LANES : (block + 1) * LANES]
            total += jnp.dot(gate, high, preferred_element_type=F32)
            total += jnp.dot(gate, low, preferred_element_type=F32)
        out_ref[:, slot] = (total * scale).reshape(out_ref.shape[0], -1, LANES)


def lag_profiles(series, signs, gate_hot, scale):
    sources, slots = series.shape[:2]
    return pl.pallas_call(
        functools.partial(lag_kernel, scale),
        out_shape=jax.ShapeDtypeStruct((sources, slots, GATES // sources, LANES), F32),
        compiler_params=pltpu.CompilerParams(vmem_limit_bytes=VMEM),
        name="lag_profiles",
    )(series, signs, gate_hot)


def sign_rows(code_signs, periods, row_groups):
    signs = jnp.repeat((2 * code_signs - 1).astype(F32), BAUD_LEN, axis=1)
    signs = jnp.tile(signs, (periods // NCODES, 1))
    return signs.reshape(periods // row_groups, row_groups, LANES).transpose(1, 0, 2)


def gate_rows(gate_map):
    position = jnp.arange(IPP_LEN)
    position = position // LANES * LANES + (LANES - 1 - position % LANES)
    gates = jnp.repeat(gate_map, SEC_LEN).reshape(BLOCKS, LANES)[:, ::-1].reshape(IPP_LEN)
    return (jnp.arange(GATES)[:, None] == gates[None, :]).astype(BF16)


def body(streams, beam_weights, code_signs, gate_map):
    groups = lax.axis_size("sub")
    sources = lax.axis_size("tm")
    beams = beam_weights.shape[1] // groups
    samples = streams.shape[2]
    slots = -(-beams // sources)
    periods = samples * sources // IPP_LEN
    here = lax.axis_index("sub")
    signs = sign_rows(code_signs, periods, sources // PER_ROW)
    gate_hot = gate_rows(gate_map)

    partial = partial_beams(streams, beam_weights)
    limit = 2 * streams.shape[1] * STREAM_MAX * WEIGHT_MAX
    gain = 2.0 ** math.floor(math.log2(60000.0 / limit))

    def block_of(group):
        return lax.dynamic_slice_in_dim(partial, group * beams, beams, 1)

    summed = block_of(here)
    for step in range(groups - 1, 0, -1):
        sent = (block_of(here ^ step) * gain).astype(jnp.float16)
        came = lax.ppermute(sent, "sub", [(i, i ^ step) for i in range(groups)])
        summed = summed + came.astype(F32) * (1.0 / gain)
    early = summed.astype(BF16).transpose(1, 0, 2, 3)
    early = jnp.pad(early, ((0, sources * slots - beams), (0, 0), (0, 0), (0, 0)))
    early = early.reshape((sources, slots) + early.shape[1:])
    series = lax.all_to_all(early, "tm", 0, 0, tiled=True)
    scale = 1.0 / math.sqrt(periods * IPP_LEN / GATES)
    term = lag_profiles(series, signs, gate_hot, scale)
    arrived = lax.all_to_all(term, "tm", 0, 0, tiled=True)
    arrived = arrived.reshape((sources * slots,) + arrived.shape[2:])
    return arrived[:beams].transpose(1, 0, 2)


def solution(mesh):
    placed = (P(None, "sub", "tm"), P(None, None, "sub"), P(), P())
    return jax.shard_map(
        body, mesh=mesh, in_specs=placed, out_specs=P("tm", "sub", None), check_vma=False
    )
```

time: 680 us -> 85.8 us (0.13)
  local copies, waits for them, and re-layouts: 234 us -> 16.3 us
  other arithmetic: 179 us -> 2.76 us
  blocking collectives: 116 us -> 12.1 us
  matrix products: 55.6 us -> 0 us
  loops' own time: 21.4 us -> 0 us
  between operations: 14.4 us -> 0.11 us
  waiting for transfers between devices: 47.1 us -> 33.4 us
  Pallas kernels: 0 us -> 11.4 us
    reshape x68 -> x0, local copies, waits for them, and re-layouts: 122 us -> none  [the longest x64 111 us: one_lag(): jnp.stack([real_part, imag_part], 1)]
    unnamed x1 -> x0, blocking collectives: 116 us -> none
    another operation x72 -> x4, local copies, waits for them, and re-layouts: 70.1 us -> 0.08 us  [sign_rows(): signs = jnp.tile(signs, (periods // NCODES, 1))]
    reduce_sum x64 -> x0, other arithmetic: 69.9 us -> none  [one_lag(): folded = jnp.sum(terms * decode[None, :, :], axis=1)]
    dot_general x68 -> x0, matrix products: 55.6 us -> none  [the longest x64 48.8 us: one_lag(): return jnp.dot(folded, position_gate, precision=lax.Precision.HIGHEST)]
    add x8 -> x0, other arithmetic: 47.8 us -> none  [one_lag(): real_part = later[:, 0] * base_real + later[:, 1] * base_imag]
    another operation x33 -> x0, other arithmetic: 47.8 us -> none  [the longest x32 47.6 us: one_lag(): jnp.stack([real_part, imag_part], 1)]
    reduce_scatter x1 -> x0, waiting for transfers between devices: 34 us -> none  [body(): return lax.psum_scatter(term, 'tm', scatter_dimension=0, tiled=True)]
  transfers between devices with their start and end apart: 3 -> 4, of which waited for: 3 -> 3; matrix products, arithmetic and copies ran while one was open for 0% -> 0% of each run, Pallas kernels for 0% -> 0%
where the time goes in v1:
time: 85.8 us; the launch traced here: 85.4 us
  waiting for transfers between devices  33.4 us (39%)
  local copies, waits for them, and re-layouts  16.3 us (19%)
  blocking collectives  12.1 us (14%)
  Pallas kernels  11.4 us (13%)
  starting transfers between devices  9.34 us (11%)
  other arithmetic  2.76 us (3%)
    ppermute x3, waiting for transfers between devices, body(): came = lax.ppermute(sent, 'sub', [(i, i ^ step) for i in range(groups)])  18.5 us
    all_to_all x1, waiting for transfers between devices, body(): series = lax.all_to_all(early, 'tm', 0, 0, tiled=True)  14.9 us
    unnamed x7, local copies, waits for them, and re-layouts  14.4 us
    all_to_all x1, blocking collectives, body(): arrived = lax.all_to_all(term, 'tm', 0, 0, tiled=True)  12.1 us
    pallas_call x1, Pallas kernels, partial_beams(): pl.pallas_call(beam_kernel, grid=(samples // tile,), in_specs=[pl.BlockSp...  7.21 us
    all_to_all x1, starting transfers between devices, body(): series = lax.all_to_all(early, 'tm', 0, 0, tiled=True)  4.88 us
    ppermute x3, starting transfers between devices, body(): came = lax.ppermute(sent, 'sub', [(i, i ^ step) for i in range(groups)])  4.46 us
    pallas_call x1, Pallas kernels, lag_profiles(): pl.pallas_call(functools.partial(lag_kernel, scale), out_shape=jax.ShapeD...  4.15 us
  transfers between devices with their start and end apart: 4, of which 3 were waited for; matrix products, arithmetic and copies ran while one was open for 0% of the time, Pallas kernels for 0%

profile of v1, /device:TPU:0, one launch (start us, length us, event | category | flops | bytes accessed | tf_op | source)
XLA Modules:
  0.0 85.4 jit_solution(5887229556508388829)
XLA Ops:
  0.0 1.0 %copy.14.w_ref = bf16[2,100,540]{2,1,0:T(8,128)(2,1)S(1)} copy(bf16[2,100,540]{2,0,1:T(2,128)(2,1)} %param.5) | data formatting | bytes 432000 | tf_op args[1]
  1.0 13.4 %copy.15.x_ref = bf16[2,540,4096]{2,1,0:T(8,128)(2,1)} copy(bf16[2,540,4096]{2,0,1:T(2,128)(2,1)} %param.4) | data formatting | bytes 17694720 | tf_op args[0]
  14.3 7.2 %partial_beams.1 = f32[2,100,32,128]{3,2,1,0:T(8,128)S(1)} custom-call(bf16[2,100,540]{2,1,0:T(8,128)(2,1)S(1)} %copy.14.w_ref, bf16[2,540,4096]{2,1,0:T(8,128)(2,1)} %copy.15.x_ref), custom_call_target="tpu_custom_call" | custom-call | flops 1769472000 | bytes 12124160 | tf_op jit(solution)/shard_map/partial_beams/pallas_call | solution.py:54
  21.6 1.2 %multiply_convert_fusion.2 = (f16[2,25,32,128]{3,2,1,0:T(8,128)(2,1)}, f16[2,25,32,128]{3,2,1,0:T(8,128)(2,1)}, f16[2,25,32,128]{3,2,1,0:T(8,128)(2,1)}) fusion(f32[2,100,32,128]{3,2,1,0:T(8,128)S(1)} %partial_beams.1, s32[]{:T(128)S(6)} %select_n.13, s32[]{:T(128)S(6)} %select_n.15, s32[]{:T(128)S(6)} %select_n.14), kind=kLoop, calls=%fused_computation.3 | loop fusion | flops 1228800 | bytes 3686412 | tf_op jit(solution)/shard_map/convert_element_type | solution.py:179
  22.8 0.0 copy-start
  22.8 0.0 copy-start.1
  22.8 2.9 %collective-permute-start.2 = (f16[2,25,32,128]{3,2,1,0:T(8,128)(2,1)}, f16[2,25,32,128]{3,2,1,0:T(8,128)(2,1)}, u32[]{:S(2)}, u32[]{:S(2)}) collective-permute-start(f16[2,25,32,128]{3,2,1,0:T(8,128)(2,1)} %get-tuple-element.6), channel_id=1, source_target_pairs={{0,8},{8,0},{16,24},{24,16},{1,9},{9,1},{17,25},{25,17},{2,10},{10... | collective-permute-start | bytes 1228808 | tf_op jit(solution)/shard_map/ppermute | solution.py:180
  25.7 1.5 %collective-permute-start.1 = (f16[2,25,32,128]{3,2,1,0:T(8,128)(2,1)}, f16[2,25,32,128]{3,2,1,0:T(8,128)(2,1)}, u32[]{:S(2)}, u32[]{:S(2)}) collective-permute-start(f16[2,25,32,128]{3,2,1,0:T(8,128)(2,1)} %get-tuple-element.7), channel_id=1, source_target_pairs={{0,16},{8,24},{16,0},{24,8},{1,17},{9,25},{17,1},{25,9},{2,18},{10... | collective-permute-start | bytes 1228808 | tf_op jit(solution)/shard_map/ppermute | solution.py:180
  27.2 0.0 collective-permute-start
  27.2 9.1 %collective-permute-done.2 = f16[2,25,32,128]{3,2,1,0:T(8,128)(2,1)} collective-permute-done((f16[2,25,32,128]{3,2,1,0:T(8,128)(2,1)}, f16[2,25,32,128]{3,2,1,0:T(8,128)(2,1)}, u32[]{:S(2)}, u32[]{:S(2)}) %collective-permute-start.2) | collective-permute-done | bytes 409632 | tf_op jit(solution)/shard_map/ppermute | solution.py:180
  36.3 9.4 %collective-permute-done.1 = f16[2,25,32,128]{3,2,1,0:T(8,128)(2,1)} collective-permute-done((f16[2,25,32,128]{3,2,1,0:T(8,128)(2,1)}, f16[2,25,32,128]{3,2,1,0:T(8,128)(2,1)}, u32[]{:S(2)}, u32[]{:S(2)}) %collective-permute-start.1) | collective-permute-done | bytes 409632 | tf_op jit(solution)/shard_map/ppermute | solution.py:180
  45.7 0.0 collective-permute-done
  45.7 1.5 %fusion = bf16[25,2,32,128]{3,2,0,1:T(8,128)(2,1)S(1)} fusion(f16[2,25,32,128]{3,2,1,0:T(8,128)(2,1)} %collective-permute-done.2, f16[2,25,32,128]{3,2,1,0:T(8,128)(2,1)} %collective-permute-done.1, f16[2,25,32,128]{3,2,1,0:T(8,128)(2,1)} %collective-permute-done, f32[2,100,32,128]{3,2,1,0:T(8,128)S(1)} %partial_beams.1, s32[]{:T(128)S(6)} %select_n.12), kind=kLoop, calls=%fused_computation.4 | loop fusion | flops 2048000 | bytes 2457604 | tf_op jit(solution)/shard_map/transpose | solution.py:182
  47.3 0.9 %pad.4.clone = bf16[32,2,32,128]{3,2,1,0:T(8,128)(2,1)} pad(bf16[25,2,32,128]{3,2,1,0:T(8,128)(2,1)S(1)} %copy.21, bf16[]{:T(256)} %constant.25.clone.1), padding=0_7x0_0x0_0x0_0 | pad | bytes 933890 | tf_op jit(solution)/shard_map/jit(_pad)/pad | solution.py:183
  48.2 4.9 %all-to-all-start = ((bf16[8,4,2,32,128]{4,3,2,1,0:T(8,128)(2,1)}), bf16[8,4,2,32,128]{4,3,2,1,0:T(8,128)(2,1)S(1)}, u32[]{:S(2)}, u32[]{:S(2)}) async-start(bf16[8,4,2,32,128]{4,3,2,1,0:T(8,128)(2,1)} %bitcast.1), calls=%async_computation | async-start | bytes 1048576 | tf_op jit(solution)/shard_map/all_to_all | solution.py:185
  53.0 0.0 copy-done
  53.1 0.1 copy.17
  53.2 0.0 copy-done.1
  53.2 0.1 broadcast_in_dim.12
  53.2 0.1 copy.19
  53.4 0.1 copy.20
  53.5 14.9 %all-to-all-done.x_ref = bf16[8,4,2,32,128]{4,3,2,1,0:T(8,128)(2,1)S(1)} async-done(((bf16[8,4,2,32,128]{4,3,2,1,0:T(8,128)(2,1)}), bf16[8,4,2,32,128]{4,3,2,1,0:T(8,128)(2,1)S(1)}, u32[]{:S(2)}, u32[]{:S(2)}) %all-to-all-start) | async-done | bytes 524320 | tf_op jit(solution)/shard_map/all_to_all | solution.py:185
  68.4 4.1 %lag_profiles.1 = f32[8,4,16,128]{3,2,1,0:T(8,128)S(1)} custom-call(bf16[8,4,2,32,128]{4,3,2,1,0:T(8,128)(2,1)S(1)} %all-to-all-done.x_ref, f32[2,32,128]{2,1,0:T(8,128)S(1)} %bitcast.14, bf16[128,512]{1,0:T(8,128)(2,1)S(1)} %fusion.1.gate_ref), custom_call_target="tpu_custom_call" | custom-call | tf_op jit(solution)/shard_map/lag_profiles/pallas_call | solution.py:138
  72.6 12.1 %all_to_all.10 = f32[8,4,16,128]{3,2,1,0:T(8,128)S(1)} all-to-all(f32[8,4,16,128]{3,2,1,0:T(8,128)S(1)} %lag_profiles.1), channel_id=1, replica_groups=mesh['sub'=4,'tm'=8] {'tm'}, dimensions={0} | all-to-all | bytes 524288 | tf_op jit(solution)/shard_map/all_to_all | solution.py:188
  84.7 0.7 slice_bitcast_fusion
  (8 shorter events, 0.2 us)
Async XLA Ops:
  22.8 30.3 %copy-start = (s32[32,16]{0,1:T(8,128)S(1)}, s32[32,16]{0,1:T(8,128)}, u32[]{:S(2)}) copy-start(s32[32,16]{0,1:T(8,128)} %param.6) | copy-start | bytes 6148
  22.8 30.4 %copy-start.1 = (s32[256]{0:T(256)S(1)}, s32[256]{0:T(256)}, u32[]{:S(2)}) copy-start(s32[256]{0:T(256)} %param.7) | copy-start | bytes 3076
  22.8 13.5 %collective-permute-start.2 = (f16[2,25,32,128]{3,2,1,0:T(8,128)(2,1)}, f16[2,25,32,128]{3,2,1,0:T(8,128)(2,1)}, u32[]{:S(2)}, u32[]{:S(2)}) collective-permute-start(f16[2,25,32,128]{3,2,1,0:T(8,128)(2,1)} %get-tuple-element.6), channel_id=1, source_target_pairs={{0,8},{8,0},{16,24},{24,16},{1,9},{9,1},{17,25},{25,17},{2,10},{10... | collective-permute-start | bytes 1228808 | tf_op jit(solution)/shard_map/ppermute | solution.py:180
  25.7 20.0 %collective-permute-start.1 = (f16[2,25,32,128]{3,2,1,0:T(8,128)(2,1)}, f16[2,25,32,128]{3,2,1,0:T(8,128)(2,1)}, u32[]{:S(2)}, u32[]{:S(2)}) collective-permute-start(f16[2,25,32,128]{3,2,1,0:T(8,128)(2,1)} %get-tuple-element.7), channel_id=1, source_target_pairs={{0,16},{8,24},{16,0},{24,8},{1,17},{9,25},{17,1},{25,9},{2,18},{10... | collective-permute-start | bytes 1228808 | tf_op jit(solution)/shard_map/ppermute | solution.py:180
  27.2 18.5 %collective-permute-start = (f16[2,25,32,128]{3,2,1,0:T(8,128)(2,1)}, f16[2,25,32,128]{3,2,1,0:T(8,128)(2,1)}, u32[]{:S(2)}, u32[]{:S(2)}) collective-permute-start(f16[2,25,32,128]{3,2,1,0:T(8,128)(2,1)} %get-tuple-element.5), channel_id=1, source_target_pairs={{0,24},{8,16},{16,8},{24,0},{1,25},{9,17},{17,9},{25,1},{2,26},{10... | collective-permute-start | bytes 1228808 | tf_op jit(solution)/shard_map/ppermute | solution.py:180
  48.2 20.2 %all-to-all-start = ((bf16[8,4,2,32,128]{4,3,2,1,0:T(8,128)(2,1)}), bf16[8,4,2,32,128]{4,3,2,1,0:T(8,128)(2,1)S(1)}, u32[]{:S(2)}, u32[]{:S(2)}) async-start(bf16[8,4,2,32,128]{4,3,2,1,0:T(8,128)(2,1)} %bitcast.1), calls=%async_computation | async-start | bytes 1048576 | tf_op jit(solution)/shard_map/all_to_all | solution.py:185

commit v2 on v1

--- a/solution.py
+++ b/solution.py
@@ -22,59 +22,70 @@
 STREAM_MAX = 6.0
 WEIGHT_MAX = 0.09375
 VMEM = 48 * 1024 * 1024
+CHUNKS = 1
 F32 = jnp.float32
 BF16 = jnp.bfloat16
 
 
-def beam_kernel(w_ref, x_ref, out_ref, first_ref, second_ref):
-    beams = w_ref.shape[1]
-    half = first_ref.shape[0] // 2
-
-    @pl.when(pl.program_id(0) == 0)
-    def _():
-        first_ref[:beams] = w_ref[0]
-        first_ref[half : half + beams] = w_ref[1]
-        second_ref[:beams] = -w_ref[1]
-        second_ref[half : half + beams] = w_ref[0]
-
-    product = jnp.dot(first_ref[...], x_ref[0], preferred_element_type=F32)
-    product += jnp.dot(second_ref[...], x_ref[1], preferred_element_type=F32)
+def beam_kernel(w_ref, x_ref, out_ref):
+    beams = out_ref.shape[1]
+    depth, parts, samples = x_ref.shape
+    product = jnp.dot(
+        w_ref[...], x_ref[...].reshape(depth * parts, samples), preferred_element_type=F32
+    )
     for row in range(out_ref.shape[2]):
         piece = product[:, row * LANES : (row + 1) * LANES]
         out_ref[0, :, row, :] = piece[:beams]
-        out_ref[1, :, row, :] = piece[half : half + beams]
-
-
-def partial_beams(streams, beam_weights):
-    beams = beam_weights.shape[1]
-    depth = streams.shape[1]
-    samples = streams.shape[2]
+        out_ref[1, :, row, :] = piece[beams:]
+
+
+def partial_beams(streams, weights, chunk, chunks):
+    depth, _, samples = streams.shape
+    beams = weights.shape[0] // 2
     tile = 8 * LANES
-    padded = (beams + 15) // 16 * 16
+    tiles = samples // (tile * chunks)
     return pl.pallas_call(
         beam_kernel,
-        grid=(samples // tile,),
+        grid=(tiles,),
         in_specs=[
-            pl.BlockSpec((2, beams, depth), lambda t: (0, 0, 0)),
-            pl.BlockSpec((2, depth, tile), lambda t: (0, 0, t)),
+            pl.BlockSpec(weights.shape, lambda t: (0, 0)),
+            pl.BlockSpec((depth, 2, tile), lambda t: (0, 0, t + chunk * tiles)),
         ],
         out_specs=pl.BlockSpec((2, beams, 8, LANES), lambda t: (0, 0, t, 0)),
-        out_shape=jax.ShapeDtypeStruct((2, beams, samples // LANES, LANES), F32),
-        scratch_shapes=[pltpu.VMEM((2 * padded, depth), BF16)] * 2,
+        out_shape=jax.ShapeDtypeStruct((2, beams, tiles * 8, LANES), F32),
         compiler_params=pltpu.CompilerParams(vmem_limit_bytes=VMEM),
         cost_estimate=pl.CostEstimate(
-            flops=8 * beams * depth * samples,
-            bytes_accessed=4 * depth * samples + 8 * beams * samples,
+            flops=8 * beams * depth * samples // chunks,
+            bytes_accessed=(4 * depth * samples + 8 * beams * samples) // chunks,
             transcendentals=0,
         ),
         name="partial_beams",
-    )(beam_weights, streams)
-
-
-def lag_kernel(scale, x_ref, sign_ref, gate_ref, out_ref):
+    )(weights, streams)
+
+
+def mixed_weights(beam_weights):
+    real = beam_weights[0]
+    imag = beam_weights[1]
+    rows = jnp.concatenate([jnp.stack([real, -imag], 2), jnp.stack([imag, real], 2)], 0)
+    return rows.reshape(rows.shape[0], -1)
+
+
+def lag_kernel(scale, count, place_ref, sign_ref, gate_ref, *refs):
+    pieces_in = refs[:count]
+    out_refs = refs[count:-2]
+    x_ref, sum_ref = refs[-2:]
     sources, slots, _, rows, _ = x_ref.shape
+    chips = len(out_refs)
+    chunks = count // sources
+    chip = place_ref[0]
+    core = place_ref[1]
+    taken = pieces_in[0].shape[0] - slots
+    span = pieces_in[0].shape[2]
+    for index, ref in enumerate(pieces_in):
+        chunk, step, other = index // sources, index // 2 % chips, index % 2
+        source = 2 * (chip ^ step) + (core ^ other)
+        x_ref[source, :, :, chunk * span : (chunk + 1) * span] = ref[pl.ds(core * taken, slots)]
     row_groups = sign_ref.shape[0]
-    depth = row_groups * rows
     lane = lax.broadcasted_iota(jnp.int32, (rows, LANES), 1)
     row = lax.broadcasted_iota(jnp.int32, (rows, LANES), 0)
     flip = (
@@ -130,17 +141,60 @@
             gate = gate_ref[:, block * LANES : (block + 1) * LANES]
             total += jnp.dot(gate, high, preferred_element_type=F32)
             total += jnp.dot(gate, low, preferred_element_type=F32)
-        out_ref[:, slot] = (total * scale).reshape(out_ref.shape[0], -1, LANES)
-
-
-def lag_profiles(series, signs, gate_hot, scale):
-    sources, slots = series.shape[:2]
+        sum_ref[slot] = total * scale
+    for step, out_ref in enumerate(out_refs):
+        gates = out_ref.shape[1] * out_ref.shape[2]
+        first = pl.multiple_of((chip ^ step) * gates, gates)
+        out_ref[...] = sum_ref[:, pl.ds(first, gates), :].reshape(out_ref.shape)
+
+
+def lag_profiles(place, signs, gate_hot, pieces, sources, slots, scale):
+    chips = sources // 2
+    rows = signs.shape[1]
+    out = jax.ShapeDtypeStruct((slots, 2, GATES // sources, LANES), F32)
+    vmem = pl.BlockSpec(memory_space=pltpu.VMEM)
     return pl.pallas_call(
-        functools.partial(lag_kernel, scale),
-        out_shape=jax.ShapeDtypeStruct((sources, slots, GATES // sources, LANES), F32),
+        functools.partial(lag_kernel, scale, len(pieces)),
+        in_specs=[pl.BlockSpec(memory_space=pltpu.SMEM)] + [vmem] * (2 + len(pieces)),
+        out_specs=[vmem] * chips,
+        out_shape=[out] * chips,
+        scratch_shapes=[
+            pltpu.VMEM((sources, slots, 2, rows, LANES), BF16),
+            pltpu.VMEM((slots, GATES, LANES), F32),
+        ],
         compiler_params=pltpu.CompilerParams(vmem_limit_bytes=VMEM),
         name="lag_profiles",
-    )(series, signs, gate_hot)
+    )(place, signs, gate_hot, *pieces)
+
+
+def gather_kernel(starts, width, place_ref, *refs):
+    pieces_in = refs[:-2]
+    out_ref, held_ref = refs[-2:]
+    chips, _, slots = held_ref.shape[:3]
+    chip = place_ref[0]
+    core = place_ref[1]
+    for index, ref in enumerate(pieces_in):
+        held_ref[chip ^ (index // 2), core ^ (index % 2)] = ref[:, core]
+    for beam in range(out_ref.shape[1]):
+        owner = max(i for i in range(chips) if starts[i] <= beam)
+        offset = beam - starts[owner]
+        core_of = 0 if offset < slots else 1
+        slot = offset - core_of * (width - slots)
+        out_ref[:, beam, :] = held_ref[owner, core_of, slot]
+
+
+def gather_beams(place, pieces, starts, width, beams):
+    slots, _, gates, _ = pieces[0].shape
+    vmem = pl.BlockSpec(memory_space=pltpu.VMEM)
+    return pl.pallas_call(
+        functools.partial(gather_kernel, starts, width),
+        in_specs=[pl.BlockSpec(memory_space=pltpu.SMEM)] + [vmem] * len(pieces),
+        out_specs=vmem,
+        out_shape=jax.ShapeDtypeStruct((gates, beams, LANES), F32),
+        scratch_shapes=[pltpu.VMEM((len(starts), 2, slots, gates, LANES), F32)],
+        compiler_params=pltpu.CompilerParams(vmem_limit_bytes=VMEM),
+        name="gather_beams",
+    )(place, *pieces)
 
 
 def sign_rows(code_signs, periods, row_groups):
@@ -156,38 +210,58 @@
     return (jnp.arange(GATES)[:, None] == gates[None, :]).astype(BF16)
 
 
+def exchanged(block, axis, step):
+    return lax.ppermute(block, axis, [(i, i ^ step) for i in range(lax.axis_size(axis))])
+
+
+def spread(blocks):
+    pieces = []
+    for step, block in enumerate(blocks):
+        block = exchanged(block, "tm", 2 * step) if step else block
+        pieces += [block, exchanged(block, "tm", 1)]
+    return pieces
+
+
 def body(streams, beam_weights, code_signs, gate_map):
     groups = lax.axis_size("sub")
     sources = lax.axis_size("tm")
+    chips = sources // 2
     beams = beam_weights.shape[1] // groups
     samples = streams.shape[2]
-    slots = -(-beams // sources)
+    width = -(-beams // chips)
+    slots = -(-width // 2)
+    starts = [i * (beams - width) // (chips - 1) for i in range(chips)]
     periods = samples * sources // IPP_LEN
+    scale = 1.0 / math.sqrt(periods * IPP_LEN / GATES)
     here = lax.axis_index("sub")
+    place = jnp.stack([lax.axis_index("tm") // 2, lax.axis_index("tm") % 2]).astype(jnp.int32)
+    chip = place[0]
     signs = sign_rows(code_signs, periods, sources // PER_ROW)
     gate_hot = gate_rows(gate_map)
-
-    partial = partial_beams(streams, beam_weights)
+    weights = mixed_weights(beam_weights)
     limit = 2 * streams.shape[1] * STREAM_MAX * WEIGHT_MAX
     gain = 2.0 ** math.floor(math.log2(60000.0 / limit))
-
-    def block_of(group):
-        return lax.dynamic_slice_in_dim(partial, group * beams, beams, 1)
-
-    summed = block_of(here)
-    for step in range(groups - 1, 0, -1):
-        sent = (block_of(here ^ step) * gain).astype(jnp.float16)
-        came = lax.ppermute(sent, "sub", [(i, i ^ step) for i in range(groups)])
-        summed = summed + came.astype(F32) * (1.0 / gain)
-    early = summed.astype(BF16).transpose(1, 0, 2, 3)
-    early = jnp.pad(early, ((0, sources * slots - beams), (0, 0), (0, 0), (0, 0)))
-    early = early.reshape((sources, slots) + early.shape[1:])
-    series = lax.all_to_all(early, "tm", 0, 0, tiled=True)
-    scale = 1.0 / math.sqrt(periods * IPP_LEN / GATES)
-    term = lag_profiles(series, signs, gate_hot, scale)
-    arrived = lax.all_to_all(term, "tm", 0, 0, tiled=True)
-    arrived = arrived.reshape((sources * slots,) + arrived.shape[2:])
-    return arrived[:beams].transpose(1, 0, 2)
+    by_channel = streams.transpose(1, 0, 2)
+
+    pieces = []
+    for chunk in range(CHUNKS):
+        partial = partial_beams(by_channel, weights, chunk, CHUNKS)
+
+        def block_of(group):
+            return lax.dynamic_slice_in_dim(partial, group * beams, beams, 1)
+
+        summed = block_of(here)
+        for step in range(groups - 1, 0, -1):
+            sent = (block_of(here ^ step) * gain).astype(jnp.float16)
+            summed = summed + exchanged(sent, "sub", step).astype(F32) * (1.0 / gain)
+        early = summed.astype(BF16).transpose(1, 0, 2, 3)
+        blocks = []
+        for step in range(chips):
+            first = (chip ^ step) * (beams - width) // (chips - 1)
+            blocks.append(lax.dynamic_slice_in_dim(early, first, width, 0))
+        pieces += spread(blocks)
+    terms = lag_profiles(place, signs, gate_hot, pieces, sources, slots, scale)
+    return gather_beams(place, spread(terms), starts, width, beams)
 
 
 def solution(mesh):

time: 85.8 us -> 66.7 us (0.78)
  blocking collectives: 12.1 us -> 0 us
  local copies, waits for them, and re-layouts: 16.3 us -> 4.88 us
  starting transfers between devices: 9.34 us -> 15.2 us
  other arithmetic: 2.76 us -> 0.86 us
  Pallas kernels: 11.4 us -> 12.6 us
    all_to_all x1 -> x0, waiting for transfers between devices: 14.9 us -> none  [body(): series = lax.all_to_all(early, 'tm', 0, 0, tiled=True)]
    unnamed x7 -> x5, local copies, waits for them, and re-layouts: 14.4 us -> 0.03 us
    ppermute x3 -> x17, waiting for transfers between devices: 18.5 us -> 32.7 us  [exchanged(): lax.ppermute(block, axis, [(i, i ^ step) for i in range(lax.axis_size(axi...]
    all_to_all x1 -> x0, blocking collectives: 12.1 us -> none  [body(): arrived = lax.all_to_all(term, 'tm', 0, 0, tiled=True)]
    ppermute x3 -> x17, starting transfers between devices: 4.46 us -> 15.2 us  [exchanged(): lax.ppermute(block, axis, [(i, i ^ step) for i in range(lax.axis_size(axi...]
    all_to_all x1 -> x0, starting transfers between devices: 4.88 us -> none  [body(): series = lax.all_to_all(early, 'tm', 0, 0, tiled=True)]
    transpose x1 -> x0, other arithmetic: 1.52 us -> none  [body(): early = summed.astype(BF16).transpose(1, 0, 2, 3)]
    slice x0 -> x1, local copies, waits for them, and re-layouts: none -> 1.51 us  [mixed_weights(): imag = beam_weights[1]]
  transfers between devices with their start and end apart: 4 -> 17, of which waited for: 3 -> 10; matrix products, arithmetic and copies ran while one was open for 0% -> 1% of each run, Pallas kernels for 0% -> 0%
where the time goes in v2:
time: 66.7 us; the launch traced here: 66.5 us
  waiting for transfers between devices  32.7 us (49%)
  starting transfers between devices  15.2 us (23%)
  Pallas kernels  12.6 us (19%)
  local copies, waits for them, and re-layouts  4.88 us (7%)
  other arithmetic  0.86 us (1%)
    ppermute x17, waiting for transfers between devices, exchanged(): lax.ppermute(block, axis, [(i, i ^ step) for i in range(lax.axis_size(axi...  32.7 us
    ppermute x17, starting transfers between devices, exchanged(): lax.ppermute(block, axis, [(i, i ^ step) for i in range(lax.axis_size(axi...  15.2 us
    pallas_call x1, Pallas kernels, partial_beams(): pl.pallas_call(beam_kernel, grid=(tiles,), in_specs=[pl.BlockSpec(weights...  7.12 us
    pallas_call x1, Pallas kernels, lag_profiles(): pl.pallas_call(functools.partial(lag_kernel, scale, len(pieces)), in_spec...  4.74 us
    slice x1, local copies, waits for them, and re-layouts, mixed_weights(): imag = beam_weights[1]  1.51 us
  transfers between devices with their start and end apart: 17, of which 10 were waited for; matrix products, arithmetic and copies ran while one was open for 1% of the time, Pallas kernels for 0%

profile of v2, /device:TPU:0, one launch (start us, length us, event | category | flops | bytes accessed | tf_op | source)
XLA Modules:
  0.0 66.5 jit_solution(5749073110193877531)
XLA Ops:
  0.0 1.5 %fusion.8 = (bf16[1,100,540]{2,0,1:T(2,128)(2,1)S(1)}, bf16[1,100,540]{2,0,1:T(2,128)(2,1)S(1)}) fusion(bf16[2,100,540]{2,0,1:T(2,128)(2,1)} %param.5), kind=kLoop, calls=%fused_computation.28 | loop fusion | bytes 432000 | tf_op jit(solution)/shard_map/slice | solution.py:68
  1.7 1.0 %copy.30 = bf16[200,540,2]{0,2,1:T(2,128)(2,1)S(1)} copy(bf16[200,540,2]{1,0,2:T(8,128)(2,1)S(1)} %maximum_maximum_fusion) | data formatting | bytes 864000 | tf_op jit(solution)/shard_map/concatenate | solution.py:69
  2.6 0.5 reshape.20
  3.2 0.3 copy.31.w_ref
  3.4 7.1 %partial_beams.1 = f32[2,100,32,128]{3,2,1,0:T(8,128)S(1)} custom-call(bf16[200,1080]{1,0:T(8,128)(2,1)S(1)} %copy.31.w_ref, bf16[540,2,4096]{2,1,0:T(2,128)(2,1)} %bitcast.28), custom_call_target="tpu_custom_call" | custom-call | flops 1769472000 | bytes 12124160 | tf_op jit(solution)/shard_map/partial_beams/pallas_call | solution.py:47
  10.6 0.4 constant_dynamic-slice_fusion.2
  11.1 4.0 %collective-permute-start = (f16[2,25,32,128]{3,2,0,1:T(8,128)(2,1)S(1)}, f16[2,25,32,128]{3,2,0,1:T(8,128)(2,1)S(1)}, u32[]{:S(2)}, u32[]{:S(2)}) collective-permute-start(f16[2,25,32,128]{3,2,0,1:T(8,128)(2,1)S(1)} %fusion.2), channel_id=1, source_target_pairs={{0,24},{8,16},{16,8},{24,0},{1,25},{9,17},{17,9},{25,1},{2,26},{10... | collective-permute-start | bytes 1228808 | tf_op jit(solution)/shard_map/ppermute | solution.py:214
  15.2 0.6 collective-permute-start.1
  15.8 0.1 collective-permute-start.2
  16.4 9.0 %collective-permute-done = f16[2,25,32,128]{3,2,0,1:T(8,128)(2,1)S(1)} collective-permute-done((f16[2,25,32,128]{3,2,0,1:T(8,128)(2,1)S(1)}, f16[2,25,32,128]{3,2,0,1:T(8,128)(2,1)S(1)}, u32[]{:S(2)}, u32[]{:S(2)}) %collective-permute-start) | collective-permute-done | bytes 409632 | tf_op jit(solution)/shard_map/ppermute | solution.py:214
  25.4 7.9 %collective-permute-done.1 = f16[2,25,32,128]{3,2,0,1:T(8,128)(2,1)S(1)} collective-permute-done((f16[2,25,32,128]{3,2,0,1:T(8,128)(2,1)S(1)}, f16[2,25,32,128]{3,2,0,1:T(8,128)(2,1)S(1)}, u32[]{:S(2)}, u32[]{:S(2)}) %collective-permute-start.1) | collective-permute-done | bytes 409632 | tf_op jit(solution)/shard_map/ppermute | solution.py:214
  33.3 0.3 collective-permute-done.2
  33.6 0.3 fusion.5
  34.0 1.6 %collective-permute-start.4 = (bf16[7,2,32,128]{3,2,1,0:T(8,128)(2,1)S(1)}, bf16[7,2,32,128]{3,2,1,0:T(8,128)(2,1)S(1)}, u32[]{:S(2)}, u32[]{:S(2)}) collective-permute-start(bf16[7,2,32,128]{3,2,1,0:T(8,128)(2,1)S(1)} %get-tuple-element.21), channel_id=1, source_target_pairs={{0,2},{1,3},{2,0},{3,1},{4,6},{5,7},{6,4},{7,5},{8,10},{9,11},{10,... | collective-permute-start | bytes 344072 | tf_op jit(solution)/shard_map/ppermute | solution.py:214
  35.6 2.6 %collective-permute-start.6 = (bf16[7,2,32,128]{3,2,1,0:T(8,128)(2,1)S(1)}, bf16[7,2,32,128]{3,2,1,0:T(8,128)(2,1)S(1)}, u32[]{:S(2)}, u32[]{:S(2)}) collective-permute-start(bf16[7,2,32,128]{3,2,1,0:T(8,128)(2,1)S(1)} %get-tuple-element.20), channel_id=1, source_target_pairs={{0,4},{1,5},{2,6},{3,7},{4,0},{5,1},{6,2},{7,3},{8,12},{9,13},{10,... | collective-permute-start | bytes 344072 | tf_op jit(solution)/shard_map/ppermute | solution.py:214
  38.2 0.2 collective-permute-start.8
  38.4 0.4 collective-permute-done.4.refs_2_
  38.9 8.4 %collective-permute-done.6.refs_4_ = bf16[7,2,32,128]{3,2,1,0:T(8,128)(2,1)S(1)} collective-permute-done((bf16[7,2,32,128]{3,2,1,0:T(8,128)(2,1)S(1)}, bf16[7,2,32,128]{3,2,1,0:T(8,128)(2,1)S(1)}, u32[]{:S(2)}, u32[]{:S(2)}) %collective-permute-start.6) | collective-permute-done | bytes 114720 | tf_op jit(solution)/shard_map/ppermute | solution.py:214
  47.4 0.5 collective-permute-start.9
  48.1 0.6 collective-permute-done.7.refs_5_
  48.7 0.2 collective-permute-done.9.refs_7_
  48.9 4.7 %lag_profiles.1 = (f32[4,2,16,128]{3,2,1,0:T(8,128)S(1)}, f32[4,2,16,128]{3,2,1,0:T(8,128)S(1)}, f32[4,2,16,128]{3,2,1,0:T(8,128)S(1)}, f32[4,2,16,128]{3,2,1,0:T(8,128)S(1)}) custom-call(s32[2]{0:T(128)S(1)} %pad_add_fusion.place_ref, f32[2,32,128]{2,1,0:T(8,128)S(1)} %bitcast.27, bf16[128,512]{1,0:T(8,128)(2,1)S(1)} %fusion.6.gate_ref, ...), custom_call_target="tpu_custom_call" | custom-call | tf_op jit(solution)/shard_map/lag_profiles/pallas_call | solution.py:156
  53.6 1.7 %collective-permute-start.11 = (f32[4,2,16,128]{3,2,1,0:T(8,128)S(1)}, f32[4,2,16,128]{3,2,1,0:T(8,128)S(1)}, u32[]{:S(2)}, u32[]{:S(2)}) collective-permute-start(f32[4,2,16,128]{3,2,1,0:T(8,128)S(1)} %get-tuple-element.10), channel_id=1, source_target_pairs={{0,2},{1,3},{2,0},{3,1},{4,6},{5,7},{6,4},{7,5},{8,10},{9,11},{10,... | collective-permute-start | bytes 196616 | tf_op jit(solution)/shard_map/ppermute | solution.py:214
  55.3 1.4 %collective-permute-start.13 = (f32[4,2,16,128]{3,2,1,0:T(8,128)S(1)}, f32[4,2,16,128]{3,2,1,0:T(8,128)S(1)}, u32[]{:S(2)}, u32[]{:S(2)}) collective-permute-start(f32[4,2,16,128]{3,2,1,0:T(8,128)S(1)} %get-tuple-element.11), channel_id=1, source_target_pairs={{0,4},{1,5},{2,6},{3,7},{4,0},{5,1},{6,2},{7,3},{8,12},{9,13},{10,... | collective-permute-start | bytes 196616 | tf_op jit(solution)/shard_map/ppermute | solution.py:214
  56.7 1.4 %collective-permute-start.15 = (f32[4,2,16,128]{3,2,1,0:T(8,128)S(1)}, f32[4,2,16,128]{3,2,1,0:T(8,128)S(1)}, u32[]{:S(2)}, u32[]{:S(2)}) collective-permute-start(f32[4,2,16,128]{3,2,1,0:T(8,128)S(1)} %get-tuple-element.12), channel_id=1, source_target_pairs={{0,6},{1,7},{2,4},{3,5},{4,2},{5,3},{6,0},{7,1},{8,14},{9,15},{10,... | collective-permute-start | bytes 196616 | tf_op jit(solution)/shard_map/ppermute | solution.py:214
  58.1 0.5 collective-permute-start.12
  58.6 5.0 %collective-permute-done.13.refs_4_ = f32[4,2,16,128]{3,2,1,0:T(8,128)S(1)} collective-permute-done((f32[4,2,16,128]{3,2,1,0:T(8,128)S(1)}, f32[4,2,16,128]{3,2,1,0:T(8,128)S(1)}, u32[]{:S(2)}, u32[]{:S(2)}) %collective-permute-start.13) | collective-permute-done | bytes 65568 | tf_op jit(solution)/shard_map/ppermute | solution.py:214
  63.6 0.5 collective-permute-start.16
  64.1 0.7 %collective-permute-done.14.refs_5_ = f32[4,2,16,128]{3,2,1,0:T(8,128)S(1)} collective-permute-done((f32[4,2,16,128]{3,2,1,0:T(8,128)S(1)}, f32[4,2,16,128]{3,2,1,0:T(8,128)S(1)}, u32[]{:S(2)}, u32[]{:S(2)}) %collective-permute-start.14) | collective-permute-done | bytes 65568 | tf_op jit(solution)/shard_map/ppermute | solution.py:214
  64.8 0.2 collective-permute-done.16.refs_7_
  65.0 0.7 %gather_beams.1 = f32[16,25,128]{2,1,0:T(8,128)S(1)} custom-call(s32[2]{0:T(128)S(1)} %pad_add_fusion.place_ref, f32[4,2,16,128]{3,2,1,0:T(8,128)S(1)} %get-tuple-element.9.refs_0_, f32[4,2,16,128]{3,2,1,0:T(8,128)S(1)} %collective-permute-done.10.refs_1_, f32[4,2,16,128]{3,2,1,0:T(8,128)S(1)} %collective-permute-done.11.refs_2_, ...), custom_call_target="tpu_custom_call" | custom-call | tf_op jit(solution)/shard_map/gather_beams/pallas_call | solution.py:189
  65.7 0.8 %copy.36 = f32[16,25,128]{2,0,1:T(8,128)} copy(f32[16,25,128]{2,1,0:T(8,128)S(1)} %gather_beams.1) | data formatting | bytes 409600 | tf_op jit(solution)/shard_map/gather_beams/pallas_call | solution.py:189
  (35 shorter events, 1.1 us)
Async XLA Ops:
  11.0 5.1 %copy-start.1 = (s32[256]{0:T(256)S(1)}, s32[256]{0:T(256)}, u32[]{:S(2)}) copy-start(s32[256]{0:T(256)} %param.7) | copy-start | bytes 3076
  11.1 27.3 %copy-start = (s32[32,16]{0,1:T(8,128)S(1)}, s32[32,16]{0,1:T(8,128)}, u32[]{:S(2)}) copy-start(s32[32,16]{0,1:T(8,128)} %param.6) | copy-start | bytes 6148
  11.1 14.3 %collective-permute-start = (f16[2,25,32,128]{3,2,0,1:T(8,128)(2,1)S(1)}, f16[2,25,32,128]{3,2,0,1:T(8,128)(2,1)S(1)}, u32[]{:S(2)}, u32[]{:S(2)}) collective-permute-start(f16[2,25,32,128]{3,2,0,1:T(8,128)(2,1)S(1)} %fusion.2), channel_id=1, source_target_pairs={{0,24},{8,16},{16,8},{24,0},{1,25},{9,17},{17,9},{25,1},{2,26},{10... | collective-permute-start | bytes 1228808 | tf_op jit(solution)/shard_map/ppermute | solution.py:214
  15.2 18.1 %collective-permute-start.1 = (f16[2,25,32,128]{3,2,0,1:T(8,128)(2,1)S(1)}, f16[2,25,32,128]{3,2,0,1:T(8,128)(2,1)S(1)}, u32[]{:S(2)}, u32[]{:S(2)}) collective-permute-start(f16[2,25,32,128]{3,2,0,1:T(8,128)(2,1)S(1)} %fusion.1), channel_id=1, source_target_pairs={{0,16},{8,24},{16,0},{24,8},{1,17},{9,25},{17,1},{25,9},{2,18},{10... | collective-permute-start | bytes 1228808 | tf_op jit(solution)/shard_map/ppermute | solution.py:214
  15.8 17.8 %collective-permute-start.2 = (f16[2,25,32,128]{3,2,0,1:T(8,128)(2,1)S(1)}, f16[2,25,32,128]{3,2,0,1:T(8,128)(2,1)S(1)}, u32[]{:S(2)}, u32[]{:S(2)}) collective-permute-start(f16[2,25,32,128]{3,2,0,1:T(8,128)(2,1)S(1)} %fusion), channel_id=1, source_target_pairs={{0,8},{8,0},{16,24},{24,16},{1,9},{9,1},{17,25},{25,17},{2,10},{10... | collective-permute-start | bytes 1228808 | tf_op jit(solution)/shard_map/ppermute | solution.py:214
  34.0 4.9 %collective-permute-start.4 = (bf16[7,2,32,128]{3,2,1,0:T(8,128)(2,1)S(1)}, bf16[7,2,32,128]{3,2,1,0:T(8,128)(2,1)S(1)}, u32[]{:S(2)}, u32[]{:S(2)}) collective-permute-start(bf16[7,2,32,128]{3,2,1,0:T(8,128)(2,1)S(1)} %get-tuple-element.21), channel_id=1, source_target_pairs={{0,2},{1,3},{2,0},{3,1},{4,6},{5,7},{6,4},{7,5},{8,10},{9,11},{10,... | collective-permute-start | bytes 344072 | tf_op jit(solution)/shard_map/ppermute | solution.py:214
  35.6 11.8 %collective-permute-start.6 = (bf16[7,2,32,128]{3,2,1,0:T(8,128)(2,1)S(1)}, bf16[7,2,32,128]{3,2,1,0:T(8,128)(2,1)S(1)}, u32[]{:S(2)}, u32[]{:S(2)}) collective-permute-start(bf16[7,2,32,128]{3,2,1,0:T(8,128)(2,1)S(1)} %get-tuple-element.20), channel_id=1, source_target_pairs={{0,4},{1,5},{2,6},{3,7},{4,0},{5,1},{6,2},{7,3},{8,12},{9,13},{10,... | collective-permute-start | bytes 344072 | tf_op jit(solution)/shard_map/ppermute | solution.py:214
  38.2 9.2 %collective-permute-start.8 = (bf16[7,2,32,128]{3,2,1,0:T(8,128)(2,1)S(1)}, bf16[7,2,32,128]{3,2,1,0:T(8,128)(2,1)S(1)}, u32[]{:S(2)}, u32[]{:S(2)}) collective-permute-start(bf16[7,2,32,128]{3,2,1,0:T(8,128)(2,1)S(1)} %get-tuple-element.19), channel_id=1, source_target_pairs={{0,6},{1,7},{2,4},{3,5},{4,2},{5,3},{6,0},{7,1},{8,14},{9,15},{10,... | collective-permute-start | bytes 344072 | tf_op jit(solution)/shard_map/ppermute | solution.py:214
  38.4 9.6 %collective-permute-start.3 = (bf16[7,2,32,128]{3,2,1,0:T(8,128)(2,1)S(1)}, bf16[7,2,32,128]{3,2,1,0:T(8,128)(2,1)S(1)}, u32[]{:S(2)}, u32[]{:S(2)}) collective-permute-start(bf16[7,2,32,128]{3,2,1,0:T(8,128)(2,1)S(1)} %get-tuple-element.22.refs_0_), channel_id=1, source_target_pairs={{0,1},{1,0},{2,3},{3,2},{4,5},{5,4},{6,7},{7,6},{8,9},{9,8},{10,11... | collective-permute-start | bytes 344072 | tf_op jit(solution)/shard_map/ppermute | solution.py:214
  38.9 9.2 %collective-permute-start.5 = (bf16[7,2,32,128]{3,2,1,0:T(8,128)(2,1)S(1)}, bf16[7,2,32,128]{3,2,1,0:T(8,128)(2,1)S(1)}, u32[]{:S(2)}, u32[]{:S(2)}) collective-permute-start(bf16[7,2,32,128]{3,2,1,0:T(8,128)(2,1)S(1)} %collective-permute-done.4.refs_2_), channel_id=1, source_target_pairs={{0,1},{1,0},{2,3},{3,2},{4,5},{5,4},{6,7},{7,6},{8,9},{9,8},{10,11... | collective-permute-start | bytes 344072 | tf_op jit(solution)/shard_map/ppermute | solution.py:214
  47.4 1.3 %collective-permute-start.7 = (bf16[7,2,32,128]{3,2,1,0:T(8,128)(2,1)S(1)}, bf16[7,2,32,128]{3,2,1,0:T(8,128)(2,1)S(1)}, u32[]{:S(2)}, u32[]{:S(2)}) collective-permute-start(bf16[7,2,32,128]{3,2,1,0:T(8,128)(2,1)S(1)} %collective-permute-done.6.refs_4_), channel_id=1, source_target_pairs={{0,1},{1,0},{2,3},{3,2},{4,5},{5,4},{6,7},{7,6},{8,9},{9,8},{10,11... | collective-permute-start | bytes 344072 | tf_op jit(solution)/shard_map/ppermute | solution.py:214
  47.4 1.5 %collective-permute-start.9 = (bf16[7,2,32,128]{3,2,1,0:T(8,128)(2,1)S(1)}, bf16[7,2,32,128]{3,2,1,0:T(8,128)(2,1)S(1)}, u32[]{:S(2)}, u32[]{:S(2)}) collective-permute-start(bf16[7,2,32,128]{3,2,1,0:T(8,128)(2,1)S(1)} %collective-permute-done.8.refs_6_), channel_id=1, source_target_pairs={{0,1},{1,0},{2,3},{3,2},{4,5},{5,4},{6,7},{7,6},{8,9},{9,8},{10,11... | collective-permute-start | bytes 344072 | tf_op jit(solution)/shard_map/ppermute | solution.py:214
  53.6 4.5 %collective-permute-start.11 = (f32[4,2,16,128]{3,2,1,0:T(8,128)S(1)}, f32[4,2,16,128]{3,2,1,0:T(8,128)S(1)}, u32[]{:S(2)}, u32[]{:S(2)}) collective-permute-start(f32[4,2,16,128]{3,2,1,0:T(8,128)S(1)} %get-tuple-element.10), channel_id=1, source_target_pairs={{0,2},{1,3},{2,0},{3,1},{4,6},{5,7},{6,4},{7,5},{8,10},{9,11},{10,... | collective-permute-start | bytes 196616 | tf_op jit(solution)/shard_map/ppermute | solution.py:214
  55.3 8.2 %collective-permute-start.13 = (f32[4,2,16,128]{3,2,1,0:T(8,128)S(1)}, f32[4,2,16,128]{3,2,1,0:T(8,128)S(1)}, u32[]{:S(2)}, u32[]{:S(2)}) collective-permute-start(f32[4,2,16,128]{3,2,1,0:T(8,128)S(1)} %get-tuple-element.11), channel_id=1, source_target_pairs={{0,4},{1,5},{2,6},{3,7},{4,0},{5,1},{6,2},{7,3},{8,12},{9,13},{10,... | collective-permute-start | bytes 196616 | tf_op jit(solution)/shard_map/ppermute | solution.py:214
  56.7 6.9 %collective-permute-start.15 = (f32[4,2,16,128]{3,2,1,0:T(8,128)S(1)}, f32[4,2,16,128]{3,2,1,0:T(8,128)S(1)}, u32[]{:S(2)}, u32[]{:S(2)}) collective-permute-start(f32[4,2,16,128]{3,2,1,0:T(8,128)S(1)} %get-tuple-element.12), channel_id=1, source_target_pairs={{0,6},{1,7},{2,4},{3,5},{4,2},{5,3},{6,0},{7,1},{8,14},{9,15},{10,... | collective-permute-start | bytes 196616 | tf_op jit(solution)/shard_map/ppermute | solution.py:214
  58.1 6.0 %collective-permute-start.10 = (f32[4,2,16,128]{3,2,1,0:T(8,128)S(1)}, f32[4,2,16,128]{3,2,1,0:T(8,128)S(1)}, u32[]{:S(2)}, u32[]{:S(2)}) collective-permute-start(f32[4,2,16,128]{3,2,1,0:T(8,128)S(1)} %get-tuple-element.9.refs_0_), channel_id=1, source_target_pairs={{0,1},{1,0},{2,3},{3,2},{4,5},{5,4},{6,7},{7,6},{8,9},{9,8},{10,11... | collective-permute-start | bytes 196616 | tf_op jit(solution)/shard_map/ppermute | solution.py:214
  58.1 6.0 %collective-permute-start.12 = (f32[4,2,16,128]{3,2,1,0:T(8,128)S(1)}, f32[4,2,16,128]{3,2,1,0:T(8,128)S(1)}, u32[]{:S(2)}, u32[]{:S(2)}) collective-permute-start(f32[4,2,16,128]{3,2,1,0:T(8,128)S(1)} %collective-permute-done.11.refs_2_), channel_id=1, source_target_pairs={{0,1},{1,0},{2,3},{3,2},{4,5},{5,4},{6,7},{7,6},{8,9},{9,8},{10,11... | collective-permute-start | bytes 196616 | tf_op jit(solution)/shard_map/ppermute | solution.py:214
  63.6 1.3 %collective-permute-start.14 = (f32[4,2,16,128]{3,2,1,0:T(8,128)S(1)}, f32[4,2,16,128]{3,2,1,0:T(8,128)S(1)}, u32[]{:S(2)}, u32[]{:S(2)}) collective-permute-start(f32[4,2,16,128]{3,2,1,0:T(8,128)S(1)} %collective-permute-done.13.refs_4_), channel_id=1, source_target_pairs={{0,1},{1,0},{2,3},{3,2},{4,5},{5,4},{6,7},{7,6},{8,9},{9,8},{10,11... | collective-permute-start | bytes 196616 | tf_op jit(solution)/shard_map/ppermute | solution.py:214
  63.6 1.4 %collective-permute-start.16 = (f32[4,2,16,128]{3,2,1,0:T(8,128)S(1)}, f32[4,2,16,128]{3,2,1,0:T(8,128)S(1)}, u32[]{:S(2)}, u32[]{:S(2)}) collective-permute-start(f32[4,2,16,128]{3,2,1,0:T(8,128)S(1)} %collective-permute-done.15.refs_6_), channel_id=1, source_target_pairs={{0,1},{1,0},{2,3},{3,2},{4,5},{5,4},{6,7},{7,6},{8,9},{9,8},{10,11... | collective-permute-start | bytes 196616 | tf_op jit(solution)/shard_map/ppermute | solution.py:214

commit v3 on v2

--- a/solution.py
+++ b/solution.py
@@ -22,37 +22,70 @@
 STREAM_MAX = 6.0
 WEIGHT_MAX = 0.09375
 VMEM = 48 * 1024 * 1024
-CHUNKS = 1
+CHUNKS = 2
 F32 = jnp.float32
 BF16 = jnp.bfloat16
 
 
-def beam_kernel(w_ref, x_ref, out_ref):
-    beams = out_ref.shape[1]
-    depth, parts, samples = x_ref.shape
+def beam_kernel(w_ref, x_ref, out_ref, first_ref, second_ref, mixed_ref):
+    beams, _, depth = w_ref.shape
+    samples = x_ref.shape[2]
+    rows = mixed_ref.shape[0]
+    half = rows // 2
+
+    @pl.when(pl.program_id(0) == 0)
+    def _():
+        first_ref[...] = jnp.zeros_like(first_ref)
+        second_ref[...] = jnp.zeros_like(second_ref)
+        weights = w_ref[...].astype(F32)
+        real = weights[:, 0, :]
+        imag = weights[:, 1, :]
+        first_ref[:beams, :depth] = real
+        first_ref[half : half + beams, :depth] = imag
+        second_ref[:beams, :depth] = -imag
+        second_ref[half : half + beams, :depth] = real
+        source = lax.broadcasted_iota(jnp.int32, (2 * LANES, 2 * LANES), 0)
+        target = lax.broadcasted_iota(jnp.int32, (2 * LANES, 2 * LANES), 1)
+        weave = source % LANES * 2 + source // LANES == target
+        weave = weave.astype(F32).astype(BF16)
+        for block in range(first_ref.shape[1] // LANES):
+            columns = slice(block * LANES, (block + 1) * LANES)
+            pair = jnp.concatenate([first_ref[:, columns], second_ref[:, columns]], 1)
+            woven = jnp.dot(pair.astype(BF16), weave, preferred_element_type=F32)
+            mixed_ref[:, 2 * block * LANES : 2 * (block + 1) * LANES] = woven.astype(BF16)
+
     product = jnp.dot(
-        w_ref[...], x_ref[...].reshape(depth * parts, samples), preferred_element_type=F32
+        mixed_ref[:, : 2 * depth],
+        x_ref[...].reshape(2 * depth, samples),
+        preferred_element_type=F32,
     )
     for row in range(out_ref.shape[2]):
         piece = product[:, row * LANES : (row + 1) * LANES]
         out_ref[0, :, row, :] = piece[:beams]
-        out_ref[1, :, row, :] = piece[beams:]
+        out_ref[1, :, row, :] = piece[half : half + beams]
 
 
 def partial_beams(streams, weights, chunk, chunks):
     depth, _, samples = streams.shape
-    beams = weights.shape[0] // 2
+    beams = weights.shape[0]
     tile = 8 * LANES
     tiles = samples // (tile * chunks)
+    rows = 2 * (-(-beams // 8) * 8)
+    columns = -(-depth // LANES) * LANES
     return pl.pallas_call(
         beam_kernel,
         grid=(tiles,),
         in_specs=[
-            pl.BlockSpec(weights.shape, lambda t: (0, 0)),
+            pl.BlockSpec(weights.shape, lambda t: (0, 0, 0)),
             pl.BlockSpec((depth, 2, tile), lambda t: (0, 0, t + chunk * tiles)),
         ],
         out_specs=pl.BlockSpec((2, beams, 8, LANES), lambda t: (0, 0, t, 0)),
         out_shape=jax.ShapeDtypeStruct((2, beams, tiles * 8, LANES), F32),
+        scratch_shapes=[
+            pltpu.VMEM((rows, columns), F32),
+            pltpu.VMEM((rows, columns), F32),
+            pltpu.VMEM((rows, 2 * columns), BF16),
+        ],
         compiler_params=pltpu.CompilerParams(vmem_limit_bytes=VMEM),
         cost_estimate=pl.CostEstimate(
             flops=8 * beams * depth * samples // chunks,
@@ -61,13 +94,6 @@
         ),
         name="partial_beams",
     )(weights, streams)
-
-
-def mixed_weights(beam_weights):
-    real = beam_weights[0]
-    imag = beam_weights[1]
-    rows = jnp.concatenate([jnp.stack([real, -imag], 2), jnp.stack([imag, real], 2)], 0)
-    return rows.reshape(rows.shape[0], -1)
 
 
 def lag_kernel(scale, count, place_ref, sign_ref, gate_ref, *refs):
@@ -145,13 +171,13 @@
     for step, out_ref in enumerate(out_refs):
         gates = out_ref.shape[1] * out_ref.shape[2]
         first = pl.multiple_of((chip ^ step) * gates, gates)
-        out_ref[...] = sum_ref[:, pl.ds(first, gates), :].reshape(out_ref.shape)
+        out_ref[...] = sum_ref[:, pl.ds(first, gates), :].reshape(out_ref.shape).astype(BF16)
 
 
 def lag_profiles(place, signs, gate_hot, pieces, sources, slots, scale):
     chips = sources // 2
     rows = signs.shape[1]
-    out = jax.ShapeDtypeStruct((slots, 2, GATES // sources, LANES), F32)
+    out = jax.ShapeDtypeStruct((slots, 2, GATES // sources, LANES), BF16)
     vmem = pl.BlockSpec(memory_space=pltpu.VMEM)
     return pl.pallas_call(
         functools.partial(lag_kernel, scale, len(pieces)),
@@ -174,13 +200,13 @@
     chip = place_ref[0]
     core = place_ref[1]
     for index, ref in enumerate(pieces_in):
-        held_ref[chip ^ (index // 2), core ^ (index % 2)] = ref[:, core]
-    for beam in range(out_ref.shape[1]):
+        held_ref[chip ^ (index // 2), core ^ (index % 2)] = ref[:, core].astype(F32)
+    for beam in range(out_ref.shape[0]):
         owner = max(i for i in range(chips) if starts[i] <= beam)
         offset = beam - starts[owner]
         core_of = 0 if offset < slots else 1
         slot = offset - core_of * (width - slots)
-        out_ref[:, beam, :] = held_ref[owner, core_of, slot]
+        out_ref[beam] = held_ref[owner, core_of, slot]
 
 
 def gather_beams(place, pieces, starts, width, beams):
@@ -190,7 +216,7 @@
         functools.partial(gather_kernel, starts, width),
         in_specs=[pl.BlockSpec(memory_space=pltpu.SMEM)] + [vmem] * len(pieces),
         out_specs=vmem,
-        out_shape=jax.ShapeDtypeStruct((gates, beams, LANES), F32),
+        out_shape=jax.ShapeDtypeStruct((beams, gates, LANES), F32),
         scratch_shapes=[pltpu.VMEM((len(starts), 2, slots, gates, LANES), F32)],
         compiler_params=pltpu.CompilerParams(vmem_limit_bytes=VMEM),
         name="gather_beams",
@@ -238,22 +264,25 @@
     chip = place[0]
     signs = sign_rows(code_signs, periods, sources // PER_ROW)
     gate_hot = gate_rows(gate_map)
-    weights = mixed_weights(beam_weights)
+    weights = beam_weights.transpose(1, 0, 2)
     limit = 2 * streams.shape[1] * STREAM_MAX * WEIGHT_MAX
     gain = 2.0 ** math.floor(math.log2(60000.0 / limit))
     by_channel = streams.transpose(1, 0, 2)
 
+    def block_of(array, group):
+        return lax.dynamic_slice_in_dim(array, group * beams, beams, 1)
+
     pieces = []
     for chunk in range(CHUNKS):
         partial = partial_beams(by_channel, weights, chunk, CHUNKS)
-
-        def block_of(group):
-            return lax.dynamic_slice_in_dim(partial, group * beams, beams, 1)
-
-        summed = block_of(here)
+        sent = []
         for step in range(groups - 1, 0, -1):
-            sent = (block_of(here ^ step) * gain).astype(jnp.float16)
-            summed = summed + exchanged(sent, "sub", step).astype(F32) * (1.0 / gain)
+            sent.append((block_of(partial, here ^ step) * gain).astype(jnp.float16))
+        *sent, weights = lax.optimization_barrier((*sent, weights))
+        summed = block_of(partial, here)
+        for step in range(groups - 1, 0, -1):
+            came = exchanged(sent[groups - 1 - step], "sub", step)
+            summed = summed + came.astype(F32) * (1.0 / gain)
         early = summed.astype(BF16).transpose(1, 0, 2, 3)
         blocks = []
         for step in range(chips):
@@ -261,7 +290,7 @@
             blocks.append(lax.dynamic_slice_in_dim(early, first, width, 0))
         pieces += spread(blocks)
     terms = lag_profiles(place, signs, gate_hot, pieces, sources, slots, scale)
-    return gather_beams(place, spread(terms), starts, width, beams)
+    return gather_beams(place, spread(terms), starts, width, beams).transpose(1, 0, 2)
 
 
 def solution(mesh):

time: 66.7 us -> 55.9 us (0.84)
  waiting for transfers between devices: 32.7 us -> 12.6 us
  starting transfers between devices: 15.2 us -> 24.8 us
  local copies, waits for them, and re-layouts: 4.88 us -> 1.62 us
  Pallas kernels: 12.6 us -> 15.8 us
    ppermute x17 -> x27, waiting for transfers between devices: 32.7 us -> 12.6 us  [exchanged(): lax.ppermute(block, axis, [(i, i ^ step) for i in range(lax.axis_size(axi...]
    ppermute x17 -> x27, starting transfers between devices: 15.2 us -> 24.8 us  [exchanged(): lax.ppermute(block, axis, [(i, i ^ step) for i in range(lax.axis_size(axi...]
    pallas_call x1 -> x2, Pallas kernels: 7.12 us -> 9.8 us  [partial_beams(): pl.pallas_call(beam_kernel, grid=(tiles,), in_specs=[pl.BlockSpec(weights...]
    slice x1 -> x0, local copies, waits for them, and re-layouts: 1.51 us -> none  [mixed_weights(): imag = beam_weights[1]]
    concatenate x1 -> x0, local copies, waits for them, and re-layouts: 0.96 us -> none  [mixed_weights(): jnp.concatenate([jnp.stack([real, -imag], 2), jnp.stack([imag, real], 2)]...]
    unnamed x5 -> x6, local copies, waits for them, and re-layouts: 0.03 us -> 0.96 us
    pallas_call x1 -> x0, local copies, waits for them, and re-layouts: 0.8 us -> none  [gather_beams(): pl.pallas_call(functools.partial(gather_kernel, starts, width), in_specs=...]
    reshape x2 -> x0, local copies, waits for them, and re-layouts: 0.78 us -> none  [mixed_weights(): return rows.reshape(rows.shape[0], -1)]
  transfers between devices with their start and end apart: 17 -> 27, of which waited for: 10 -> 15; matrix products, arithmetic and copies ran while one was open for 1% -> 2% of each run, Pallas kernels for 0% -> 9%
where the time goes in v3:
time: 55.9 us; the launch traced here: 55.7 us
  starting transfers between devices  24.8 us (44%)
  Pallas kernels  15.8 us (28%)
  waiting for transfers between devices  12.6 us (23%)
  local copies, waits for them, and re-layouts  1.62 us (3%)
  other arithmetic  0.74 us (1%)
    ppermute x27, starting transfers between devices, exchanged(): lax.ppermute(block, axis, [(i, i ^ step) for i in range(lax.axis_size(axi...  24.8 us
    ppermute x27, waiting for transfers between devices, exchanged(): lax.ppermute(block, axis, [(i, i ^ step) for i in range(lax.axis_size(axi...  12.6 us
    pallas_call x2, Pallas kernels, partial_beams(): pl.pallas_call(beam_kernel, grid=(tiles,), in_specs=[pl.BlockSpec(weights...  9.8 us
    pallas_call x1, Pallas kernels, lag_profiles(): pl.pallas_call(functools.partial(lag_kernel, scale, len(pieces)), in_spec...  4.74 us
    pallas_call x1, Pallas kernels, gather_beams(): pl.pallas_call(functools.partial(gather_kernel, starts, width), in_specs=...  1.26 us
  transfers between devices with their start and end apart: 27, of which 15 were waited for; matrix products, arithmetic and copies ran while one was open for 2% of the time, Pallas kernels for 9%

profile of v3, /device:TPU:0, one launch (start us, length us, event | category | flops | bytes accessed | tf_op | source)
XLA Modules:
  0.0 55.7 jit_solution(9630615048504128728)
XLA Ops:
  0.0 0.9 %copy-done = bf16[2,100,540]{2,0,1:T(2,128)(2,1)S(1)} copy-done((bf16[2,100,540]{2,0,1:T(2,128)(2,1)S(1)}, bf16[2,100,540]{2,0,1:T(2,128)(2,1)}, u32[]{:S(2)}) %copy-start) | copy-done | bytes 216024
  0.9 4.9 %partial_beams.2 = f32[2,100,16,128]{3,2,1,0:T(8,128)S(1)} custom-call(bf16[100,2,540]{2,1,0:T(2,128)(2,1)S(1)} %bitcast.29, bf16[540,2,4096]{2,1,0:T(2,128)(2,1)} %bitcast.32), custom_call_target="tpu_custom_call" | custom-call | flops 884736000 | bytes 6062080 | tf_op jit(solution)/shard_map/partial_beams/pallas_call | solution.py:75
  6.1 4.0 %collective-permute-start = (f16[2,25,16,128]{3,2,0,1:T(8,128)(2,1)S(1)}, f16[2,25,16,128]{3,2,0,1:T(8,128)(2,1)S(1)}, u32[]{:S(2)}, u32[]{:S(2)}) collective-permute-start(f16[2,25,16,128]{3,2,0,1:T(8,128)(2,1)S(1)} %fusion.8), channel_id=1, source_target_pairs={{0,24},{8,16},{16,8},{24,0},{1,25},{9,17},{17,9},{25,1},{2,26},{10... | collective-permute-start | bytes 614408 | tf_op jit(solution)/shard_map/ppermute | solution.py:240
  10.1 0.5 collective-permute-start.1
  10.7 4.9 %partial_beams.3 = f32[2,100,16,128]{3,2,1,0:T(8,128)S(1)} custom-call(bf16[100,2,540]{2,1,0:T(2,128)(2,1)S(1)} %bitcast.30, bf16[540,2,4096]{2,1,0:T(2,128)(2,1)} %bitcast.33), custom_call_target="tpu_custom_call" | custom-call | flops 884736000 | bytes 6062080 | tf_op jit(solution)/shard_map/partial_beams/pallas_call | solution.py:75
  16.0 2.9 %collective-permute-start.10 = (f16[2,25,16,128]{3,2,0,1:T(8,128)(2,1)S(1)}, f16[2,25,16,128]{3,2,0,1:T(8,128)(2,1)S(1)}, u32[]{:S(2)}, u32[]{:S(2)}) collective-permute-start(f16[2,25,16,128]{3,2,0,1:T(8,128)(2,1)S(1)} %fusion.2), channel_id=1, source_target_pairs={{0,24},{8,16},{16,8},{24,0},{1,25},{9,17},{17,9},{25,1},{2,26},{10... | collective-permute-start | bytes 614408 | tf_op jit(solution)/shard_map/ppermute | solution.py:240
  18.9 0.5 collective-permute-start.11
  19.8 0.2 collective-permute-start.12
  20.0 0.3 collective-permute-done.1
  20.2 0.4 collective-permute-done.2
  20.9 3.7 %collective-permute-start.8 = (bf16[7,2,16,128]{3,2,1,0:T(8,128)(2,1)S(1)}, bf16[7,2,16,128]{3,2,1,0:T(8,128)(2,1)S(1)}, u32[]{:S(2)}, u32[]{:S(2)}) collective-permute-start(bf16[7,2,16,128]{3,2,1,0:T(8,128)(2,1)S(1)} %get-tuple-element.39), channel_id=1, source_target_pairs={{0,6},{1,7},{2,4},{3,5},{4,2},{5,3},{6,0},{7,1},{8,14},{9,15},{10,... | collective-permute-start | bytes 172040 | tf_op jit(solution)/shard_map/ppermute | solution.py:240
  24.6 0.4 collective-permute-done.10
  25.0 2.0 %collective-permute-start.4 = (bf16[7,2,16,128]{3,2,1,0:T(8,128)(2,1)S(1)}, bf16[7,2,16,128]{3,2,1,0:T(8,128)(2,1)S(1)}, u32[]{:S(2)}, u32[]{:S(2)}) collective-permute-start(bf16[7,2,16,128]{3,2,1,0:T(8,128)(2,1)S(1)} %get-tuple-element.41), channel_id=1, source_target_pairs={{0,2},{1,3},{2,0},{3,1},{4,6},{5,7},{6,4},{7,5},{8,10},{9,11},{10,... | collective-permute-start | bytes 172040 | tf_op jit(solution)/shard_map/ppermute | solution.py:240
  27.0 1.4 %collective-permute-done.11 = f16[2,25,16,128]{3,2,0,1:T(8,128)(2,1)S(1)} collective-permute-done((f16[2,25,16,128]{3,2,0,1:T(8,128)(2,1)S(1)}, f16[2,25,16,128]{3,2,0,1:T(8,128)(2,1)S(1)}, u32[]{:S(2)}, u32[]{:S(2)}) %collective-permute-start.11) | collective-permute-done | bytes 204832 | tf_op jit(solution)/shard_map/ppermute | solution.py:240
  28.3 0.3 collective-permute-done.12
  28.9 3.7 %collective-permute-start.18 = (bf16[7,2,16,128]{3,2,1,0:T(8,128)(2,1)S(1)}, bf16[7,2,16,128]{3,2,1,0:T(8,128)(2,1)S(1)}, u32[]{:S(2)}, u32[]{:S(2)}) collective-permute-start(bf16[7,2,16,128]{3,2,1,0:T(8,128)(2,1)S(1)} %get-tuple-element.35), channel_id=1, source_target_pairs={{0,6},{1,7},{2,4},{3,5},{4,2},{5,3},{6,0},{7,1},{8,14},{9,15},{10,... | collective-permute-start | bytes 172040 | tf_op jit(solution)/shard_map/ppermute | solution.py:240
  32.6 0.8 %collective-permute-start.14 = (bf16[7,2,16,128]{3,2,1,0:T(8,128)(2,1)S(1)}, bf16[7,2,16,128]{3,2,1,0:T(8,128)(2,1)S(1)}, u32[]{:S(2)}, u32[]{:S(2)}) collective-permute-start(bf16[7,2,16,128]{3,2,1,0:T(8,128)(2,1)S(1)} %get-tuple-element.37), channel_id=1, source_target_pairs={{0,2},{1,3},{2,0},{3,1},{4,6},{5,7},{6,4},{7,5},{8,10},{9,11},{10,... | collective-permute-start | bytes 172040 | tf_op jit(solution)/shard_map/ppermute | solution.py:240
  33.4 0.5 collective-permute-start.9
  34.0 1.1 %collective-permute-done.18.refs_14_ = bf16[7,2,16,128]{3,2,1,0:T(8,128)(2,1)S(1)} collective-permute-done((bf16[7,2,16,128]{3,2,1,0:T(8,128)(2,1)S(1)}, bf16[7,2,16,128]{3,2,1,0:T(8,128)(2,1)S(1)}, u32[]{:S(2)}, u32[]{:S(2)}) %collective-permute-start.18) | collective-permute-done | bytes 57376 | tf_op jit(solution)/shard_map/ppermute | solution.py:240
  35.1 2.9 %collective-permute-done.16.refs_12_ = bf16[7,2,16,128]{3,2,1,0:T(8,128)(2,1)S(1)} collective-permute-done((bf16[7,2,16,128]{3,2,1,0:T(8,128)(2,1)S(1)}, bf16[7,2,16,128]{3,2,1,0:T(8,128)(2,1)S(1)}, u32[]{:S(2)}, u32[]{:S(2)}) %collective-permute-start.16) | collective-permute-done | bytes 57376 | tf_op jit(solution)/shard_map/ppermute | solution.py:240
  38.1 0.4 collective-permute-start.19
  38.6 0.4 collective-permute-start.15
  39.4 0.4 collective-permute-done.17.refs_13_
  39.9 4.7 %lag_profiles.1 = (bf16[4,2,16,128]{3,2,1,0:T(8,128)(2,1)S(1)}, bf16[4,2,16,128]{3,2,1,0:T(8,128)(2,1)S(1)}, bf16[4,2,16,128]{3,2,1,0:T(8,128)(2,1)S(1)}, bf16[4,2,16,128]{3,2,1,0:T(8,128)(2,1)S(1)}) custom-call(s32[2]{0:T(128)S(1)} %pad_add_fusion.place_ref, f32[2,32,128]{2,1,0:T(8,128)S(1)} %bitcast.31, bf16[128,512]{1,0:T(8,128)(2,1)S(1)} %fusion.12.gate_ref, ...), custom_call_target="tpu_custom_call" | custom-call | tf_op jit(solution)/shard_map/lag_profiles/pallas_call | solution.py:182
  44.7 1.2 %collective-permute-start.21 = (bf16[4,2,16,128]{3,2,1,0:T(8,128)(2,1)S(1)}, bf16[4,2,16,128]{3,2,1,0:T(8,128)(2,1)S(1)}, u32[]{:S(2)}, u32[]{:S(2)}) collective-permute-start(bf16[4,2,16,128]{3,2,1,0:T(8,128)(2,1)S(1)} %get-tuple-element.24), channel_id=1, source_target_pairs={{0,2},{1,3},{2,0},{3,1},{4,6},{5,7},{6,4},{7,5},{8,10},{9,11},{10,... | collective-permute-start | bytes 98312 | tf_op jit(solution)/shard_map/ppermute | solution.py:240
  45.8 1.7 %collective-permute-start.23 = (bf16[4,2,16,128]{3,2,1,0:T(8,128)(2,1)S(1)}, bf16[4,2,16,128]{3,2,1,0:T(8,128)(2,1)S(1)}, u32[]{:S(2)}, u32[]{:S(2)}) collective-permute-start(bf16[4,2,16,128]{3,2,1,0:T(8,128)(2,1)S(1)} %get-tuple-element.25), channel_id=1, source_target_pairs={{0,4},{1,5},{2,6},{3,7},{4,0},{5,1},{6,2},{7,3},{8,12},{9,13},{10,... | collective-permute-start | bytes 98312 | tf_op jit(solution)/shard_map/ppermute | solution.py:240
  47.6 1.5 %collective-permute-start.25 = (bf16[4,2,16,128]{3,2,1,0:T(8,128)(2,1)S(1)}, bf16[4,2,16,128]{3,2,1,0:T(8,128)(2,1)S(1)}, u32[]{:S(2)}, u32[]{:S(2)}) collective-permute-start(bf16[4,2,16,128]{3,2,1,0:T(8,128)(2,1)S(1)} %get-tuple-element.26), channel_id=1, source_target_pairs={{0,6},{1,7},{2,4},{3,5},{4,2},{5,3},{6,0},{7,1},{8,14},{9,15},{10,... | collective-permute-start | bytes 98312 | tf_op jit(solution)/shard_map/ppermute | solution.py:240
  49.1 0.5 collective-permute-start.22
  49.6 1.5 %collective-permute-done.23.refs_4_ = bf16[4,2,16,128]{3,2,1,0:T(8,128)(2,1)S(1)} collective-permute-done((bf16[4,2,16,128]{3,2,1,0:T(8,128)(2,1)S(1)}, bf16[4,2,16,128]{3,2,1,0:T(8,128)(2,1)S(1)}, u32[]{:S(2)}, u32[]{:S(2)}) %collective-permute-start.23) | collective-permute-done | bytes 32800 | tf_op jit(solution)/shard_map/ppermute | solution.py:240
  51.2 2.1 %collective-permute-done.25.refs_6_ = bf16[4,2,16,128]{3,2,1,0:T(8,128)(2,1)S(1)} collective-permute-done((bf16[4,2,16,128]{3,2,1,0:T(8,128)(2,1)S(1)}, bf16[4,2,16,128]{3,2,1,0:T(8,128)(2,1)S(1)}, u32[]{:S(2)}, u32[]{:S(2)}) %collective-permute-start.25) | collective-permute-done | bytes 32800 | tf_op jit(solution)/shard_map/ppermute | solution.py:240
  53.3 1.2 %collective-permute-done.26.refs_7_ = bf16[4,2,16,128]{3,2,1,0:T(8,128)(2,1)S(1)} collective-permute-done((bf16[4,2,16,128]{3,2,1,0:T(8,128)(2,1)S(1)}, bf16[4,2,16,128]{3,2,1,0:T(8,128)(2,1)S(1)}, u32[]{:S(2)}, u32[]{:S(2)}) %collective-permute-start.26) | collective-permute-done | bytes 32800 | tf_op jit(solution)/shard_map/ppermute | solution.py:240
  54.5 1.3 %gather_beams.1 = f32[25,16,128]{2,1,0:T(8,128)} custom-call(s32[2]{0:T(128)S(1)} %pad_add_fusion.place_ref, bf16[4,2,16,128]{3,2,1,0:T(8,128)(2,1)S(1)} %get-tuple-element.23.refs_0_, bf16[4,2,16,128]{3,2,1,0:T(8,128)(2,1)S(1)} %collective-permute-done.20.refs_1_, bf16[4,2,16,128]{3,2,1,0:T(8,128)(2,1)S(1)} %collective-permute-done.21.refs_2_, ...), custom_call_target="tpu_custom_call" | custom-call | tf_op jit(solution)/shard_map/gather_beams/pallas_call | solution.py:215
  (55 shorter events, 2.2 us)
Async XLA Ops:
  0.0 0.9 %copy-start = (bf16[2,100,540]{2,0,1:T(2,128)(2,1)S(1)}, bf16[2,100,540]{2,0,1:T(2,128)(2,1)}, u32[]{:S(2)}) copy-start(bf16[2,100,540]{2,0,1:T(2,128)(2,1)} %param.5) | copy-start | bytes 648004
  6.1 13.7 %collective-permute-start = (f16[2,25,16,128]{3,2,0,1:T(8,128)(2,1)S(1)}, f16[2,25,16,128]{3,2,0,1:T(8,128)(2,1)S(1)}, u32[]{:S(2)}, u32[]{:S(2)}) collective-permute-start(f16[2,25,16,128]{3,2,0,1:T(8,128)(2,1)S(1)} %fusion.8), channel_id=1, source_target_pairs={{0,24},{8,16},{16,8},{24,0},{1,25},{9,17},{17,9},{25,1},{2,26},{10... | collective-permute-start | bytes 614408 | tf_op jit(solution)/shard_map/ppermute | solution.py:240
  10.1 10.2 %collective-permute-start.1 = (f16[2,25,16,128]{3,2,0,1:T(8,128)(2,1)S(1)}, f16[2,25,16,128]{3,2,0,1:T(8,128)(2,1)S(1)}, u32[]{:S(2)}, u32[]{:S(2)}) collective-permute-start(f16[2,25,16,128]{3,2,0,1:T(8,128)(2,1)S(1)} %get-tuple-element.17), channel_id=1, source_target_pairs={{0,16},{8,24},{16,0},{24,8},{1,17},{9,25},{17,1},{25,9},{2,18},{10... | collective-permute-start | bytes 614408 | tf_op jit(solution)/shard_map/ppermute | solution.py:240
  10.6 10.0 %collective-permute-start.2 = (f16[2,25,16,128]{3,2,0,1:T(8,128)(2,1)S(1)}, f16[2,25,16,128]{3,2,0,1:T(8,128)(2,1)S(1)}, u32[]{:S(2)}, u32[]{:S(2)}) collective-permute-start(f16[2,25,16,128]{3,2,0,1:T(8,128)(2,1)S(1)} %get-tuple-element.18), channel_id=1, source_target_pairs={{0,8},{8,0},{16,24},{24,16},{1,9},{9,1},{17,25},{25,17},{2,10},{10... | collective-permute-start | bytes 614408 | tf_op jit(solution)/shard_map/ppermute | solution.py:240
  15.8 3.6 %copy-start.2 = (s32[256]{0:T(256)S(1)}, s32[256]{0:T(256)}, u32[]{:S(2)}) copy-start(s32[256]{0:T(256)} %param.7) | copy-start | bytes 3076
  15.8 4.0 %copy-start.1 = (s32[32,16]{0,1:T(8,128)S(1)}, s32[32,16]{0,1:T(8,128)}, u32[]{:S(2)}) copy-start(s32[32,16]{0,1:T(8,128)} %param.6) | copy-start | bytes 6148
  16.0 9.0 %collective-permute-start.10 = (f16[2,25,16,128]{3,2,0,1:T(8,128)(2,1)S(1)}, f16[2,25,16,128]{3,2,0,1:T(8,128)(2,1)S(1)}, u32[]{:S(2)}, u32[]{:S(2)}) collective-permute-start(f16[2,25,16,128]{3,2,0,1:T(8,128)(2,1)S(1)} %fusion.2), channel_id=1, source_target_pairs={{0,24},{8,16},{16,8},{24,0},{1,25},{9,17},{17,9},{25,1},{2,26},{10... | collective-permute-start | bytes 614408 | tf_op jit(solution)/shard_map/ppermute | solution.py:240
  18.9 9.5 %collective-permute-start.11 = (f16[2,25,16,128]{3,2,0,1:T(8,128)(2,1)S(1)}, f16[2,25,16,128]{3,2,0,1:T(8,128)(2,1)S(1)}, u32[]{:S(2)}, u32[]{:S(2)}) collective-permute-start(f16[2,25,16,128]{3,2,0,1:T(8,128)(2,1)S(1)} %fusion.1), channel_id=1, source_target_pairs={{0,16},{8,24},{16,0},{24,8},{1,17},{9,25},{17,1},{25,9},{2,18},{10... | collective-permute-start | bytes 614408 | tf_op jit(solution)/shard_map/ppermute | solution.py:240
  19.8 8.9 %collective-permute-start.12 = (f16[2,25,16,128]{3,2,0,1:T(8,128)(2,1)S(1)}, f16[2,25,16,128]{3,2,0,1:T(8,128)(2,1)S(1)}, u32[]{:S(2)}, u32[]{:S(2)}) collective-permute-start(f16[2,25,16,128]{3,2,0,1:T(8,128)(2,1)S(1)} %fusion), channel_id=1, source_target_pairs={{0,8},{8,0},{16,24},{24,16},{1,9},{9,1},{17,25},{25,17},{2,10},{10... | collective-permute-start | bytes 614408 | tf_op jit(solution)/shard_map/ppermute | solution.py:240
  20.9 11.7 %collective-permute-start.8 = (bf16[7,2,16,128]{3,2,1,0:T(8,128)(2,1)S(1)}, bf16[7,2,16,128]{3,2,1,0:T(8,128)(2,1)S(1)}, u32[]{:S(2)}, u32[]{:S(2)}) collective-permute-start(bf16[7,2,16,128]{3,2,1,0:T(8,128)(2,1)S(1)} %get-tuple-element.39), channel_id=1, source_target_pairs={{0,6},{1,7},{2,4},{3,5},{4,2},{5,3},{6,0},{7,1},{8,14},{9,15},{10,... | collective-permute-start | bytes 172040 | tf_op jit(solution)/shard_map/ppermute | solution.py:240
  24.5 8.0 %collective-permute-start.6 = (bf16[7,2,16,128]{3,2,1,0:T(8,128)(2,1)S(1)}, bf16[7,2,16,128]{3,2,1,0:T(8,128)(2,1)S(1)}, u32[]{:S(2)}, u32[]{:S(2)}) collective-permute-start(bf16[7,2,16,128]{3,2,1,0:T(8,128)(2,1)S(1)} %get-tuple-element.40), channel_id=1, source_target_pairs={{0,4},{1,5},{2,6},{3,7},{4,0},{5,1},{6,2},{7,3},{8,12},{9,13},{10,... | collective-permute-start | bytes 172040 | tf_op jit(solution)/shard_map/ppermute | solution.py:240
  25.0 8.4 %collective-permute-start.4 = (bf16[7,2,16,128]{3,2,1,0:T(8,128)(2,1)S(1)}, bf16[7,2,16,128]{3,2,1,0:T(8,128)(2,1)S(1)}, u32[]{:S(2)}, u32[]{:S(2)}) collective-permute-start(bf16[7,2,16,128]{3,2,1,0:T(8,128)(2,1)S(1)} %get-tuple-element.41), channel_id=1, source_target_pairs={{0,2},{1,3},{2,0},{3,1},{4,6},{5,7},{6,4},{7,5},{8,10},{9,11},{10,... | collective-permute-start | bytes 172040 | tf_op jit(solution)/shard_map/ppermute | solution.py:240
  28.3 5.0 %collective-permute-start.3 = (bf16[7,2,16,128]{3,2,1,0:T(8,128)(2,1)S(1)}, bf16[7,2,16,128]{3,2,1,0:T(8,128)(2,1)S(1)}, u32[]{:S(2)}, u32[]{:S(2)}) collective-permute-start(bf16[7,2,16,128]{3,2,1,0:T(8,128)(2,1)S(1)} %get-tuple-element.42.refs_0_), channel_id=1, source_target_pairs={{0,1},{1,0},{2,3},{3,2},{4,5},{5,4},{6,7},{7,6},{8,9},{9,8},{10,11... | collective-permute-start | bytes 172040 | tf_op jit(solution)/shard_map/ppermute | solution.py:240
  28.9 6.2 %collective-permute-start.18 = (bf16[7,2,16,128]{3,2,1,0:T(8,128)(2,1)S(1)}, bf16[7,2,16,128]{3,2,1,0:T(8,128)(2,1)S(1)}, u32[]{:S(2)}, u32[]{:S(2)}) collective-permute-start(bf16[7,2,16,128]{3,2,1,0:T(8,128)(2,1)S(1)} %get-tuple-element.35), channel_id=1, source_target_pairs={{0,6},{1,7},{2,4},{3,5},{4,2},{5,3},{6,0},{7,1},{8,14},{9,15},{10,... | collective-permute-start | bytes 172040 | tf_op jit(solution)/shard_map/ppermute | solution.py:240
  32.6 5.4 %collective-permute-start.16 = (bf16[7,2,16,128]{3,2,1,0:T(8,128)(2,1)S(1)}, bf16[7,2,16,128]{3,2,1,0:T(8,128)(2,1)S(1)}, u32[]{:S(2)}, u32[]{:S(2)}) collective-permute-start(bf16[7,2,16,128]{3,2,1,0:T(8,128)(2,1)S(1)} %get-tuple-element.36), channel_id=1, source_target_pairs={{0,4},{1,5},{2,6},{3,7},{4,0},{5,1},{6,2},{7,3},{8,12},{9,13},{10,... | collective-permute-start | bytes 172040 | tf_op jit(solution)/shard_map/ppermute | solution.py:240
  32.6 5.5 %collective-permute-start.14 = (bf16[7,2,16,128]{3,2,1,0:T(8,128)(2,1)S(1)}, bf16[7,2,16,128]{3,2,1,0:T(8,128)(2,1)S(1)}, u32[]{:S(2)}, u32[]{:S(2)}) collective-permute-start(bf16[7,2,16,128]{3,2,1,0:T(8,128)(2,1)S(1)} %get-tuple-element.37), channel_id=1, source_target_pairs={{0,2},{1,3},{2,0},{3,1},{4,6},{5,7},{6,4},{7,5},{8,10},{9,11},{10,... | collective-permute-start | bytes 172040 | tf_op jit(solution)/shard_map/ppermute | solution.py:240
  33.4 5.1 %collective-permute-start.13 = (bf16[7,2,16,128]{3,2,1,0:T(8,128)(2,1)S(1)}, bf16[7,2,16,128]{3,2,1,0:T(8,128)(2,1)S(1)}, u32[]{:S(2)}, u32[]{:S(2)}) collective-permute-start(bf16[7,2,16,128]{3,2,1,0:T(8,128)(2,1)S(1)} %get-tuple-element.38.refs_8_), channel_id=1, source_target_pairs={{0,1},{1,0},{2,3},{3,2},{4,5},{5,4},{6,7},{7,6},{8,9},{9,8},{10,11... | collective-permute-start | bytes 172040 | tf_op jit(solution)/shard_map/ppermute | solution.py:240
  33.4 5.2 %collective-permute-start.9 = (bf16[7,2,16,128]{3,2,1,0:T(8,128)(2,1)S(1)}, bf16[7,2,16,128]{3,2,1,0:T(8,128)(2,1)S(1)}, u32[]{:S(2)}, u32[]{:S(2)}) collective-permute-start(bf16[7,2,16,128]{3,2,1,0:T(8,128)(2,1)S(1)} %collective-permute-done.8.refs_6_), channel_id=1, source_target_pairs={{0,1},{1,0},{2,3},{3,2},{4,5},{5,4},{6,7},{7,6},{8,9},{9,8},{10,11... | collective-permute-start | bytes 172040 | tf_op jit(solution)/shard_map/ppermute | solution.py:240
  35.1 4.0 %collective-permute-start.7 = (bf16[7,2,16,128]{3,2,1,0:T(8,128)(2,1)S(1)}, bf16[7,2,16,128]{3,2,1,0:T(8,128)(2,1)S(1)}, u32[]{:S(2)}, u32[]{:S(2)}) collective-permute-start(bf16[7,2,16,128]{3,2,1,0:T(8,128)(2,1)S(1)} %collective-permute-done.6.refs_4_), channel_id=1, source_target_pairs={{0,1},{1,0},{2,3},{3,2},{4,5},{5,4},{6,7},{7,6},{8,9},{9,8},{10,11... | collective-permute-start | bytes 172040 | tf_op jit(solution)/shard_map/ppermute | solution.py:240
  38.0 1.2 %collective-permute-start.5 = (bf16[7,2,16,128]{3,2,1,0:T(8,128)(2,1)S(1)}, bf16[7,2,16,128]{3,2,1,0:T(8,128)(2,1)S(1)}, u32[]{:S(2)}, u32[]{:S(2)}) collective-permute-start(bf16[7,2,16,128]{3,2,1,0:T(8,128)(2,1)S(1)} %collective-permute-done.4.refs_2_), channel_id=1, source_target_pairs={{0,1},{1,0},{2,3},{3,2},{4,5},{5,4},{6,7},{7,6},{8,9},{9,8},{10,11... | collective-permute-start | bytes 172040 | tf_op jit(solution)/shard_map/ppermute | solution.py:240
  38.1 1.3 %collective-permute-start.19 = (bf16[7,2,16,128]{3,2,1,0:T(8,128)(2,1)S(1)}, bf16[7,2,16,128]{3,2,1,0:T(8,128)(2,1)S(1)}, u32[]{:S(2)}, u32[]{:S(2)}) collective-permute-start(bf16[7,2,16,128]{3,2,1,0:T(8,128)(2,1)S(1)} %collective-permute-done.18.refs_14_), channel_id=1, source_target_pairs={{0,1},{1,0},{2,3},{3,2},{4,5},{5,4},{6,7},{7,6},{8,9},{9,8},{10,11... | collective-permute-start | bytes 172040 | tf_op jit(solution)/shard_map/ppermute | solution.py:240
  38.5 1.2 %collective-permute-start.17 = (bf16[7,2,16,128]{3,2,1,0:T(8,128)(2,1)S(1)}, bf16[7,2,16,128]{3,2,1,0:T(8,128)(2,1)S(1)}, u32[]{:S(2)}, u32[]{:S(2)}) collective-permute-start(bf16[7,2,16,128]{3,2,1,0:T(8,128)(2,1)S(1)} %collective-permute-done.16.refs_12_), channel_id=1, source_target_pairs={{0,1},{1,0},{2,3},{3,2},{4,5},{5,4},{6,7},{7,6},{8,9},{9,8},{10,11... | collective-permute-start | bytes 172040 | tf_op jit(solution)/shard_map/ppermute | solution.py:240
  38.6 1.3 %collective-permute-start.15 = (bf16[7,2,16,128]{3,2,1,0:T(8,128)(2,1)S(1)}, bf16[7,2,16,128]{3,2,1,0:T(8,128)(2,1)S(1)}, u32[]{:S(2)}, u32[]{:S(2)}) collective-permute-start(bf16[7,2,16,128]{3,2,1,0:T(8,128)(2,1)S(1)} %collective-permute-done.14.refs_10_), channel_id=1, source_target_pairs={{0,1},{1,0},{2,3},{3,2},{4,5},{5,4},{6,7},{7,6},{8,9},{9,8},{10,11... | collective-permute-start | bytes 172040 | tf_op jit(solution)/shard_map/ppermute | solution.py:240
  44.7 4.5 %collective-permute-start.21 = (bf16[4,2,16,128]{3,2,1,0:T(8,128)(2,1)S(1)}, bf16[4,2,16,128]{3,2,1,0:T(8,128)(2,1)S(1)}, u32[]{:S(2)}, u32[]{:S(2)}) collective-permute-start(bf16[4,2,16,128]{3,2,1,0:T(8,128)(2,1)S(1)} %get-tuple-element.24), channel_id=1, source_target_pairs={{0,2},{1,3},{2,0},{3,1},{4,6},{5,7},{6,4},{7,5},{8,10},{9,11},{10,... | collective-permute-start | bytes 98312 | tf_op jit(solution)/shard_map/ppermute | solution.py:240
  45.8 5.3 %collective-permute-start.23 = (bf16[4,2,16,128]{3,2,1,0:T(8,128)(2,1)S(1)}, bf16[4,2,16,128]{3,2,1,0:T(8,128)(2,1)S(1)}, u32[]{:S(2)}, u32[]{:S(2)}) collective-permute-start(bf16[4,2,16,128]{3,2,1,0:T(8,128)(2,1)S(1)} %get-tuple-element.25), channel_id=1, source_target_pairs={{0,4},{1,5},{2,6},{3,7},{4,0},{5,1},{6,2},{7,3},{8,12},{9,13},{10,... | collective-permute-start | bytes 98312 | tf_op jit(solution)/shard_map/ppermute | solution.py:240
  47.6 5.7 %collective-permute-start.25 = (bf16[4,2,16,128]{3,2,1,0:T(8,128)(2,1)S(1)}, bf16[4,2,16,128]{3,2,1,0:T(8,128)(2,1)S(1)}, u32[]{:S(2)}, u32[]{:S(2)}) collective-permute-start(bf16[4,2,16,128]{3,2,1,0:T(8,128)(2,1)S(1)} %get-tuple-element.26), channel_id=1, source_target_pairs={{0,6},{1,7},{2,4},{3,5},{4,2},{5,3},{6,0},{7,1},{8,14},{9,15},{10,... | collective-permute-start | bytes 98312 | tf_op jit(solution)/shard_map/ppermute | solution.py:240
  49.1 4.2 %collective-permute-start.20 = (bf16[4,2,16,128]{3,2,1,0:T(8,128)(2,1)S(1)}, bf16[4,2,16,128]{3,2,1,0:T(8,128)(2,1)S(1)}, u32[]{:S(2)}, u32[]{:S(2)}) collective-permute-start(bf16[4,2,16,128]{3,2,1,0:T(8,128)(2,1)S(1)} %get-tuple-element.23.refs_0_), channel_id=1, source_target_pairs={{0,1},{1,0},{2,3},{3,2},{4,5},{5,4},{6,7},{7,6},{8,9},{9,8},{10,11... | collective-permute-start | bytes 98312 | tf_op jit(solution)/shard_map/ppermute | solution.py:240
  49.1 4.2 %collective-permute-start.22 = (bf16[4,2,16,128]{3,2,1,0:T(8,128)(2,1)S(1)}, bf16[4,2,16,128]{3,2,1,0:T(8,128)(2,1)S(1)}, u32[]{:S(2)}, u32[]{:S(2)}) collective-permute-start(bf16[4,2,16,128]{3,2,1,0:T(8,128)(2,1)S(1)} %collective-permute-done.21.refs_2_), channel_id=1, source_target_pairs={{0,1},{1,0},{2,3},{3,2},{4,5},{5,4},{6,7},{7,6},{8,9},{9,8},{10,11... | collective-permute-start | bytes 98312 | tf_op jit(solution)/shard_map/ppermute | solution.py:240
  51.1 2.1 %collective-permute-start.24 = (bf16[4,2,16,128]{3,2,1,0:T(8,128)(2,1)S(1)}, bf16[4,2,16,128]{3,2,1,0:T(8,128)(2,1)S(1)}, u32[]{:S(2)}, u32[]{:S(2)}) collective-permute-start(bf16[4,2,16,128]{3,2,1,0:T(8,128)(2,1)S(1)} %collective-permute-done.23.refs_4_), channel_id=1, source_target_pairs={{0,1},{1,0},{2,3},{3,2},{4,5},{5,4},{6,7},{7,6},{8,9},{9,8},{10,11... | collective-permute-start | bytes 98312 | tf_op jit(solution)/shard_map/ppermute | solution.py:240
  53.3 1.2 %collective-permute-start.26 = (bf16[4,2,16,128]{3,2,1,0:T(8,128)(2,1)S(1)}, bf16[4,2,16,128]{3,2,1,0:T(8,128)(2,1)S(1)}, u32[]{:S(2)}, u32[]{:S(2)}) collective-permute-start(bf16[4,2,16,128]{3,2,1,0:T(8,128)(2,1)S(1)} %collective-permute-done.25.refs_6_), channel_id=1, source_target_pairs={{0,1},{1,0},{2,3},{3,2},{4,5},{5,4},{6,7},{7,6},{8,9},{9,8},{10,11... | collective-permute-start | bytes 98312 | tf_op jit(solution)/shard_map/ppermute | solution.py:240

commit v4 on v3

v4 whole, which is shorter than its diff:
```python
import functools
import math

import jax
import jax.numpy as jnp
from jax import lax
from jax.experimental import pallas as pl
from jax.experimental.pallas import tpu as pltpu
from jax.sharding import PartitionSpec as P

PKT = 32
IPP_LEN = 512
LAGS = 64
NCODES = 32
BAUD_LEN = 8
SEC_LEN = 2
GATES = 128
LANES = 128
BLOCKS = IPP_LEN // LANES
PER_ROW = LANES // PKT
PKTS = IPP_LEN // PKT
STREAM_MAX = 6.0
WEIGHT_MAX = 0.09375
VMEM = 48 * 1024 * 1024
CHUNKS = 2
SLICE = 8
F32 = jnp.float32
BF16 = jnp.bfloat16


def beam_kernel(first_column, w_hbm, x_hbm, out_ref, w_ref, x_ref, first_ref, second_ref, mixed_ref, sems):
    beams, _, depth = w_ref.shape
    slices, _, _, width = x_ref.shape
    half = mixed_ref.shape[0] // 2
    w_copy = pltpu.make_async_copy(w_hbm, w_ref, sems.at[slices])
    w_copy.start()
    copies = []
    for index in range(slices):
        columns = pl.ds(first_column + index * width, width)
        copies.append(
            pltpu.make_async_copy(x_hbm.at[:, :, columns], x_ref.at[index], sems.at[index])
        )
        copies[-1].start()
    first_ref[...] = jnp.zeros_like(first_ref)
    second_ref[...] = jnp.zeros_like(second_ref)
    source = lax.broadcasted_iota(jnp.int32, (2 * LANES, 2 * LANES), 0)
    target = lax.broadcasted_iota(jnp.int32, (2 * LANES, 2 * LANES), 1)
    weave = source % LANES * 2 + source // LANES == target
    weave = weave.astype(F32).astype(BF16)
    w_copy.wait()
    weights = w_ref[...].astype(F32)
    real = weights[:, 0, :]
    imag = weights[:, 1, :]
    first_ref[:beams, :depth] = real
    first_ref[half : half + beams, :depth] = imag
    second_ref[:beams, :depth] = -imag
    second_ref[half : half + beams, :depth] = real
    for block in range(first_ref.shape[1] // LANES):
        columns = slice(block * LANES, (block + 1) * LANES)
        pair = jnp.concatenate([first_ref[:, columns], second_ref[:, columns]], 1)
        woven = jnp.dot(pair.astype(BF16), weave, preferred_element_type=F32)
        mixed_ref[:, 2 * block * LANES : 2 * (block + 1) * LANES] = woven.astype(BF16)
    for index in range(slices):
        copies[index].wait()
        product = jnp.dot(
            mixed_ref[:, : 2 * depth],
            x_ref[index].reshape(2 * depth, width),
            preferred_element_type=F32,
        )
        rows = product.reshape(2 * half, width // LANES, LANES)
        place = slice(index * (width // LANES), (index + 1) * (width // LANES))
        out_ref[0, :, place, :] = rows[:beams]
        out_ref[1, :, place, :] = rows[half : half + beams]


def partial_beams(streams, weights, chunk, chunks):
    depth, _, samples = streams.shape
    beams = weights.shape[0]
    samples = samples // chunks
    width = SLICE * LANES
    rows = 2 * (-(-beams // 8) * 8)
    columns = -(-depth // LANES) * LANES
    return pl.pallas_call(
        functools.partial(beam_kernel, chunk * samples),
        in_specs=[pl.BlockSpec(memory_space=pltpu.HBM)] * 2,
        out_specs=pl.BlockSpec(memory_space=pltpu.VMEM),
        out_shape=jax.ShapeDtypeStruct((2, beams, samples // LANES, LANES), F32),
        scratch_shapes=[
            pltpu.VMEM(weights.shape, BF16),
            pltpu.VMEM((samples // width, depth, 2, width), BF16),
            pltpu.VMEM((rows, columns), F32),
            pltpu.VMEM((rows, columns), F32),
            pltpu.VMEM((rows, 2 * columns), BF16),
            pltpu.SemaphoreType.DMA((samples // width + 1,)),
        ],
        compiler_params=pltpu.CompilerParams(vmem_limit_bytes=VMEM),
        cost_estimate=pl.CostEstimate(
            flops=8 * beams * depth * samples,
            bytes_accessed=4 * depth * samples + 8 * beams * samples,
            transcendentals=0,
        ),
        name="partial_beams",
    )(weights, streams)


def lag_kernel(scale, count, place_ref, sign_ref, gate_ref, *refs):
    pieces_in = refs[:count]
    out_refs = refs[count:-4]
    x_ref, both_ref, lag_ref, sum_ref = refs[-4:]
    sources, slots, _, rows, _ = x_ref.shape
    chips = len(out_refs)
    chip = place_ref[0]
    core = place_ref[1]
    taken = pieces_in[0].shape[0] - slots
    span = pieces_in[0].shape[2]
    for index, ref in enumerate(pieces_in):
        chunk, step, other = index // sources, index // 2 % chips, index % 2
        source = 2 * (chip ^ step) + (core ^ other)
        x_ref[source, :, :, chunk * span : (chunk + 1) * span] = ref[pl.ds(core * taken, slots)]
    row_groups = sign_ref.shape[0]
    depth = row_groups * rows
    lane = lax.broadcasted_iota(jnp.int32, (rows, LANES), 1)
    row = lax.broadcasted_iota(jnp.int32, (rows, LANES), 0)
    flip = (
        lax.broadcasted_iota(jnp.int32, (LANES, LANES), 0)
        + lax.broadcasted_iota(jnp.int32, (LANES, LANES), 1)
        == LANES - 1
    ).astype(F32).astype(BF16)
    real_lane = lax.broadcasted_iota(jnp.int32, (LANES, LANES), 1) < LAGS
    real_depth = lax.broadcasted_iota(jnp.int32, (LANES, 2 * depth), 1) < depth

    def assemble(slot, part):
        loaded = [x_ref[d, slot, part].astype(F32) for d in range(sources)]
        raw = []
        for group in range(row_groups):
            blocks = []
            for block in range(BLOCKS):
                total = None
                for place in range(PER_ROW):
                    packet = group * PKTS + block * PER_ROW + place
                    shift = (place - packet // sources) * PKT % LANES
                    piece = loaded[packet % sources]
                    if shift:
                        piece = pltpu.roll(piece, shift, 1)
                    total = piece if total is None else jnp.where(lane >= place * PKT, piece, total)
                blocks.append(total)
            raw.append(blocks)
        raw.append([jnp.where(row == rows - 1, 0.0, pltpu.roll(raw[0][0], rows - 1, 0))])
        for group in range(row_groups):
            top = part * depth + group * rows
            for block in range(BLOCKS + 1):
                piece = raw[group][block] if block < BLOCKS else raw[group + 1][0]
                columns = slice(block * LANES, (block + 1) * LANES)
                both_ref[slot, top : top + rows, columns] = (piece * sign_ref[group]).astype(BF16)

    for slot in range(slots):
        assemble(slot, 0)
        assemble(slot, 1)
    for slot in range(slots):
        held = slice(slot * LANES, (slot + 1) * LANES)
        for block in range(BLOCKS):
            columns = slice(block * LANES, (block + 1) * LANES)
            base = lax.dot_general(
                flip,
                both_ref[slot, :, columns],
                (((1,), (1,)), ((), ())),
                preferred_element_type=F32,
            )
            swapped = pltpu.roll(base, depth, 1)
            turned = jnp.where(real_depth, -swapped, swapped)
            gram = jnp.dot(
                jnp.concatenate([base, turned], 0).astype(BF16),
                both_ref[slot, :, block * LANES : (block + 2) * LANES],
                preferred_element_type=F32,
            )
            real_lags = pltpu.roll(gram[:LANES], LANES, 1, stride=1, stride_axis=0)
            imag_lags = pltpu.roll(gram[LANES:], LANES + LAGS, 1, stride=1, stride_axis=0)
            lags = jnp.where(real_lane, real_lags[:, :LANES], imag_lags[:, :LANES])
            high = lags.astype(BF16)
            low = (lags - high.astype(F32)).astype(BF16)
            top = 2 * block * LANES
            lag_ref[top : top + LANES, held] = high
            lag_ref[top + LANES : top + 2 * LANES, held] = low
    gates = [gate_ref[:, b * LANES : (b + 1) * LANES] for b in range(BLOCKS)]
    gates = jnp.concatenate([gate for gate in gates for _ in range(2)], 1)
    sums = jnp.dot(gates, lag_ref[...], preferred_element_type=F32)
    for slot in range(slots):
        sum_ref[slot] = sums[:, slot * LANES : (slot + 1) * LANES] * scale
    for step, out_ref in enumerate(out_refs):
        gates = out_ref.shape[1] * out_ref.shape[2]
        first = pl.multiple_of((chip ^ step) * gates, gates)
        out_ref[...] = sum_ref[:, pl.ds(first, gates), :].reshape(out_ref.shape).astype(BF16)


def lag_profiles(place, signs, gate_hot, pieces, sources, slots, scale):
    chips = sources // 2
    row_groups, rows, _ = signs.shape
    out = jax.ShapeDtypeStruct((slots, 2, GATES // sources, LANES), BF16)
    vmem = pl.BlockSpec(memory_space=pltpu.VMEM)
    return pl.pallas_call(
        functools.partial(lag_kernel, scale, len(pieces)),
        in_specs=[pl.BlockSpec(memory_space=pltpu.SMEM)] + [vmem] * (2 + len(pieces)),
        out_specs=[vmem] * chips,
        out_shape=[out] * chips,
        scratch_shapes=[
            pltpu.VMEM((sources, slots, 2, rows, LANES), BF16),
            pltpu.VMEM((slots, 2 * row_groups * rows, (BLOCKS + 1) * LANES), BF16),
            pltpu.VMEM((2 * IPP_LEN, slots * LANES), BF16),
            pltpu.VMEM((slots, GATES, LANES), F32),
        ],
        compiler_params=pltpu.CompilerParams(vmem_limit_bytes=VMEM),
        name="lag_profiles",
    )(place, signs, gate_hot, *pieces)


def gather_kernel(width, place_ref, *refs):
    pieces_in = refs[:-1]
    out_ref = refs[-1]
    chips = len(pieces_in) // 2
    beams = out_ref.shape[0]
    slots = pieces_in[0].shape[0]
    chip = place_ref[0]
    core = place_ref[1]
    for index, ref in enumerate(pieces_in):
        first = (chip ^ (index // 2)) * (beams - width) // (chips - 1)
        first += (core ^ (index % 2)) * (width - slots)
        out_ref[pl.ds(first, slots)] = ref[:, core].astype(F32)


def gather_beams(place, pieces, width, beams):
    gates = pieces[0].shape[2]
    vmem = pl.BlockSpec(memory_space=pltpu.VMEM)
    return pl.pallas_call(
        functools.partial(gather_kernel, width),
        in_specs=[pl.BlockSpec(memory_space=pltpu.SMEM)] + [vmem] * len(pieces),
        out_specs=vmem,
        out_shape=jax.ShapeDtypeStruct((beams, gates, LANES), F32),
        compiler_params=pltpu.CompilerParams(vmem_limit_bytes=VMEM),
        name="gather_beams",
    )(place, *pieces)


def sign_rows(code_signs, periods, row_groups):
    signs = jnp.repeat((2 * code_signs - 1).astype(F32), BAUD_LEN, axis=1)
    signs = jnp.tile(signs, (periods // NCODES, 1))
    return signs.reshape(periods // row_groups, row_groups, LANES).transpose(1, 0, 2)


def gate_rows(gate_map):
    position = jnp.arange(IPP_LEN)
    position = position // LANES * LANES + (LANES - 1 - position % LANES)
    gates = jnp.repeat(gate_map, SEC_LEN).reshape(BLOCKS, LANES)[:, ::-1].reshape(IPP_LEN)
    return (jnp.arange(GATES)[:, None] == gates[None, :]).astype(BF16)


def exchanged(block, axis, step):
    return lax.ppermute(block, axis, [(i, i ^ step) for i in range(lax.axis_size(axis))])


def spread(blocks):
    pieces = []
    for step in reversed(range(len(blocks))):
        block = exchanged(blocks[step], "tm", 2 * step) if step else blocks[0]
        pieces = [block, exchanged(block, "tm", 1)] + pieces
    return pieces


def body(streams, beam_weights, code_signs, gate_map):
    groups = lax.axis_size("sub")
    sources = lax.axis_size("tm")
    chips = sources // 2
    beams = beam_weights.shape[1] // groups
    samples = streams.shape[2]
    width = -(-beams // chips)
    slots = -(-width // 2)
    periods = samples * sources // IPP_LEN
    scale = 1.0 / math.sqrt(periods * IPP_LEN / GATES)
    here = lax.axis_index("sub")
    place = jnp.stack([lax.axis_index("tm") // 2, lax.axis_index("tm") % 2]).astype(jnp.int32)
    chip = place[0]
    signs = sign_rows(code_signs, periods, sources // PER_ROW)
    gate_hot = gate_rows(gate_map)
    weights = pltpu.with_memory_space_constraint(beam_weights.transpose(1, 0, 2), pltpu.HBM)
    limit = 2 * streams.shape[1] * STREAM_MAX * WEIGHT_MAX
    gain = 2.0 ** math.floor(math.log2(60000.0 / limit))
    by_channel = streams.transpose(1, 0, 2)

    def block_of(array, group):
        return lax.dynamic_slice_in_dim(array, group * beams, beams, 1)

    pieces = []
    for chunk in range(CHUNKS):
        partial = partial_beams(by_channel, weights, chunk, CHUNKS)
        sent = []
        for step in range(groups - 1, 0, -1):
            sent.append((block_of(partial, here ^ step) * gain).astype(jnp.float16))
        *sent, weights = lax.optimization_barrier((*sent, weights))
        summed = block_of(partial, here)
        for step in range(groups - 1, 0, -1):
            came = exchanged(sent[groups - 1 - step], "sub", step)
            summed = summed + came.astype(F32) * (1.0 / gain)
        early = summed.astype(BF16).transpose(1, 0, 2, 3)
        blocks = []
        for step in range(chips):
            first = (chip ^ step) * (beams - width) // (chips - 1)
            blocks.append(lax.dynamic_slice_in_dim(early, first, width, 0))
        pieces += spread(blocks)
    terms = lag_profiles(place, signs, gate_hot, pieces, sources, slots, scale)
    return gather_beams(place, spread(terms), width, beams).transpose(1, 0, 2)


def solution(mesh):
    placed = (P(None, "sub", "tm"), P(None, None, "sub"), P(), P())
    return jax.shard_map(
        body, mesh=mesh, in_specs=placed, out_specs=P("tm", "sub", None), check_vma=False
    )
```

time: 55.9 us -> 52.1 us (0.932)
  Pallas kernels: 15.8 us -> 11.5 us
  waiting for transfers between devices: 12.6 us -> 14 us
  local copies, waits for them, and re-layouts: 1.62 us -> 0.73 us
    pallas_call x3, Pallas kernels: 11.1 us -> 8.08 us  [the longest x2 6.82 us: partial_beams(): pl.pallas_call(functools.partial(beam_kernel, chunk * samples), in_specs=...]
    ppermute x27, waiting for transfers between devices: 12.6 us -> 14 us  [exchanged(): lax.ppermute(block, axis, [(i, i ^ step) for i in range(lax.axis_size(axi...]
    pallas_call x1, Pallas kernels: 4.74 us -> 3.38 us  [lag_profiles(): pl.pallas_call(functools.partial(lag_kernel, scale, len(pieces)), in_spec...]
    unnamed x6 -> x4, local copies, waits for them, and re-layouts: 0.96 us -> 0.01 us
  transfers between devices with their start and end apart: 27 -> 27, of which waited for: 15 -> 14; matrix products, arithmetic and copies ran while one was open for 2% -> 2% of each run, Pallas kernels for 9% -> 7%
where the time goes in v4:
time: 52.1 us; the launch traced here: 52 us
  starting transfers between devices  24.8 us (48%)
  waiting for transfers between devices  14 us (27%)
  Pallas kernels  11.5 us (22%)
  other arithmetic  0.74 us (1%)
  local copies, waits for them, and re-layouts  0.73 us (1%)
    ppermute x27, starting transfers between devices, exchanged(): lax.ppermute(block, axis, [(i, i ^ step) for i in range(lax.axis_size(axi...  24.8 us
    ppermute x27, waiting for transfers between devices, exchanged(): lax.ppermute(block, axis, [(i, i ^ step) for i in range(lax.axis_size(axi...  14 us
    pallas_call x2, Pallas kernels, partial_beams(): pl.pallas_call(functools.partial(beam_kernel, chunk * samples), in_specs=...  6.82 us
    pallas_call x1, Pallas kernels, lag_profiles(): pl.pallas_call(functools.partial(lag_kernel, scale, len(pieces)), in_spec...  3.38 us
    pallas_call x1, Pallas kernels, gather_beams(): pl.pallas_call(functools.partial(gather_kernel, width), in_specs=[pl.Bloc...  1.26 us
  transfers between devices with their start and end apart: 27, of which 14 were waited for; matrix products, arithmetic and copies ran while one was open for 2% of the time, Pallas kernels for 7%

profile of v4, /device:TPU:0, one launch (start us, length us, event | category | flops | bytes accessed | tf_op | source)
XLA Modules:
  0.0 52.0 jit_solution(1682195384520966363)
XLA Ops:
  0.0 3.4 %partial_beams.2 = f32[2,100,16,128]{3,2,1,0:T(8,128)S(1)} custom-call(bf16[100,2,540]{2,1,0:T(2,128)(2,1)} %bitcast.32, bf16[540,2,4096]{2,1,0:T(2,128)(2,1)} %bitcast.30), custom_call_target="tpu_custom_call" | custom-call | flops 884736000 | bytes 6062080 | tf_op jit(solution)/shard_map/partial_beams/pallas_call | solution.py:83
  3.7 4.0 %collective-permute-start = (f16[2,25,16,128]{3,2,0,1:T(8,128)(2,1)S(1)}, f16[2,25,16,128]{3,2,0,1:T(8,128)(2,1)S(1)}, u32[]{:S(2)}, u32[]{:S(2)}) collective-permute-start(f16[2,25,16,128]{3,2,0,1:T(8,128)(2,1)S(1)} %fusion.8), channel_id=1, source_target_pairs={{0,24},{8,16},{16,8},{24,0},{1,25},{9,17},{17,9},{25,1},{2,26},{10... | collective-permute-start | bytes 614408 | tf_op jit(solution)/shard_map/ppermute | solution.py:257
  7.7 0.5 collective-permute-start.1
  8.3 3.4 %partial_beams.3 = f32[2,100,16,128]{3,2,1,0:T(8,128)S(1)} custom-call(bf16[100,2,540]{2,1,0:T(2,128)(2,1)} %bitcast.33, bf16[540,2,4096]{2,1,0:T(2,128)(2,1)} %bitcast.31), custom_call_target="tpu_custom_call" | custom-call | flops 884736000 | bytes 6062080 | tf_op jit(solution)/shard_map/partial_beams/pallas_call | solution.py:83
  12.1 2.9 %collective-permute-start.10 = (f16[2,25,16,128]{3,2,0,1:T(8,128)(2,1)S(1)}, f16[2,25,16,128]{3,2,0,1:T(8,128)(2,1)S(1)}, u32[]{:S(2)}, u32[]{:S(2)}) collective-permute-start(f16[2,25,16,128]{3,2,0,1:T(8,128)(2,1)S(1)} %fusion.2), channel_id=1, source_target_pairs={{0,24},{8,16},{16,8},{24,0},{1,25},{9,17},{17,9},{25,1},{2,26},{10... | collective-permute-start | bytes 614408 | tf_op jit(solution)/shard_map/ppermute | solution.py:257
  15.0 0.5 collective-permute-start.11
  15.9 0.2 collective-permute-start.12
  16.1 2.0 %collective-permute-done.1 = f16[2,25,16,128]{3,2,0,1:T(8,128)(2,1)S(1)} collective-permute-done((f16[2,25,16,128]{3,2,0,1:T(8,128)(2,1)S(1)}, f16[2,25,16,128]{3,2,0,1:T(8,128)(2,1)S(1)}, u32[]{:S(2)}, u32[]{:S(2)}) %collective-permute-start.1) | collective-permute-done | bytes 204832 | tf_op jit(solution)/shard_map/ppermute | solution.py:257
  18.1 0.5 collective-permute-done.2
  18.6 0.2 fusion.11
  18.8 3.7 %collective-permute-start.8 = (bf16[7,2,16,128]{3,2,1,0:T(8,128)(2,1)S(1)}, bf16[7,2,16,128]{3,2,1,0:T(8,128)(2,1)S(1)}, u32[]{:S(2)}, u32[]{:S(2)}) collective-permute-start(bf16[7,2,16,128]{3,2,1,0:T(8,128)(2,1)S(1)} %get-tuple-element.39), channel_id=1, source_target_pairs={{0,6},{1,7},{2,4},{3,5},{4,2},{5,3},{6,0},{7,1},{8,14},{9,15},{10,... | collective-permute-start | bytes 172040 | tf_op jit(solution)/shard_map/ppermute | solution.py:257
  22.5 2.1 %collective-permute-start.4 = (bf16[7,2,16,128]{3,2,1,0:T(8,128)(2,1)S(1)}, bf16[7,2,16,128]{3,2,1,0:T(8,128)(2,1)S(1)}, u32[]{:S(2)}, u32[]{:S(2)}) collective-permute-start(bf16[7,2,16,128]{3,2,1,0:T(8,128)(2,1)S(1)} %get-tuple-element.41), channel_id=1, source_target_pairs={{0,2},{1,3},{2,0},{3,1},{4,6},{5,7},{6,4},{7,5},{8,10},{9,11},{10,... | collective-permute-start | bytes 172040 | tf_op jit(solution)/shard_map/ppermute | solution.py:257
  24.6 1.4 %collective-permute-done.11 = f16[2,25,16,128]{3,2,0,1:T(8,128)(2,1)S(1)} collective-permute-done((f16[2,25,16,128]{3,2,0,1:T(8,128)(2,1)S(1)}, f16[2,25,16,128]{3,2,0,1:T(8,128)(2,1)S(1)}, u32[]{:S(2)}, u32[]{:S(2)}) %collective-permute-start.11) | collective-permute-done | bytes 204832 | tf_op jit(solution)/shard_map/ppermute | solution.py:257
  25.9 0.3 collective-permute-done.12
  26.3 0.2 fusion.5
  26.5 3.7 %collective-permute-start.18 = (bf16[7,2,16,128]{3,2,1,0:T(8,128)(2,1)S(1)}, bf16[7,2,16,128]{3,2,1,0:T(8,128)(2,1)S(1)}, u32[]{:S(2)}, u32[]{:S(2)}) collective-permute-start(bf16[7,2,16,128]{3,2,1,0:T(8,128)(2,1)S(1)} %get-tuple-element.35), channel_id=1, source_target_pairs={{0,6},{1,7},{2,4},{3,5},{4,2},{5,3},{6,0},{7,1},{8,14},{9,15},{10,... | collective-permute-start | bytes 172040 | tf_op jit(solution)/shard_map/ppermute | solution.py:257
  30.2 0.8 %collective-permute-start.14 = (bf16[7,2,16,128]{3,2,1,0:T(8,128)(2,1)S(1)}, bf16[7,2,16,128]{3,2,1,0:T(8,128)(2,1)S(1)}, u32[]{:S(2)}, u32[]{:S(2)}) collective-permute-start(bf16[7,2,16,128]{3,2,1,0:T(8,128)(2,1)S(1)} %get-tuple-element.37), channel_id=1, source_target_pairs={{0,2},{1,3},{2,0},{3,1},{4,6},{5,7},{6,4},{7,5},{8,10},{9,11},{10,... | collective-permute-start | bytes 172040 | tf_op jit(solution)/shard_map/ppermute | solution.py:257
  30.9 0.5 collective-permute-start.9
  31.6 1.2 %collective-permute-done.18.refs_14_ = bf16[7,2,16,128]{3,2,1,0:T(8,128)(2,1)S(1)} collective-permute-done((bf16[7,2,16,128]{3,2,1,0:T(8,128)(2,1)S(1)}, bf16[7,2,16,128]{3,2,1,0:T(8,128)(2,1)S(1)}, u32[]{:S(2)}, u32[]{:S(2)}) %collective-permute-start.18) | collective-permute-done | bytes 57376 | tf_op jit(solution)/shard_map/ppermute | solution.py:257
  32.7 2.8 %collective-permute-done.16.refs_12_ = bf16[7,2,16,128]{3,2,1,0:T(8,128)(2,1)S(1)} collective-permute-done((bf16[7,2,16,128]{3,2,1,0:T(8,128)(2,1)S(1)}, bf16[7,2,16,128]{3,2,1,0:T(8,128)(2,1)S(1)}, u32[]{:S(2)}, u32[]{:S(2)}) %collective-permute-start.16) | collective-permute-done | bytes 57376 | tf_op jit(solution)/shard_map/ppermute | solution.py:257
  35.6 0.4 collective-permute-start.19
  36.2 0.4 collective-permute-start.15
  37.0 0.4 collective-permute-done.17.refs_13_
  37.5 3.4 %lag_profiles.1 = (bf16[4,2,16,128]{3,2,1,0:T(8,128)(2,1)S(1)}, bf16[4,2,16,128]{3,2,1,0:T(8,128)(2,1)S(1)}, bf16[4,2,16,128]{3,2,1,0:T(8,128)(2,1)S(1)}, bf16[4,2,16,128]{3,2,1,0:T(8,128)(2,1)S(1)}) custom-call(s32[2]{0:T(128)S(1)} %pad_add_fusion.place_ref, f32[2,32,128]{2,1,0:T(8,128)S(1)} %bitcast.29, bf16[128,512]{1,0:T(8,128)(2,1)S(1)} %fusion.12.gate_ref, ...), custom_call_target="tpu_custom_call" | custom-call | tf_op jit(solution)/shard_map/lag_profiles/pallas_call | solution.py:200
  40.9 1.2 %collective-permute-start.21 = (bf16[4,2,16,128]{3,2,1,0:T(8,128)(2,1)S(1)}, bf16[4,2,16,128]{3,2,1,0:T(8,128)(2,1)S(1)}, u32[]{:S(2)}, u32[]{:S(2)}) collective-permute-start(bf16[4,2,16,128]{3,2,1,0:T(8,128)(2,1)S(1)} %get-tuple-element.24), channel_id=1, source_target_pairs={{0,2},{1,3},{2,0},{3,1},{4,6},{5,7},{6,4},{7,5},{8,10},{9,11},{10,... | collective-permute-start | bytes 98312 | tf_op jit(solution)/shard_map/ppermute | solution.py:257
  42.1 1.7 %collective-permute-start.23 = (bf16[4,2,16,128]{3,2,1,0:T(8,128)(2,1)S(1)}, bf16[4,2,16,128]{3,2,1,0:T(8,128)(2,1)S(1)}, u32[]{:S(2)}, u32[]{:S(2)}) collective-permute-start(bf16[4,2,16,128]{3,2,1,0:T(8,128)(2,1)S(1)} %get-tuple-element.25), channel_id=1, source_target_pairs={{0,4},{1,5},{2,6},{3,7},{4,0},{5,1},{6,2},{7,3},{8,12},{9,13},{10,... | collective-permute-start | bytes 98312 | tf_op jit(solution)/shard_map/ppermute | solution.py:257
  43.8 1.5 %collective-permute-start.25 = (bf16[4,2,16,128]{3,2,1,0:T(8,128)(2,1)S(1)}, bf16[4,2,16,128]{3,2,1,0:T(8,128)(2,1)S(1)}, u32[]{:S(2)}, u32[]{:S(2)}) collective-permute-start(bf16[4,2,16,128]{3,2,1,0:T(8,128)(2,1)S(1)} %get-tuple-element.26), channel_id=1, source_target_pairs={{0,6},{1,7},{2,4},{3,5},{4,2},{5,3},{6,0},{7,1},{8,14},{9,15},{10,... | collective-permute-start | bytes 98312 | tf_op jit(solution)/shard_map/ppermute | solution.py:257
  45.3 0.5 collective-permute-start.22
  45.8 1.5 %collective-permute-done.23.refs_4_ = bf16[4,2,16,128]{3,2,1,0:T(8,128)(2,1)S(1)} collective-permute-done((bf16[4,2,16,128]{3,2,1,0:T(8,128)(2,1)S(1)}, bf16[4,2,16,128]{3,2,1,0:T(8,128)(2,1)S(1)}, u32[]{:S(2)}, u32[]{:S(2)}) %collective-permute-start.23) | collective-permute-done | bytes 32800 | tf_op jit(solution)/shard_map/ppermute | solution.py:257
  47.4 2.1 %collective-permute-done.25.refs_6_ = bf16[4,2,16,128]{3,2,1,0:T(8,128)(2,1)S(1)} collective-permute-done((bf16[4,2,16,128]{3,2,1,0:T(8,128)(2,1)S(1)}, bf16[4,2,16,128]{3,2,1,0:T(8,128)(2,1)S(1)}, u32[]{:S(2)}, u32[]{:S(2)}) %collective-permute-start.25) | collective-permute-done | bytes 32800 | tf_op jit(solution)/shard_map/ppermute | solution.py:257
  49.5 1.2 %collective-permute-done.26.refs_7_ = bf16[4,2,16,128]{3,2,1,0:T(8,128)(2,1)S(1)} collective-permute-done((bf16[4,2,16,128]{3,2,1,0:T(8,128)(2,1)S(1)}, bf16[4,2,16,128]{3,2,1,0:T(8,128)(2,1)S(1)}, u32[]{:S(2)}, u32[]{:S(2)}) %collective-permute-start.26) | collective-permute-done | bytes 32800 | tf_op jit(solution)/shard_map/ppermute | solution.py:257
  50.7 1.3 %gather_beams.1 = f32[25,16,128]{2,1,0:T(8,128)} custom-call(s32[2]{0:T(128)S(1)} %pad_add_fusion.place_ref, bf16[4,2,16,128]{3,2,1,0:T(8,128)(2,1)S(1)} %get-tuple-element.23.refs_0_, bf16[4,2,16,128]{3,2,1,0:T(8,128)(2,1)S(1)} %collective-permute-done.20.refs_1_, bf16[4,2,16,128]{3,2,1,0:T(8,128)(2,1)S(1)} %collective-permute-done.21.refs_2_, ...), custom_call_target="tpu_custom_call" | custom-call | tf_op jit(solution)/shard_map/gather_beams/pallas_call | solution.py:233
  (53 shorter events, 2.0 us)
Async XLA Ops:
  3.7 12.2 %collective-permute-start = (f16[2,25,16,128]{3,2,0,1:T(8,128)(2,1)S(1)}, f16[2,25,16,128]{3,2,0,1:T(8,128)(2,1)S(1)}, u32[]{:S(2)}, u32[]{:S(2)}) collective-permute-start(f16[2,25,16,128]{3,2,0,1:T(8,128)(2,1)S(1)} %fusion.8), channel_id=1, source_target_pairs={{0,24},{8,16},{16,8},{24,0},{1,25},{9,17},{17,9},{25,1},{2,26},{10... | collective-permute-start | bytes 614408 | tf_op jit(solution)/shard_map/ppermute | solution.py:257
  7.7 10.4 %collective-permute-start.1 = (f16[2,25,16,128]{3,2,0,1:T(8,128)(2,1)S(1)}, f16[2,25,16,128]{3,2,0,1:T(8,128)(2,1)S(1)}, u32[]{:S(2)}, u32[]{:S(2)}) collective-permute-start(f16[2,25,16,128]{3,2,0,1:T(8,128)(2,1)S(1)} %get-tuple-element.17), channel_id=1, source_target_pairs={{0,16},{8,24},{16,0},{24,8},{1,17},{9,25},{17,1},{25,9},{2,18},{10... | collective-permute-start | bytes 614408 | tf_op jit(solution)/shard_map/ppermute | solution.py:257
  8.2 10.4 %collective-permute-start.2 = (f16[2,25,16,128]{3,2,0,1:T(8,128)(2,1)S(1)}, f16[2,25,16,128]{3,2,0,1:T(8,128)(2,1)S(1)}, u32[]{:S(2)}, u32[]{:S(2)}) collective-permute-start(f16[2,25,16,128]{3,2,0,1:T(8,128)(2,1)S(1)} %get-tuple-element.18), channel_id=1, source_target_pairs={{0,8},{8,0},{16,24},{24,16},{1,9},{9,1},{17,25},{25,17},{2,10},{10... | collective-permute-start | bytes 614408 | tf_op jit(solution)/shard_map/ppermute | solution.py:257
  11.9 3.6 %copy-start.1 = (s32[256]{0:T(256)S(1)}, s32[256]{0:T(256)}, u32[]{:S(2)}) copy-start(s32[256]{0:T(256)} %param.7) | copy-start | bytes 3076
  11.9 4.0 %copy-start = (s32[32,16]{0,1:T(8,128)S(1)}, s32[32,16]{0,1:T(8,128)}, u32[]{:S(2)}) copy-start(s32[32,16]{0,1:T(8,128)} %param.6) | copy-start | bytes 6148
  12.1 10.4 %collective-permute-start.10 = (f16[2,25,16,128]{3,2,0,1:T(8,128)(2,1)S(1)}, f16[2,25,16,128]{3,2,0,1:T(8,128)(2,1)S(1)}, u32[]{:S(2)}, u32[]{:S(2)}) collective-permute-start(f16[2,25,16,128]{3,2,0,1:T(8,128)(2,1)S(1)} %fusion.2), channel_id=1, source_target_pairs={{0,24},{8,16},{16,8},{24,0},{1,25},{9,17},{17,9},{25,1},{2,26},{10... | collective-permute-start | bytes 614408 | tf_op jit(solution)/shard_map/ppermute | solution.py:257
  15.0 10.9 %collective-permute-start.11 = (f16[2,25,16,128]{3,2,0,1:T(8,128)(2,1)S(1)}, f16[2,25,16,128]{3,2,0,1:T(8,128)(2,1)S(1)}, u32[]{:S(2)}, u32[]{:S(2)}) collective-permute-start(f16[2,25,16,128]{3,2,0,1:T(8,128)(2,1)S(1)} %fusion.1), channel_id=1, source_target_pairs={{0,16},{8,24},{16,0},{24,8},{1,17},{9,25},{17,1},{25,9},{2,18},{10... | collective-permute-start | bytes 614408 | tf_op jit(solution)/shard_map/ppermute | solution.py:257
  15.9 10.4 %collective-permute-start.12 = (f16[2,25,16,128]{3,2,0,1:T(8,128)(2,1)S(1)}, f16[2,25,16,128]{3,2,0,1:T(8,128)(2,1)S(1)}, u32[]{:S(2)}, u32[]{:S(2)}) collective-permute-start(f16[2,25,16,128]{3,2,0,1:T(8,128)(2,1)S(1)} %fusion), channel_id=1, source_target_pairs={{0,8},{8,0},{16,24},{24,16},{1,9},{9,1},{17,25},{25,17},{2,10},{10... | collective-permute-start | bytes 614408 | tf_op jit(solution)/shard_map/ppermute | solution.py:257
  18.8 11.4 %collective-permute-start.8 = (bf16[7,2,16,128]{3,2,1,0:T(8,128)(2,1)S(1)}, bf16[7,2,16,128]{3,2,1,0:T(8,128)(2,1)S(1)}, u32[]{:S(2)}, u32[]{:S(2)}) collective-permute-start(bf16[7,2,16,128]{3,2,1,0:T(8,128)(2,1)S(1)} %get-tuple-element.39), channel_id=1, source_target_pairs={{0,6},{1,7},{2,4},{3,5},{4,2},{5,3},{6,0},{7,1},{8,14},{9,15},{10,... | collective-permute-start | bytes 172040 | tf_op jit(solution)/shard_map/ppermute | solution.py:257
  22.5 7.7 %collective-permute-start.6 = (bf16[7,2,16,128]{3,2,1,0:T(8,128)(2,1)S(1)}, bf16[7,2,16,128]{3,2,1,0:T(8,128)(2,1)S(1)}, u32[]{:S(2)}, u32[]{:S(2)}) collective-permute-start(bf16[7,2,16,128]{3,2,1,0:T(8,128)(2,1)S(1)} %get-tuple-element.40), channel_id=1, source_target_pairs={{0,4},{1,5},{2,6},{3,7},{4,0},{5,1},{6,2},{7,3},{8,12},{9,13},{10,... | collective-permute-start | bytes 172040 | tf_op jit(solution)/shard_map/ppermute | solution.py:257
  22.5 8.4 %collective-permute-start.4 = (bf16[7,2,16,128]{3,2,1,0:T(8,128)(2,1)S(1)}, bf16[7,2,16,128]{3,2,1,0:T(8,128)(2,1)S(1)}, u32[]{:S(2)}, u32[]{:S(2)}) collective-permute-start(bf16[7,2,16,128]{3,2,1,0:T(8,128)(2,1)S(1)} %get-tuple-element.41), channel_id=1, source_target_pairs={{0,2},{1,3},{2,0},{3,1},{4,6},{5,7},{6,4},{7,5},{8,10},{9,11},{10,... | collective-permute-start | bytes 172040 | tf_op jit(solution)/shard_map/ppermute | solution.py:257
  25.9 5.0 %collective-permute-start.3 = (bf16[7,2,16,128]{3,2,1,0:T(8,128)(2,1)S(1)}, bf16[7,2,16,128]{3,2,1,0:T(8,128)(2,1)S(1)}, u32[]{:S(2)}, u32[]{:S(2)}) collective-permute-start(bf16[7,2,16,128]{3,2,1,0:T(8,128)(2,1)S(1)} %get-tuple-element.42.refs_0_), channel_id=1, source_target_pairs={{0,1},{1,0},{2,3},{3,2},{4,5},{5,4},{6,7},{7,6},{8,9},{9,8},{10,11... | collective-permute-start | bytes 172040 | tf_op jit(solution)/shard_map/ppermute | solution.py:257
  26.5 6.2 %collective-permute-start.18 = (bf16[7,2,16,128]{3,2,1,0:T(8,128)(2,1)S(1)}, bf16[7,2,16,128]{3,2,1,0:T(8,128)(2,1)S(1)}, u32[]{:S(2)}, u32[]{:S(2)}) collective-permute-start(bf16[7,2,16,128]{3,2,1,0:T(8,128)(2,1)S(1)} %get-tuple-element.35), channel_id=1, source_target_pairs={{0,6},{1,7},{2,4},{3,5},{4,2},{5,3},{6,0},{7,1},{8,14},{9,15},{10,... | collective-permute-start | bytes 172040 | tf_op jit(solution)/shard_map/ppermute | solution.py:257
  30.2 5.4 %collective-permute-start.16 = (bf16[7,2,16,128]{3,2,1,0:T(8,128)(2,1)S(1)}, bf16[7,2,16,128]{3,2,1,0:T(8,128)(2,1)S(1)}, u32[]{:S(2)}, u32[]{:S(2)}) collective-permute-start(bf16[7,2,16,128]{3,2,1,0:T(8,128)(2,1)S(1)} %get-tuple-element.36), channel_id=1, source_target_pairs={{0,4},{1,5},{2,6},{3,7},{4,0},{5,1},{6,2},{7,3},{8,12},{9,13},{10,... | collective-permute-start | bytes 172040 | tf_op jit(solution)/shard_map/ppermute | solution.py:257
  30.2 5.5 %collective-permute-start.14 = (bf16[7,2,16,128]{3,2,1,0:T(8,128)(2,1)S(1)}, bf16[7,2,16,128]{3,2,1,0:T(8,128)(2,1)S(1)}, u32[]{:S(2)}, u32[]{:S(2)}) collective-permute-start(bf16[7,2,16,128]{3,2,1,0:T(8,128)(2,1)S(1)} %get-tuple-element.37), channel_id=1, source_target_pairs={{0,2},{1,3},{2,0},{3,1},{4,6},{5,7},{6,4},{7,5},{8,10},{9,11},{10,... | collective-permute-start | bytes 172040 | tf_op jit(solution)/shard_map/ppermute | solution.py:257
  30.9 5.1 %collective-permute-start.13 = (bf16[7,2,16,128]{3,2,1,0:T(8,128)(2,1)S(1)}, bf16[7,2,16,128]{3,2,1,0:T(8,128)(2,1)S(1)}, u32[]{:S(2)}, u32[]{:S(2)}) collective-permute-start(bf16[7,2,16,128]{3,2,1,0:T(8,128)(2,1)S(1)} %get-tuple-element.38.refs_8_), channel_id=1, source_target_pairs={{0,1},{1,0},{2,3},{3,2},{4,5},{5,4},{6,7},{7,6},{8,9},{9,8},{10,11... | collective-permute-start | bytes 172040 | tf_op jit(solution)/shard_map/ppermute | solution.py:257
  30.9 5.2 %collective-permute-start.9 = (bf16[7,2,16,128]{3,2,1,0:T(8,128)(2,1)S(1)}, bf16[7,2,16,128]{3,2,1,0:T(8,128)(2,1)S(1)}, u32[]{:S(2)}, u32[]{:S(2)}) collective-permute-start(bf16[7,2,16,128]{3,2,1,0:T(8,128)(2,1)S(1)} %collective-permute-done.8.refs_6_), channel_id=1, source_target_pairs={{0,1},{1,0},{2,3},{3,2},{4,5},{5,4},{6,7},{7,6},{8,9},{9,8},{10,11... | collective-permute-start | bytes 172040 | tf_op jit(solution)/shard_map/ppermute | solution.py:257
  32.7 4.0 %collective-permute-start.7 = (bf16[7,2,16,128]{3,2,1,0:T(8,128)(2,1)S(1)}, bf16[7,2,16,128]{3,2,1,0:T(8,128)(2,1)S(1)}, u32[]{:S(2)}, u32[]{:S(2)}) collective-permute-start(bf16[7,2,16,128]{3,2,1,0:T(8,128)(2,1)S(1)} %collective-permute-done.6.refs_4_), channel_id=1, source_target_pairs={{0,1},{1,0},{2,3},{3,2},{4,5},{5,4},{6,7},{7,6},{8,9},{9,8},{10,11... | collective-permute-start | bytes 172040 | tf_op jit(solution)/shard_map/ppermute | solution.py:257
  35.6 1.2 %collective-permute-start.5 = (bf16[7,2,16,128]{3,2,1,0:T(8,128)(2,1)S(1)}, bf16[7,2,16,128]{3,2,1,0:T(8,128)(2,1)S(1)}, u32[]{:S(2)}, u32[]{:S(2)}) collective-permute-start(bf16[7,2,16,128]{3,2,1,0:T(8,128)(2,1)S(1)} %collective-permute-done.4.refs_2_), channel_id=1, source_target_pairs={{0,1},{1,0},{2,3},{3,2},{4,5},{5,4},{6,7},{7,6},{8,9},{9,8},{10,11... | collective-permute-start | bytes 172040 | tf_op jit(solution)/shard_map/ppermute | solution.py:257
  35.6 1.3 %collective-permute-start.19 = (bf16[7,2,16,128]{3,2,1,0:T(8,128)(2,1)S(1)}, bf16[7,2,16,128]{3,2,1,0:T(8,128)(2,1)S(1)}, u32[]{:S(2)}, u32[]{:S(2)}) collective-permute-start(bf16[7,2,16,128]{3,2,1,0:T(8,128)(2,1)S(1)} %collective-permute-done.18.refs_14_), channel_id=1, source_target_pairs={{0,1},{1,0},{2,3},{3,2},{4,5},{5,4},{6,7},{7,6},{8,9},{9,8},{10,11... | collective-permute-start | bytes 172040 | tf_op jit(solution)/shard_map/ppermute | solution.py:257
  36.1 1.2 %collective-permute-start.17 = (bf16[7,2,16,128]{3,2,1,0:T(8,128)(2,1)S(1)}, bf16[7,2,16,128]{3,2,1,0:T(8,128)(2,1)S(1)}, u32[]{:S(2)}, u32[]{:S(2)}) collective-permute-start(bf16[7,2,16,128]{3,2,1,0:T(8,128)(2,1)S(1)} %collective-permute-done.16.refs_12_), channel_id=1, source_target_pairs={{0,1},{1,0},{2,3},{3,2},{4,5},{5,4},{6,7},{7,6},{8,9},{9,8},{10,11... | collective-permute-start | bytes 172040 | tf_op jit(solution)/shard_map/ppermute | solution.py:257
  36.2 1.3 %collective-permute-start.15 = (bf16[7,2,16,128]{3,2,1,0:T(8,128)(2,1)S(1)}, bf16[7,2,16,128]{3,2,1,0:T(8,128)(2,1)S(1)}, u32[]{:S(2)}, u32[]{:S(2)}) collective-permute-start(bf16[7,2,16,128]{3,2,1,0:T(8,128)(2,1)S(1)} %collective-permute-done.14.refs_10_), channel_id=1, source_target_pairs={{0,1},{1,0},{2,3},{3,2},{4,5},{5,4},{6,7},{7,6},{8,9},{9,8},{10,11... | collective-permute-start | bytes 172040 | tf_op jit(solution)/shard_map/ppermute | solution.py:257
  40.9 4.5 %collective-permute-start.21 = (bf16[4,2,16,128]{3,2,1,0:T(8,128)(2,1)S(1)}, bf16[4,2,16,128]{3,2,1,0:T(8,128)(2,1)S(1)}, u32[]{:S(2)}, u32[]{:S(2)}) collective-permute-start(bf16[4,2,16,128]{3,2,1,0:T(8,128)(2,1)S(1)} %get-tuple-element.24), channel_id=1, source_target_pairs={{0,2},{1,3},{2,0},{3,1},{4,6},{5,7},{6,4},{7,5},{8,10},{9,11},{10,... | collective-permute-start | bytes 98312 | tf_op jit(solution)/shard_map/ppermute | solution.py:257
  42.1 5.3 %collective-permute-start.23 = (bf16[4,2,16,128]{3,2,1,0:T(8,128)(2,1)S(1)}, bf16[4,2,16,128]{3,2,1,0:T(8,128)(2,1)S(1)}, u32[]{:S(2)}, u32[]{:S(2)}) collective-permute-start(bf16[4,2,16,128]{3,2,1,0:T(8,128)(2,1)S(1)} %get-tuple-element.25), channel_id=1, source_target_pairs={{0,4},{1,5},{2,6},{3,7},{4,0},{5,1},{6,2},{7,3},{8,12},{9,13},{10,... | collective-permute-start | bytes 98312 | tf_op jit(solution)/shard_map/ppermute | solution.py:257
  43.8 5.7 %collective-permute-start.25 = (bf16[4,2,16,128]{3,2,1,0:T(8,128)(2,1)S(1)}, bf16[4,2,16,128]{3,2,1,0:T(8,128)(2,1)S(1)}, u32[]{:S(2)}, u32[]{:S(2)}) collective-permute-start(bf16[4,2,16,128]{3,2,1,0:T(8,128)(2,1)S(1)} %get-tuple-element.26), channel_id=1, source_target_pairs={{0,6},{1,7},{2,4},{3,5},{4,2},{5,3},{6,0},{7,1},{8,14},{9,15},{10,... | collective-permute-start | bytes 98312 | tf_op jit(solution)/shard_map/ppermute | solution.py:257
  45.3 4.2 %collective-permute-start.20 = (bf16[4,2,16,128]{3,2,1,0:T(8,128)(2,1)S(1)}, bf16[4,2,16,128]{3,2,1,0:T(8,128)(2,1)S(1)}, u32[]{:S(2)}, u32[]{:S(2)}) collective-permute-start(bf16[4,2,16,128]{3,2,1,0:T(8,128)(2,1)S(1)} %get-tuple-element.23.refs_0_), channel_id=1, source_target_pairs={{0,1},{1,0},{2,3},{3,2},{4,5},{5,4},{6,7},{7,6},{8,9},{9,8},{10,11... | collective-permute-start | bytes 98312 | tf_op jit(solution)/shard_map/ppermute | solution.py:257
  45.3 4.2 %collective-permute-start.22 = (bf16[4,2,16,128]{3,2,1,0:T(8,128)(2,1)S(1)}, bf16[4,2,16,128]{3,2,1,0:T(8,128)(2,1)S(1)}, u32[]{:S(2)}, u32[]{:S(2)}) collective-permute-start(bf16[4,2,16,128]{3,2,1,0:T(8,128)(2,1)S(1)} %collective-permute-done.21.refs_2_), channel_id=1, source_target_pairs={{0,1},{1,0},{2,3},{3,2},{4,5},{5,4},{6,7},{7,6},{8,9},{9,8},{10,11... | collective-permute-start | bytes 98312 | tf_op jit(solution)/shard_map/ppermute | solution.py:257
  47.4 2.2 %collective-permute-start.24 = (bf16[4,2,16,128]{3,2,1,0:T(8,128)(2,1)S(1)}, bf16[4,2,16,128]{3,2,1,0:T(8,128)(2,1)S(1)}, u32[]{:S(2)}, u32[]{:S(2)}) collective-permute-start(bf16[4,2,16,128]{3,2,1,0:T(8,128)(2,1)S(1)} %collective-permute-done.23.refs_4_), channel_id=1, source_target_pairs={{0,1},{1,0},{2,3},{3,2},{4,5},{5,4},{6,7},{7,6},{8,9},{9,8},{10,11... | collective-permute-start | bytes 98312 | tf_op jit(solution)/shard_map/ppermute | solution.py:257
  49.5 1.2 %collective-permute-start.26 = (bf16[4,2,16,128]{3,2,1,0:T(8,128)(2,1)S(1)}, bf16[4,2,16,128]{3,2,1,0:T(8,128)(2,1)S(1)}, u32[]{:S(2)}, u32[]{:S(2)}) collective-permute-start(bf16[4,2,16,128]{3,2,1,0:T(8,128)(2,1)S(1)} %collective-permute-done.25.refs_6_), channel_id=1, source_target_pairs={{0,1},{1,0},{2,3},{3,2},{4,5},{5,4},{6,7},{7,6},{8,9},{9,8},{10,11... | collective-permute-start | bytes 98312 | tf_op jit(solution)/shard_map/ppermute | solution.py:257

commit v5 on v4

--- a/solution.py
+++ b/solution.py
@@ -22,21 +22,24 @@
 STREAM_MAX = 6.0
 WEIGHT_MAX = 0.09375
 VMEM = 48 * 1024 * 1024
-CHUNKS = 2
 SLICE = 8
 F32 = jnp.float32
 BF16 = jnp.bfloat16
 
 
-def beam_kernel(first_column, w_hbm, x_hbm, out_ref, w_ref, x_ref, first_ref, second_ref, mixed_ref, sems):
-    beams, _, depth = w_ref.shape
+def beam_kernel(place_ref, w_hbm, x_hbm, *refs):
+    out_refs = refs[:-6]
+    w_ref, x_ref, first_ref, second_ref, mixed_ref, sems = refs[-6:]
+    groups = len(out_refs)
+    depth = w_ref.shape[2]
     slices, _, _, width = x_ref.shape
     half = mixed_ref.shape[0] // 2
+    count = out_refs[0].shape[1]
     w_copy = pltpu.make_async_copy(w_hbm, w_ref, sems.at[slices])
     w_copy.start()
     copies = []
     for index in range(slices):
-        columns = pl.ds(first_column + index * width, width)
+        columns = pl.ds(index * width, width)
         copies.append(
             pltpu.make_async_copy(x_hbm.at[:, :, columns], x_ref.at[index], sems.at[index])
         )
@@ -48,13 +51,17 @@
     weave = source % LANES * 2 + source // LANES == target
     weave = weave.astype(F32).astype(BF16)
     w_copy.wait()
-    weights = w_ref[...].astype(F32)
-    real = weights[:, 0, :]
-    imag = weights[:, 1, :]
-    first_ref[:beams, :depth] = real
-    first_ref[half : half + beams, :depth] = imag
-    second_ref[:beams, :depth] = -imag
-    second_ref[half : half + beams, :depth] = real
+    for group in range(groups):
+        owner = place_ref[0] ^ group
+        chosen = pl.ds(owner * (w_ref.shape[0] // groups) + place_ref[1], count)
+        weights = w_ref[chosen].astype(F32)
+        real = weights[:, 0, :]
+        imag = weights[:, 1, :]
+        top = group * count
+        first_ref[top : top + count, :depth] = real
+        first_ref[half + top : half + top + count, :depth] = imag
+        second_ref[top : top + count, :depth] = -imag
+        second_ref[half + top : half + top + count, :depth] = real
     for block in range(first_ref.shape[1] // LANES):
         columns = slice(block * LANES, (block + 1) * LANES)
         pair = jnp.concatenate([first_ref[:, columns], second_ref[:, columns]], 1)
@@ -69,22 +76,24 @@
         )
         rows = product.reshape(2 * half, width // LANES, LANES)
         place = slice(index * (width // LANES), (index + 1) * (width // LANES))
-        out_ref[0, :, place, :] = rows[:beams]
-        out_ref[1, :, place, :] = rows[half : half + beams]
-
-
-def partial_beams(streams, weights, chunk, chunks):
+        for group, out_ref in enumerate(out_refs):
+            top = group * count
+            out_ref[0, :, place, :] = rows[top : top + count]
+            out_ref[1, :, place, :] = rows[half + top : half + top + count]
+
+
+def partial_beams(streams, weights, place, groups, count):
     depth, _, samples = streams.shape
-    beams = weights.shape[0]
-    samples = samples // chunks
+    beams = groups * count
     width = SLICE * LANES
     rows = 2 * (-(-beams // 8) * 8)
     columns = -(-depth // LANES) * LANES
     return pl.pallas_call(
-        functools.partial(beam_kernel, chunk * samples),
-        in_specs=[pl.BlockSpec(memory_space=pltpu.HBM)] * 2,
-        out_specs=pl.BlockSpec(memory_space=pltpu.VMEM),
-        out_shape=jax.ShapeDtypeStruct((2, beams, samples // LANES, LANES), F32),
+        beam_kernel,
+        in_specs=[pl.BlockSpec(memory_space=pltpu.SMEM)]
+        + [pl.BlockSpec(memory_space=pltpu.HBM)] * 2,
+        out_specs=[pl.BlockSpec(memory_space=pltpu.VMEM)] * groups,
+        out_shape=[jax.ShapeDtypeStruct((2, count, samples // LANES, LANES), F32)] * groups,
         scratch_shapes=[
             pltpu.VMEM(weights.shape, BF16),
             pltpu.VMEM((samples // width, depth, 2, width), BF16),
@@ -100,23 +109,20 @@
             transcendentals=0,
         ),
         name="partial_beams",
-    )(weights, streams)
+    )(place, weights, streams)
 
 
 def lag_kernel(scale, count, place_ref, sign_ref, gate_ref, *refs):
     pieces_in = refs[:count]
     out_refs = refs[count:-4]
     x_ref, both_ref, lag_ref, sum_ref = refs[-4:]
-    sources, slots, _, rows, _ = x_ref.shape
-    chips = len(out_refs)
+    sources, _, slots, rows, _ = x_ref.shape
     chip = place_ref[0]
     core = place_ref[1]
-    taken = pieces_in[0].shape[0] - slots
-    span = pieces_in[0].shape[2]
+    taken = pieces_in[0].shape[1] - slots
     for index, ref in enumerate(pieces_in):
-        chunk, step, other = index // sources, index // 2 % chips, index % 2
-        source = 2 * (chip ^ step) + (core ^ other)
-        x_ref[source, :, :, chunk * span : (chunk + 1) * span] = ref[pl.ds(core * taken, slots)]
+        source = 2 * (chip ^ (index // 2)) + (core ^ (index % 2))
+        x_ref[source] = ref[:, pl.ds(core * taken, slots)]
     row_groups = sign_ref.shape[0]
     depth = row_groups * rows
     lane = lax.broadcasted_iota(jnp.int32, (rows, LANES), 1)
@@ -130,7 +136,7 @@
     real_depth = lax.broadcasted_iota(jnp.int32, (LANES, 2 * depth), 1) < depth
 
     def assemble(slot, part):
-        loaded = [x_ref[d, slot, part].astype(F32) for d in range(sources)]
+        loaded = [x_ref[d, part, slot].astype(F32) for d in range(sources)]
         raw = []
         for group in range(row_groups):
             blocks = []
@@ -186,7 +192,7 @@
     sums = jnp.dot(gates, lag_ref[...], preferred_element_type=F32)
     for slot in range(slots):
         sum_ref[slot] = sums[:, slot * LANES : (slot + 1) * LANES] * scale
-    for step, out_ref in enumerate(out_refs):
+    for step, out_ref in enumerate(reversed(out_refs)):
         gates = out_ref.shape[1] * out_ref.shape[2]
         first = pl.multiple_of((chip ^ step) * gates, gates)
         out_ref[...] = sum_ref[:, pl.ds(first, gates), :].reshape(out_ref.shape).astype(BF16)
@@ -203,7 +209,7 @@
         out_specs=[vmem] * chips,
         out_shape=[out] * chips,
         scratch_shapes=[
-            pltpu.VMEM((sources, slots, 2, rows, LANES), BF16),
+            pltpu.VMEM((sources, 2, slots, rows, LANES), BF16),
             pltpu.VMEM((slots, 2 * row_groups * rows, (BLOCKS + 1) * LANES), BF16),
             pltpu.VMEM((2 * IPP_LEN, slots * LANES), BF16),
             pltpu.VMEM((slots, GATES, LANES), F32),
@@ -259,9 +265,9 @@
 
 def spread(blocks):
     pieces = []
-    for step in reversed(range(len(blocks))):
-        block = exchanged(blocks[step], "tm", 2 * step) if step else blocks[0]
-        pieces = [block, exchanged(block, "tm", 1)] + pieces
+    for step, block in enumerate(blocks):
+        block = exchanged(block, "tm", 2 * step) if step else block
+        pieces += [block, exchanged(block, "tm", 1)]
     return pieces
 
 
@@ -285,28 +291,27 @@
     gain = 2.0 ** math.floor(math.log2(60000.0 / limit))
     by_channel = streams.transpose(1, 0, 2)
 
-    def block_of(array, group):
-        return lax.dynamic_slice_in_dim(array, group * beams, beams, 1)
-
-    pieces = []
-    for chunk in range(CHUNKS):
-        partial = partial_beams(by_channel, weights, chunk, CHUNKS)
-        sent = []
+    def first_of(owner):
+        return owner * (beams - width) // (chips - 1)
+
+    half = chips // 2
+    count = max((half - 1) * (beams - width) // (chips - 1) + width, beams - first_of(half))
+    low = chip < half
+    blocks = [None] * chips
+    for far in (True, False):
+        start = jnp.where(low == far, beams - count, 0).astype(jnp.int32)
+        chosen = jnp.stack([here, start]).astype(jnp.int32)
+        partial = partial_beams(by_channel, weights, chosen, groups, count)
+        total = partial[0]
         for step in range(groups - 1, 0, -1):
-            sent.append((block_of(partial, here ^ step) * gain).astype(jnp.float16))
-        *sent, weights = lax.optimization_barrier((*sent, weights))
-        summed = block_of(partial, here)
-        for step in range(groups - 1, 0, -1):
-            came = exchanged(sent[groups - 1 - step], "sub", step)
-            summed = summed + came.astype(F32) * (1.0 / gain)
-        early = summed.astype(BF16).transpose(1, 0, 2, 3)
-        blocks = []
-        for step in range(chips):
-            first = (chip ^ step) * (beams - width) // (chips - 1)
-            blocks.append(lax.dynamic_slice_in_dim(early, first, width, 0))
-        pieces += spread(blocks)
-    terms = lag_profiles(place, signs, gate_hot, pieces, sources, slots, scale)
-    return gather_beams(place, spread(terms), width, beams).transpose(1, 0, 2)
+            came = exchanged((partial[step] * gain).astype(jnp.float16), "sub", step)
+            total = total + came.astype(F32) * (1.0 / gain)
+        total = total.astype(BF16)
+        for step in range(half, chips) if far else range(half):
+            place_of = first_of(chip ^ step) - start
+            blocks[step] = lax.dynamic_slice_in_dim(total, place_of, width, 1)
+    terms = lag_profiles(place, signs, gate_hot, spread(blocks), sources, slots, scale)
+    return gather_beams(place, spread(terms[::-1]), width, beams).transpose(1, 0, 2)
 
 
 def solution(mesh):

time: 52.1 us -> 50.9 us (0.977)
  starting transfers between devices: 24.8 us -> 19.6 us
  Pallas kernels: 11.5 us -> 14.6 us
  other arithmetic: 0.74 us -> 1.47 us
    ppermute x27 -> x20, starting transfers between devices: 24.8 us -> 19.6 us  [exchanged(): lax.ppermute(block, axis, [(i, i ^ step) for i in range(lax.axis_size(axi...]
    pallas_call x2, Pallas kernels: 6.82 us -> 9.98 us  [partial_beams(): pl.pallas_call(beam_kernel, in_specs=[pl.BlockSpec(memory_space=pltpu.SME...]
    convert_element_type x7 -> x8, other arithmetic: 0.61 us -> 1.27 us  [the longest x6 0.98 us: body(): came = exchanged((partial[step] * gain).astype(jnp.float16), 'sub', step)]
    ppermute x27 -> x20, waiting for transfers between devices: 14 us -> 14.5 us  [exchanged(): lax.ppermute(block, axis, [(i, i ^ step) for i in range(lax.axis_size(axi...]
  transfers between devices with their start and end apart: 27 -> 20, of which waited for: 14 -> 9; matrix products, arithmetic and copies ran while one was open for 2% -> 3% of each run, Pallas kernels for 7% -> 10%
where the time goes in v5:
time: 50.9 us; the launch traced here: 50.7 us
  starting transfers between devices  19.6 us (39%)
  Pallas kernels  14.6 us (29%)
  waiting for transfers between devices  14.5 us (28%)
  other arithmetic  1.47 us (3%)
    ppermute x20, starting transfers between devices, exchanged(): lax.ppermute(block, axis, [(i, i ^ step) for i in range(lax.axis_size(axi...  19.6 us
    ppermute x20, waiting for transfers between devices, exchanged(): lax.ppermute(block, axis, [(i, i ^ step) for i in range(lax.axis_size(axi...  14.5 us
    pallas_call x2, Pallas kernels, partial_beams(): pl.pallas_call(beam_kernel, in_specs=[pl.BlockSpec(memory_space=pltpu.SME...  9.98 us
    pallas_call x1, Pallas kernels, lag_profiles(): pl.pallas_call(functools.partial(lag_kernel, scale, len(pieces)), in_spec...  3.36 us
    pallas_call x1, Pallas kernels, gather_beams(): pl.pallas_call(functools.partial(gather_kernel, width), in_specs=[pl.Bloc...  1.26 us
  transfers between devices with their start and end apart: 20, of which 9 were waited for; matrix products, arithmetic and copies ran while one was open for 3% of the time, Pallas kernels for 10%

profile of v5, /device:TPU:0, one launch (start us, length us, event | category | flops | bytes accessed | tf_op | source)
XLA Modules:
  0.0 50.7 jit_solution(1361219654505105862)
XLA Ops:
  0.1 5.0 %partial_beams.3 = (f32[2,13,32,128]{3,2,1,0:T(8,128)S(1)}, f32[2,13,32,128]{3,2,1,0:T(8,128)S(1)}, f32[2,13,32,128]{3,2,1,0:T(8,128)S(1)}, f32[2,13,32,128]{3,2,1,0:T(8,128)S(1)}) custom-call(s32[2]{0:T(128)S(1)} %get-tuple-element.34.place_ref, bf16[100,2,540]{2,1,0:T(2,128)(2,1)} %bitcast.19, bf16[540,2,4096]{2,1,0:T(2,128)(2,1)} %bitcast.17), custom_call_target="tpu_custom_call" | custom-call | flops 920125440 | bytes 10551296 | tf_op jit(solution)/shard_map/partial_beams/pallas_call | solution.py:91
  5.1 4.0 %collective-permute-start.6 = (f16[2,13,32,128]{3,2,1,0:T(8,128)(2,1)S(1)}, f16[2,13,32,128]{3,2,1,0:T(8,128)(2,1)S(1)}, u32[]{:S(2)}, u32[]{:S(2)}) collective-permute-start(f16[2,13,32,128]{3,2,1,0:T(8,128)(2,1)S(1)} %multiply_convert_fusion.2), channel_id=1, source_target_pairs={{0,24},{8,16},{16,8},{24,0},{1,25},{9,17},{17,9},{25,1},{2,26},{10... | collective-permute-start | bytes 638984 | tf_op jit(solution)/shard_map/ppermute | solution.py:263
  9.2 0.6 %collective-permute-start.7 = (f16[2,13,32,128]{3,2,1,0:T(8,128)(2,1)S(1)}, f16[2,13,32,128]{3,2,1,0:T(8,128)(2,1)S(1)}, u32[]{:S(2)}, u32[]{:S(2)}) collective-permute-start(f16[2,13,32,128]{3,2,1,0:T(8,128)(2,1)S(1)} %multiply_convert_fusion.1), channel_id=1, source_target_pairs={{0,16},{8,24},{16,0},{24,8},{1,17},{9,25},{17,1},{25,9},{2,18},{10... | collective-permute-start | bytes 638984 | tf_op jit(solution)/shard_map/ppermute | solution.py:263
  9.8 0.1 collective-permute-start.8
  9.9 5.0 %partial_beams.2 = (f32[2,13,32,128]{3,2,1,0:T(8,128)S(1)}, f32[2,13,32,128]{3,2,1,0:T(8,128)S(1)}, f32[2,13,32,128]{3,2,1,0:T(8,128)S(1)}, f32[2,13,32,128]{3,2,1,0:T(8,128)S(1)}) custom-call(s32[2]{0:T(128)S(1)} %get-tuple-element.33.place_ref, bf16[100,2,540]{2,1,0:T(2,128)(2,1)} %bitcast.20, bf16[540,2,4096]{2,1,0:T(2,128)(2,1)} %bitcast.18), custom_call_target="tpu_custom_call" | custom-call | flops 920125440 | bytes 10551296 | tf_op jit(solution)/shard_map/partial_beams/pallas_call | solution.py:91
  15.0 3.0 %collective-permute-start = (f16[2,13,32,128]{3,2,1,0:T(8,128)(2,1)S(1)}, f16[2,13,32,128]{3,2,1,0:T(8,128)(2,1)S(1)}, u32[]{:S(2)}, u32[]{:S(2)}) collective-permute-start(f16[2,13,32,128]{3,2,1,0:T(8,128)(2,1)S(1)} %multiply_convert_fusion.5), channel_id=1, source_target_pairs={{0,24},{8,16},{16,8},{24,0},{1,25},{9,17},{17,9},{25,1},{2,26},{10... | collective-permute-start | bytes 638984 | tf_op jit(solution)/shard_map/ppermute | solution.py:263
  18.0 0.6 %collective-permute-start.1 = (f16[2,13,32,128]{3,2,1,0:T(8,128)(2,1)S(1)}, f16[2,13,32,128]{3,2,1,0:T(8,128)(2,1)S(1)}, u32[]{:S(2)}, u32[]{:S(2)}) collective-permute-start(f16[2,13,32,128]{3,2,1,0:T(8,128)(2,1)S(1)} %multiply_convert_fusion.4), channel_id=1, source_target_pairs={{0,16},{8,24},{16,0},{24,8},{1,17},{9,25},{17,1},{25,9},{2,18},{10... | collective-permute-start | bytes 638984 | tf_op jit(solution)/shard_map/ppermute | solution.py:263
  18.6 0.7 %multiply_convert_fusion.3 = f16[2,13,32,128]{3,2,1,0:T(8,128)(2,1)} fusion(f32[2,13,32,128]{3,2,1,0:T(8,128)S(1)} %get-tuple-element.20), kind=kLoop, calls=%fused_computation.5 | loop fusion | flops 212992 | bytes 638976 | tf_op jit(solution)/shard_map/convert_element_type | solution.py:307
  19.3 0.1 broadcast_in_dim.12
  19.4 0.1 copy.10
  19.7 0.2 collective-permute-start.2
  19.9 0.5 collective-permute-done.8
  20.4 0.1 add_convert_fusion
  20.5 2.7 %collective-permute-start.9 = (bf16[2,7,32,128]{3,2,1,0:T(8,128)(2,1)S(1)}, bf16[2,7,32,128]{3,2,1,0:T(8,128)(2,1)S(1)}, u32[]{:S(2)}, u32[]{:S(2)}) collective-permute-start(bf16[2,7,32,128]{3,2,1,0:T(8,128)(2,1)S(1)} %get-tuple-element.30), channel_id=1, source_target_pairs={{0,4},{1,5},{2,6},{3,7},{4,0},{5,1},{6,2},{7,3},{8,12},{9,13},{10,... | collective-permute-start | bytes 344072 | tf_op jit(solution)/shard_map/ppermute | solution.py:263
  23.2 1.3 %collective-permute-start.11 = (bf16[2,7,32,128]{3,2,1,0:T(8,128)(2,1)S(1)}, bf16[2,7,32,128]{3,2,1,0:T(8,128)(2,1)S(1)}, u32[]{:S(2)}, u32[]{:S(2)}) collective-permute-start(bf16[2,7,32,128]{3,2,1,0:T(8,128)(2,1)S(1)} %get-tuple-element.29), channel_id=1, source_target_pairs={{0,6},{1,7},{2,4},{3,5},{4,2},{5,3},{6,0},{7,1},{8,14},{9,15},{10,... | collective-permute-start | bytes 344072 | tf_op jit(solution)/shard_map/ppermute | solution.py:263
  24.6 3.5 %collective-permute-done.1 = f16[2,13,32,128]{3,2,1,0:T(8,128)(2,1)S(1)} collective-permute-done((f16[2,13,32,128]{3,2,1,0:T(8,128)(2,1)S(1)}, f16[2,13,32,128]{3,2,1,0:T(8,128)(2,1)S(1)}, u32[]{:S(2)}, u32[]{:S(2)}) %collective-permute-start.1) | collective-permute-done | bytes 213024 | tf_op jit(solution)/shard_map/ppermute | solution.py:263
  28.1 0.3 collective-permute-done.2
  28.4 0.1 add_convert_fusion.1
  28.6 1.6 %collective-permute-start.4 = (bf16[2,7,32,128]{3,2,1,0:T(8,128)(2,1)S(1)}, bf16[2,7,32,128]{3,2,1,0:T(8,128)(2,1)S(1)}, u32[]{:S(2)}, u32[]{:S(2)}) collective-permute-start(bf16[2,7,32,128]{3,2,1,0:T(8,128)(2,1)S(1)} %get-tuple-element.31), channel_id=1, source_target_pairs={{0,2},{1,3},{2,0},{3,1},{4,6},{5,7},{6,4},{7,5},{8,10},{9,11},{10,... | collective-permute-start | bytes 344072 | tf_op jit(solution)/shard_map/ppermute | solution.py:263
  30.2 2.2 %collective-permute-done.9.refs_4_ = bf16[2,7,32,128]{3,2,1,0:T(8,128)(2,1)S(1)} collective-permute-done((bf16[2,7,32,128]{3,2,1,0:T(8,128)(2,1)S(1)}, bf16[2,7,32,128]{3,2,1,0:T(8,128)(2,1)S(1)}, u32[]{:S(2)}, u32[]{:S(2)}) %collective-permute-start.9) | collective-permute-done | bytes 114720 | tf_op jit(solution)/shard_map/ppermute | solution.py:263
  32.4 0.5 %collective-permute-start.12 = (bf16[2,7,32,128]{3,2,1,0:T(8,128)(2,1)S(1)}, bf16[2,7,32,128]{3,2,1,0:T(8,128)(2,1)S(1)}, u32[]{:S(2)}, u32[]{:S(2)}) collective-permute-start(bf16[2,7,32,128]{3,2,1,0:T(8,128)(2,1)S(1)} %collective-permute-done.11.refs_6_), channel_id=1, source_target_pairs={{0,1},{1,0},{2,3},{3,2},{4,5},{5,4},{6,7},{7,6},{8,9},{9,8},{10,11... | collective-permute-start | bytes 344072 | tf_op jit(solution)/shard_map/ppermute | solution.py:263
  32.9 1.2 %collective-permute-done.4.refs_2_ = bf16[2,7,32,128]{3,2,1,0:T(8,128)(2,1)S(1)} collective-permute-done((bf16[2,7,32,128]{3,2,1,0:T(8,128)(2,1)S(1)}, bf16[2,7,32,128]{3,2,1,0:T(8,128)(2,1)S(1)}, u32[]{:S(2)}, u32[]{:S(2)}) %collective-permute-start.4) | collective-permute-done | bytes 114720 | tf_op jit(solution)/shard_map/ppermute | solution.py:263
  34.3 1.1 %collective-permute-done.5.refs_3_ = bf16[2,7,32,128]{3,2,1,0:T(8,128)(2,1)S(1)} collective-permute-done((bf16[2,7,32,128]{3,2,1,0:T(8,128)(2,1)S(1)}, bf16[2,7,32,128]{3,2,1,0:T(8,128)(2,1)S(1)}, u32[]{:S(2)}, u32[]{:S(2)}) %collective-permute-start.5) | collective-permute-done | bytes 114720 | tf_op jit(solution)/shard_map/ppermute | solution.py:263
  35.4 3.4 %lag_profiles.1 = (bf16[4,2,16,128]{3,2,1,0:T(8,128)(2,1)S(1)}, bf16[4,2,16,128]{3,2,1,0:T(8,128)(2,1)S(1)}, bf16[4,2,16,128]{3,2,1,0:T(8,128)(2,1)S(1)}, bf16[4,2,16,128]{3,2,1,0:T(8,128)(2,1)S(1)}) custom-call(s32[2]{0:T(128)S(1)} %pad_add_fusion.place_ref, f32[2,32,128]{2,1,0:T(8,128)S(1)} %bitcast.16, bf16[128,512]{1,0:T(8,128)(2,1)S(1)} %fusion.gate_ref, ...), custom_call_target="tpu_custom_call" | custom-call | tf_op jit(solution)/shard_map/lag_profiles/pallas_call | solution.py:206
  38.8 1.0 %collective-permute-start.14 = (bf16[4,2,16,128]{3,2,1,0:T(8,128)(2,1)S(1)}, bf16[4,2,16,128]{3,2,1,0:T(8,128)(2,1)S(1)}, u32[]{:S(2)}, u32[]{:S(2)}) collective-permute-start(bf16[4,2,16,128]{3,2,1,0:T(8,128)(2,1)S(1)} %get-tuple-element.26), channel_id=1, source_target_pairs={{0,2},{1,3},{2,0},{3,1},{4,6},{5,7},{6,4},{7,5},{8,10},{9,11},{10,... | collective-permute-start | bytes 98312 | tf_op jit(solution)/shard_map/ppermute | solution.py:263
  39.8 2.7 %collective-permute-start.16 = (bf16[4,2,16,128]{3,2,1,0:T(8,128)(2,1)S(1)}, bf16[4,2,16,128]{3,2,1,0:T(8,128)(2,1)S(1)}, u32[]{:S(2)}, u32[]{:S(2)}) collective-permute-start(bf16[4,2,16,128]{3,2,1,0:T(8,128)(2,1)S(1)} %get-tuple-element.27), channel_id=1, source_target_pairs={{0,4},{1,5},{2,6},{3,7},{4,0},{5,1},{6,2},{7,3},{8,12},{9,13},{10,... | collective-permute-start | bytes 98312 | tf_op jit(solution)/shard_map/ppermute | solution.py:263
  42.5 0.7 %collective-permute-start.18 = (bf16[4,2,16,128]{3,2,1,0:T(8,128)(2,1)S(1)}, bf16[4,2,16,128]{3,2,1,0:T(8,128)(2,1)S(1)}, u32[]{:S(2)}, u32[]{:S(2)}) collective-permute-start(bf16[4,2,16,128]{3,2,1,0:T(8,128)(2,1)S(1)} %get-tuple-element.28), channel_id=1, source_target_pairs={{0,6},{1,7},{2,4},{3,5},{4,2},{5,3},{6,0},{7,1},{8,14},{9,15},{10,... | collective-permute-start | bytes 98312 | tf_op jit(solution)/shard_map/ppermute | solution.py:263
  43.2 0.5 %collective-permute-start.15 = (bf16[4,2,16,128]{3,2,1,0:T(8,128)(2,1)S(1)}, bf16[4,2,16,128]{3,2,1,0:T(8,128)(2,1)S(1)}, u32[]{:S(2)}, u32[]{:S(2)}) collective-permute-start(bf16[4,2,16,128]{3,2,1,0:T(8,128)(2,1)S(1)} %collective-permute-done.14.refs_2_), channel_id=1, source_target_pairs={{0,1},{1,0},{2,3},{3,2},{4,5},{5,4},{6,7},{7,6},{8,9},{9,8},{10,11... | collective-permute-start | bytes 98312 | tf_op jit(solution)/shard_map/ppermute | solution.py:263
  43.7 0.9 %collective-permute-done.16.refs_4_ = bf16[4,2,16,128]{3,2,1,0:T(8,128)(2,1)S(1)} collective-permute-done((bf16[4,2,16,128]{3,2,1,0:T(8,128)(2,1)S(1)}, bf16[4,2,16,128]{3,2,1,0:T(8,128)(2,1)S(1)}, u32[]{:S(2)}, u32[]{:S(2)}) %collective-permute-start.16) | collective-permute-done | bytes 32800 | tf_op jit(solution)/shard_map/ppermute | solution.py:263
  44.7 3.6 %collective-permute-done.18.refs_6_ = bf16[4,2,16,128]{3,2,1,0:T(8,128)(2,1)S(1)} collective-permute-done((bf16[4,2,16,128]{3,2,1,0:T(8,128)(2,1)S(1)}, bf16[4,2,16,128]{3,2,1,0:T(8,128)(2,1)S(1)}, u32[]{:S(2)}, u32[]{:S(2)}) %collective-permute-start.18) | collective-permute-done | bytes 32800 | tf_op jit(solution)/shard_map/ppermute | solution.py:263
  48.3 1.2 %collective-permute-done.19.refs_7_ = bf16[4,2,16,128]{3,2,1,0:T(8,128)(2,1)S(1)} collective-permute-done((bf16[4,2,16,128]{3,2,1,0:T(8,128)(2,1)S(1)}, bf16[4,2,16,128]{3,2,1,0:T(8,128)(2,1)S(1)}, u32[]{:S(2)}, u32[]{:S(2)}) %collective-permute-start.19) | collective-permute-done | bytes 32800 | tf_op jit(solution)/shard_map/ppermute | solution.py:263
  49.5 1.3 %gather_beams.1 = f32[25,16,128]{2,1,0:T(8,128)} custom-call(s32[2]{0:T(128)S(1)} %pad_add_fusion.place_ref, bf16[4,2,16,128]{3,2,1,0:T(8,128)(2,1)S(1)} %get-tuple-element.25.refs_0_, bf16[4,2,16,128]{3,2,1,0:T(8,128)(2,1)S(1)} %collective-permute-done.13.refs_1_, bf16[4,2,16,128]{3,2,1,0:T(8,128)(2,1)S(1)} %collective-permute-done.14.refs_2_, ...), custom_call_target="tpu_custom_call" | custom-call | tf_op jit(solution)/shard_map/gather_beams/pallas_call | solution.py:239
  (39 shorter events, 0.7 us)
Async XLA Ops:
  0.1 19.2 %copy-start.1 = (s32[256]{0:T(256)S(1)}, s32[256]{0:T(256)}, u32[]{:S(2)}) copy-start(s32[256]{0:T(256)} %param.7) | copy-start | bytes 3076
  5.1 25.1 %copy-start = (s32[32,16]{0,1:T(8,128)S(1)}, s32[32,16]{0,1:T(8,128)}, u32[]{:S(2)}) copy-start(s32[32,16]{0,1:T(8,128)} %param.6) | copy-start | bytes 6148
  5.1 14.5 %collective-permute-start.6 = (f16[2,13,32,128]{3,2,1,0:T(8,128)(2,1)S(1)}, f16[2,13,32,128]{3,2,1,0:T(8,128)(2,1)S(1)}, u32[]{:S(2)}, u32[]{:S(2)}) collective-permute-start(f16[2,13,32,128]{3,2,1,0:T(8,128)(2,1)S(1)} %multiply_convert_fusion.2), channel_id=1, source_target_pairs={{0,24},{8,16},{16,8},{24,0},{1,25},{9,17},{17,9},{25,1},{2,26},{10... | collective-permute-start | bytes 638984 | tf_op jit(solution)/shard_map/ppermute | solution.py:263
  9.2 10.7 %collective-permute-start.7 = (f16[2,13,32,128]{3,2,1,0:T(8,128)(2,1)S(1)}, f16[2,13,32,128]{3,2,1,0:T(8,128)(2,1)S(1)}, u32[]{:S(2)}, u32[]{:S(2)}) collective-permute-start(f16[2,13,32,128]{3,2,1,0:T(8,128)(2,1)S(1)} %multiply_convert_fusion.1), channel_id=1, source_target_pairs={{0,16},{8,24},{16,0},{24,8},{1,17},{9,25},{17,1},{25,9},{2,18},{10... | collective-permute-start | bytes 638984 | tf_op jit(solution)/shard_map/ppermute | solution.py:263
  9.8 10.6 %collective-permute-start.8 = (f16[2,13,32,128]{3,2,1,0:T(8,128)(2,1)S(1)}, f16[2,13,32,128]{3,2,1,0:T(8,128)(2,1)S(1)}, u32[]{:S(2)}, u32[]{:S(2)}) collective-permute-start(f16[2,13,32,128]{3,2,1,0:T(8,128)(2,1)S(1)} %multiply_convert_fusion), channel_id=1, source_target_pairs={{0,8},{8,0},{16,24},{24,16},{1,9},{9,1},{17,25},{25,17},{2,10},{10... | collective-permute-start | bytes 638984 | tf_op jit(solution)/shard_map/ppermute | solution.py:263
  15.0 9.6 %collective-permute-start = (f16[2,13,32,128]{3,2,1,0:T(8,128)(2,1)S(1)}, f16[2,13,32,128]{3,2,1,0:T(8,128)(2,1)S(1)}, u32[]{:S(2)}, u32[]{:S(2)}) collective-permute-start(f16[2,13,32,128]{3,2,1,0:T(8,128)(2,1)S(1)} %multiply_convert_fusion.5), channel_id=1, source_target_pairs={{0,24},{8,16},{16,8},{24,0},{1,25},{9,17},{17,9},{25,1},{2,26},{10... | collective-permute-start | bytes 638984 | tf_op jit(solution)/shard_map/ppermute | solution.py:263
  18.0 10.0 %collective-permute-start.1 = (f16[2,13,32,128]{3,2,1,0:T(8,128)(2,1)S(1)}, f16[2,13,32,128]{3,2,1,0:T(8,128)(2,1)S(1)}, u32[]{:S(2)}, u32[]{:S(2)}) collective-permute-start(f16[2,13,32,128]{3,2,1,0:T(8,128)(2,1)S(1)} %multiply_convert_fusion.4), channel_id=1, source_target_pairs={{0,16},{8,24},{16,0},{24,8},{1,17},{9,25},{17,1},{25,9},{2,18},{10... | collective-permute-start | bytes 638984 | tf_op jit(solution)/shard_map/ppermute | solution.py:263
  19.7 8.7 %collective-permute-start.2 = (f16[2,13,32,128]{3,2,1,0:T(8,128)(2,1)}, f16[2,13,32,128]{3,2,1,0:T(8,128)(2,1)S(1)}, u32[]{:S(2)}, u32[]{:S(2)}) collective-permute-start(f16[2,13,32,128]{3,2,1,0:T(8,128)(2,1)} %multiply_convert_fusion.3), channel_id=1, source_target_pairs={{0,8},{8,0},{16,24},{24,16},{1,9},{9,1},{17,25},{25,17},{2,10},{10... | collective-permute-start | bytes 638984 | tf_op jit(solution)/shard_map/ppermute | solution.py:263
  20.5 11.8 %collective-permute-start.9 = (bf16[2,7,32,128]{3,2,1,0:T(8,128)(2,1)S(1)}, bf16[2,7,32,128]{3,2,1,0:T(8,128)(2,1)S(1)}, u32[]{:S(2)}, u32[]{:S(2)}) collective-permute-start(bf16[2,7,32,128]{3,2,1,0:T(8,128)(2,1)S(1)} %get-tuple-element.30), channel_id=1, source_target_pairs={{0,4},{1,5},{2,6},{3,7},{4,0},{5,1},{6,2},{7,3},{8,12},{9,13},{10,... | collective-permute-start | bytes 344072 | tf_op jit(solution)/shard_map/ppermute | solution.py:263
  23.2 9.2 %collective-permute-start.11 = (bf16[2,7,32,128]{3,2,1,0:T(8,128)(2,1)S(1)}, bf16[2,7,32,128]{3,2,1,0:T(8,128)(2,1)S(1)}, u32[]{:S(2)}, u32[]{:S(2)}) collective-permute-start(bf16[2,7,32,128]{3,2,1,0:T(8,128)(2,1)S(1)} %get-tuple-element.29), channel_id=1, source_target_pairs={{0,6},{1,7},{2,4},{3,5},{4,2},{5,3},{6,0},{7,1},{8,14},{9,15},{10,... | collective-permute-start | bytes 344072 | tf_op jit(solution)/shard_map/ppermute | solution.py:263
  28.6 5.5 %collective-permute-start.4 = (bf16[2,7,32,128]{3,2,1,0:T(8,128)(2,1)S(1)}, bf16[2,7,32,128]{3,2,1,0:T(8,128)(2,1)S(1)}, u32[]{:S(2)}, u32[]{:S(2)}) collective-permute-start(bf16[2,7,32,128]{3,2,1,0:T(8,128)(2,1)S(1)} %get-tuple-element.31), channel_id=1, source_target_pairs={{0,2},{1,3},{2,0},{3,1},{4,6},{5,7},{6,4},{7,5},{8,10},{9,11},{10,... | collective-permute-start | bytes 344072 | tf_op jit(solution)/shard_map/ppermute | solution.py:263
  30.2 4.0 %collective-permute-start.3 = (bf16[2,7,32,128]{3,2,1,0:T(8,128)(2,1)S(1)}, bf16[2,7,32,128]{3,2,1,0:T(8,128)(2,1)S(1)}, u32[]{:S(2)}, u32[]{:S(2)}) collective-permute-start(bf16[2,7,32,128]{3,2,1,0:T(8,128)(2,1)S(1)} %get-tuple-element.32.refs_0_), channel_id=1, source_target_pairs={{0,1},{1,0},{2,3},{3,2},{4,5},{5,4},{6,7},{7,6},{8,9},{9,8},{10,11... | collective-permute-start | bytes 344072 | tf_op jit(solution)/shard_map/ppermute | solution.py:263
  32.4 1.9 %collective-permute-start.10 = (bf16[2,7,32,128]{3,2,1,0:T(8,128)(2,1)S(1)}, bf16[2,7,32,128]{3,2,1,0:T(8,128)(2,1)S(1)}, u32[]{:S(2)}, u32[]{:S(2)}) collective-permute-start(bf16[2,7,32,128]{3,2,1,0:T(8,128)(2,1)S(1)} %collective-permute-done.9.refs_4_), channel_id=1, source_target_pairs={{0,1},{1,0},{2,3},{3,2},{4,5},{5,4},{6,7},{7,6},{8,9},{9,8},{10,11... | collective-permute-start | bytes 344072 | tf_op jit(solution)/shard_map/ppermute | solution.py:263
  32.4 1.9 %collective-permute-start.12 = (bf16[2,7,32,128]{3,2,1,0:T(8,128)(2,1)S(1)}, bf16[2,7,32,128]{3,2,1,0:T(8,128)(2,1)S(1)}, u32[]{:S(2)}, u32[]{:S(2)}) collective-permute-start(bf16[2,7,32,128]{3,2,1,0:T(8,128)(2,1)S(1)} %collective-permute-done.11.refs_6_), channel_id=1, source_target_pairs={{0,1},{1,0},{2,3},{3,2},{4,5},{5,4},{6,7},{7,6},{8,9},{9,8},{10,11... | collective-permute-start | bytes 344072 | tf_op jit(solution)/shard_map/ppermute | solution.py:263
  34.1 1.3 %collective-permute-start.5 = (bf16[2,7,32,128]{3,2,1,0:T(8,128)(2,1)S(1)}, bf16[2,7,32,128]{3,2,1,0:T(8,128)(2,1)S(1)}, u32[]{:S(2)}, u32[]{:S(2)}) collective-permute-start(bf16[2,7,32,128]{3,2,1,0:T(8,128)(2,1)S(1)} %collective-permute-done.4.refs_2_), channel_id=1, source_target_pairs={{0,1},{1,0},{2,3},{3,2},{4,5},{5,4},{6,7},{7,6},{8,9},{9,8},{10,11... | collective-permute-start | bytes 344072 | tf_op jit(solution)/shard_map/ppermute | solution.py:263
  38.8 4.5 %collective-permute-start.14 = (bf16[4,2,16,128]{3,2,1,0:T(8,128)(2,1)S(1)}, bf16[4,2,16,128]{3,2,1,0:T(8,128)(2,1)S(1)}, u32[]{:S(2)}, u32[]{:S(2)}) collective-permute-start(bf16[4,2,16,128]{3,2,1,0:T(8,128)(2,1)S(1)} %get-tuple-element.26), channel_id=1, source_target_pairs={{0,2},{1,3},{2,0},{3,1},{4,6},{5,7},{6,4},{7,5},{8,10},{9,11},{10,... | collective-permute-start | bytes 98312 | tf_op jit(solution)/shard_map/ppermute | solution.py:263
  39.8 4.9 %collective-permute-start.16 = (bf16[4,2,16,128]{3,2,1,0:T(8,128)(2,1)S(1)}, bf16[4,2,16,128]{3,2,1,0:T(8,128)(2,1)S(1)}, u32[]{:S(2)}, u32[]{:S(2)}) collective-permute-start(bf16[4,2,16,128]{3,2,1,0:T(8,128)(2,1)S(1)} %get-tuple-element.27), channel_id=1, source_target_pairs={{0,4},{1,5},{2,6},{3,7},{4,0},{5,1},{6,2},{7,3},{8,12},{9,13},{10,... | collective-permute-start | bytes 98312 | tf_op jit(solution)/shard_map/ppermute | solution.py:263
  42.5 5.7 %collective-permute-start.18 = (bf16[4,2,16,128]{3,2,1,0:T(8,128)(2,1)S(1)}, bf16[4,2,16,128]{3,2,1,0:T(8,128)(2,1)S(1)}, u32[]{:S(2)}, u32[]{:S(2)}) collective-permute-start(bf16[4,2,16,128]{3,2,1,0:T(8,128)(2,1)S(1)} %get-tuple-element.28), channel_id=1, source_target_pairs={{0,6},{1,7},{2,4},{3,5},{4,2},{5,3},{6,0},{7,1},{8,14},{9,15},{10,... | collective-permute-start | bytes 98312 | tf_op jit(solution)/shard_map/ppermute | solution.py:263
  43.2 5.0 %collective-permute-start.13 = (bf16[4,2,16,128]{3,2,1,0:T(8,128)(2,1)S(1)}, bf16[4,2,16,128]{3,2,1,0:T(8,128)(2,1)S(1)}, u32[]{:S(2)}, u32[]{:S(2)}) collective-permute-start(bf16[4,2,16,128]{3,2,1,0:T(8,128)(2,1)S(1)} %get-tuple-element.25.refs_0_), channel_id=1, source_target_pairs={{0,1},{1,0},{2,3},{3,2},{4,5},{5,4},{6,7},{7,6},{8,9},{9,8},{10,11... | collective-permute-start | bytes 98312 | tf_op jit(solution)/shard_map/ppermute | solution.py:263
  43.2 5.0 %collective-permute-start.15 = (bf16[4,2,16,128]{3,2,1,0:T(8,128)(2,1)S(1)}, bf16[4,2,16,128]{3,2,1,0:T(8,128)(2,1)S(1)}, u32[]{:S(2)}, u32[]{:S(2)}) collective-permute-start(bf16[4,2,16,128]{3,2,1,0:T(8,128)(2,1)S(1)} %collective-permute-done.14.refs_2_), channel_id=1, source_target_pairs={{0,1},{1,0},{2,3},{3,2},{4,5},{5,4},{6,7},{7,6},{8,9},{9,8},{10,11... | collective-permute-start | bytes 98312 | tf_op jit(solution)/shard_map/ppermute | solution.py:263
  44.7 3.6 %collective-permute-start.17 = (bf16[4,2,16,128]{3,2,1,0:T(8,128)(2,1)S(1)}, bf16[4,2,16,128]{3,2,1,0:T(8,128)(2,1)S(1)}, u32[]{:S(2)}, u32[]{:S(2)}) collective-permute-start(bf16[4,2,16,128]{3,2,1,0:T(8,128)(2,1)S(1)} %collective-permute-done.16.refs_4_), channel_id=1, source_target_pairs={{0,1},{1,0},{2,3},{3,2},{4,5},{5,4},{6,7},{7,6},{8,9},{9,8},{10,11... | collective-permute-start | bytes 98312 | tf_op jit(solution)/shard_map/ppermute | solution.py:263
  48.2 1.2 %collective-permute-start.19 = (bf16[4,2,16,128]{3,2,1,0:T(8,128)(2,1)S(1)}, bf16[4,2,16,128]{3,2,1,0:T(8,128)(2,1)S(1)}, u32[]{:S(2)}, u32[]{:S(2)}) collective-permute-start(bf16[4,2,16,128]{3,2,1,0:T(8,128)(2,1)S(1)} %collective-permute-done.18.refs_6_), channel_id=1, source_target_pairs={{0,1},{1,0},{2,3},{3,2},{4,5},{5,4},{6,7},{7,6},{8,9},{9,8},{10,11... | collective-permute-start | bytes 98312 | tf_op jit(solution)/shard_map/ppermute | solution.py:263

commit v6 on v5

--- a/solution.py
+++ b/solution.py
@@ -27,7 +27,7 @@
 BF16 = jnp.bfloat16
 
 
-def beam_kernel(place_ref, w_hbm, x_hbm, *refs):
+def beam_kernel(here_ref, start_ref, w_hbm, x_hbm, *refs):
     out_refs = refs[:-6]
     w_ref, x_ref, first_ref, second_ref, mixed_ref, sems = refs[-6:]
     groups = len(out_refs)
@@ -52,8 +52,8 @@
     weave = weave.astype(F32).astype(BF16)
     w_copy.wait()
     for group in range(groups):
-        owner = place_ref[0] ^ group
-        chosen = pl.ds(owner * (w_ref.shape[0] // groups) + place_ref[1], count)
+        owner = here_ref[0] ^ group
+        chosen = pl.ds(owner * (w_ref.shape[0] // groups) + start_ref[0], count)
         weights = w_ref[chosen].astype(F32)
         real = weights[:, 0, :]
         imag = weights[:, 1, :]
@@ -82,7 +82,7 @@
             out_ref[1, :, place, :] = rows[half + top : half + top + count]
 
 
-def partial_beams(streams, weights, place, groups, count):
+def partial_beams(streams, weights, here, start, groups, count):
     depth, _, samples = streams.shape
     beams = groups * count
     width = SLICE * LANES
@@ -90,7 +90,7 @@
     columns = -(-depth // LANES) * LANES
     return pl.pallas_call(
         beam_kernel,
-        in_specs=[pl.BlockSpec(memory_space=pltpu.SMEM)]
+        in_specs=[pl.BlockSpec(memory_space=pltpu.SMEM)] * 2
         + [pl.BlockSpec(memory_space=pltpu.HBM)] * 2,
         out_specs=[pl.BlockSpec(memory_space=pltpu.VMEM)] * groups,
         out_shape=[jax.ShapeDtypeStruct((2, count, samples // LANES, LANES), F32)] * groups,
@@ -109,16 +109,16 @@
             transcendentals=0,
         ),
         name="partial_beams",
-    )(place, weights, streams)
-
-
-def lag_kernel(scale, count, place_ref, sign_ref, gate_ref, *refs):
+    )(here.reshape(1), start.reshape(1), weights, streams)
+
+
+def lag_kernel(scale, count, chip_ref, core_ref, sign_ref, gate_ref, *refs):
     pieces_in = refs[:count]
     out_refs = refs[count:-4]
     x_ref, both_ref, lag_ref, sum_ref = refs[-4:]
     sources, _, slots, rows, _ = x_ref.shape
-    chip = place_ref[0]
-    core = place_ref[1]
+    chip = chip_ref[0]
+    core = core_ref[0]
     taken = pieces_in[0].shape[1] - slots
     for index, ref in enumerate(pieces_in):
         source = 2 * (chip ^ (index // 2)) + (core ^ (index % 2))
@@ -205,7 +205,7 @@
     vmem = pl.BlockSpec(memory_space=pltpu.VMEM)
     return pl.pallas_call(
         functools.partial(lag_kernel, scale, len(pieces)),
-        in_specs=[pl.BlockSpec(memory_space=pltpu.SMEM)] + [vmem] * (2 + len(pieces)),
+        in_specs=[pl.BlockSpec(memory_space=pltpu.SMEM)] * 2 + [vmem] * (2 + len(pieces)),
         out_specs=[vmem] * chips,
         out_shape=[out] * chips,
         scratch_shapes=[
@@ -216,17 +216,17 @@
         ],
         compiler_params=pltpu.CompilerParams(vmem_limit_bytes=VMEM),
         name="lag_profiles",
-    )(place, signs, gate_hot, *pieces)
-
-
-def gather_kernel(width, place_ref, *refs):
+    )(*place, signs, gate_hot, *pieces)
+
+
+def gather_kernel(width, chip_ref, core_ref, *refs):
     pieces_in = refs[:-1]
     out_ref = refs[-1]
     chips = len(pieces_in) // 2
     beams = out_ref.shape[0]
     slots = pieces_in[0].shape[0]
-    chip = place_ref[0]
-    core = place_ref[1]
+    chip = chip_ref[0]
+    core = core_ref[0]
     for index, ref in enumerate(pieces_in):
         first = (chip ^ (index // 2)) * (beams - width) // (chips - 1)
         first += (core ^ (index % 2)) * (width - slots)
@@ -238,12 +238,12 @@
     vmem = pl.BlockSpec(memory_space=pltpu.VMEM)
     return pl.pallas_call(
         functools.partial(gather_kernel, width),
-        in_specs=[pl.BlockSpec(memory_space=pltpu.SMEM)] + [vmem] * len(pieces),
+        in_specs=[pl.BlockSpec(memory_space=pltpu.SMEM)] * 2 + [vmem] * len(pieces),
         out_specs=vmem,
         out_shape=jax.ShapeDtypeStruct((beams, gates, LANES), F32),
         compiler_params=pltpu.CompilerParams(vmem_limit_bytes=VMEM),
         name="gather_beams",
-    )(place, *pieces)
+    )(*place, *pieces)
 
 
 def sign_rows(code_signs, periods, row_groups):
@@ -282,8 +282,8 @@
     periods = samples * sources // IPP_LEN
     scale = 1.0 / math.sqrt(periods * IPP_LEN / GATES)
     here = lax.axis_index("sub")
-    place = jnp.stack([lax.axis_index("tm") // 2, lax.axis_index("tm") % 2]).astype(jnp.int32)
-    chip = place[0]
+    chip = lax.axis_index("tm") // 2
+    place = (chip.reshape(1), (lax.axis_index("tm") % 2).reshape(1))
     signs = sign_rows(code_signs, periods, sources // PER_ROW)
     gate_hot = gate_rows(gate_map)
     weights = pltpu.with_memory_space_constraint(beam_weights.transpose(1, 0, 2), pltpu.HBM)
@@ -300,8 +300,7 @@
     blocks = [None] * chips
     for far in (True, False):
         start = jnp.where(low == far, beams - count, 0).astype(jnp.int32)
-        chosen = jnp.stack([here, start]).astype(jnp.int32)
-        partial = partial_beams(by_channel, weights, chosen, groups, count)
+        partial = partial_beams(by_channel, weights, here, start, groups, count)
         total = partial[0]
         for step in range(groups - 1, 0, -1):
             came = exchanged((partial[step] * gain).astype(jnp.float16), "sub", step)

time: 50.9 us -> 49.1 us (0.965)
  Pallas kernels: 14.6 us -> 12.4 us
    pallas_call x2, Pallas kernels: 9.98 us -> 8.92 us  [partial_beams(): pl.pallas_call(beam_kernel, in_specs=[pl.BlockSpec(memory_space=pltpu.SME...]
    pallas_call x1, Pallas kernels: 1.26 us -> 0.7 us  [gather_beams(): pl.pallas_call(functools.partial(gather_kernel, width), in_specs=[pl.Bloc...]
    ppermute x20, waiting for transfers between devices: 14.5 us -> 15 us  [exchanged(): lax.ppermute(block, axis, [(i, i ^ step) for i in range(lax.axis_size(axi...]
    pallas_call x1, Pallas kernels: 3.36 us -> 2.81 us  [lag_profiles(): pl.pallas_call(functools.partial(lag_kernel, scale, len(pieces)), in_spec...]
  transfers between devices with their start and end apart: 20 -> 20, of which waited for: 9 -> 10; matrix products, arithmetic and copies ran while one was open for 3% -> 3% of each run, Pallas kernels for 10% -> 9%
where the time goes in v6:
time: 49.1 us; the launch traced here: 49 us
  starting transfers between devices  19.7 us (40%)
  waiting for transfers between devices  15 us (31%)
  Pallas kernels  12.4 us (25%)
  other arithmetic  1.29 us (3%)
    ppermute x20, starting transfers between devices, exchanged(): lax.ppermute(block, axis, [(i, i ^ step) for i in range(lax.axis_size(axi...  19.7 us
    ppermute x20, waiting for transfers between devices, exchanged(): lax.ppermute(block, axis, [(i, i ^ step) for i in range(lax.axis_size(axi...  15 us
    pallas_call x2, Pallas kernels, partial_beams(): pl.pallas_call(beam_kernel, in_specs=[pl.BlockSpec(memory_space=pltpu.SME...  8.92 us
    pallas_call x1, Pallas kernels, lag_profiles(): pl.pallas_call(functools.partial(lag_kernel, scale, len(pieces)), in_spec...  2.81 us
  transfers between devices with their start and end apart: 20, of which 10 were waited for; matrix products, arithmetic and copies ran while one was open for 3% of the time, Pallas kernels for 9%

profile of v6, /device:TPU:0, one launch (start us, length us, event | category | flops | bytes accessed | tf_op | source)
XLA Modules:
  0.0 49.0 jit_solution(18142290359617636483)
XLA Ops:
  0.0 4.5 %partial_beams.3 = (f32[2,13,32,128]{3,2,1,0:T(8,128)S(1)}, f32[2,13,32,128]{3,2,1,0:T(8,128)S(1)}, f32[2,13,32,128]{3,2,1,0:T(8,128)S(1)}, f32[2,13,32,128]{3,2,1,0:T(8,128)S(1)}) custom-call(s32[1]{0:T(128)} %bitcast.7.here_ref, s32[1]{0:T(128)} %bitcast.11.start_ref, bf16[100,2,540]{2,1,0:T(2,128)(2,1)} %bitcast.19, bf16[540,2,4096]{2,1,0:T(2,128)(2,1)} %bitcast.17), custom_call_target="tpu_custom_call" | custom-call | flops 920125440 | bytes 10551296 | tf_op jit(solution)/shard_map/partial_beams/pallas_call | solution.py:91
  4.5 4.0 %collective-permute-start.6 = (f16[2,13,32,128]{3,2,1,0:T(8,128)(2,1)S(1)}, f16[2,13,32,128]{3,2,1,0:T(8,128)(2,1)S(1)}, u32[]{:S(2)}, u32[]{:S(2)}) collective-permute-start(f16[2,13,32,128]{3,2,1,0:T(8,128)(2,1)S(1)} %multiply_convert_fusion.2), channel_id=1, source_target_pairs={{0,24},{8,16},{16,8},{24,0},{1,25},{9,17},{17,9},{25,1},{2,26},{10... | collective-permute-start | bytes 638984 | tf_op jit(solution)/shard_map/ppermute | solution.py:263
  8.6 0.6 %collective-permute-start.7 = (f16[2,13,32,128]{3,2,1,0:T(8,128)(2,1)S(1)}, f16[2,13,32,128]{3,2,1,0:T(8,128)(2,1)S(1)}, u32[]{:S(2)}, u32[]{:S(2)}) collective-permute-start(f16[2,13,32,128]{3,2,1,0:T(8,128)(2,1)S(1)} %multiply_convert_fusion.1), channel_id=1, source_target_pairs={{0,16},{8,24},{16,0},{24,8},{1,17},{9,25},{17,1},{25,9},{2,18},{10... | collective-permute-start | bytes 638984 | tf_op jit(solution)/shard_map/ppermute | solution.py:263
  9.2 0.1 collective-permute-start.8
  9.3 4.5 %partial_beams.2 = (f32[2,13,32,128]{3,2,1,0:T(8,128)S(1)}, f32[2,13,32,128]{3,2,1,0:T(8,128)S(1)}, f32[2,13,32,128]{3,2,1,0:T(8,128)S(1)}, f32[2,13,32,128]{3,2,1,0:T(8,128)S(1)}) custom-call(s32[1]{0:T(128)} %bitcast.7.here_ref, s32[1]{0:T(128)} %bitcast.8.start_ref, bf16[100,2,540]{2,1,0:T(2,128)(2,1)} %bitcast.20, bf16[540,2,4096]{2,1,0:T(2,128)(2,1)} %bitcast.18), custom_call_target="tpu_custom_call" | custom-call | flops 920125440 | bytes 10551296 | tf_op jit(solution)/shard_map/partial_beams/pallas_call | solution.py:91
  13.8 3.0 %collective-permute-start = (f16[2,13,32,128]{3,2,1,0:T(8,128)(2,1)S(1)}, f16[2,13,32,128]{3,2,1,0:T(8,128)(2,1)S(1)}, u32[]{:S(2)}, u32[]{:S(2)}) collective-permute-start(f16[2,13,32,128]{3,2,1,0:T(8,128)(2,1)S(1)} %multiply_convert_fusion.5), channel_id=1, source_target_pairs={{0,24},{8,16},{16,8},{24,0},{1,25},{9,17},{17,9},{25,1},{2,26},{10... | collective-permute-start | bytes 638984 | tf_op jit(solution)/shard_map/ppermute | solution.py:263
  16.9 0.6 %collective-permute-start.1 = (f16[2,13,32,128]{3,2,1,0:T(8,128)(2,1)S(1)}, f16[2,13,32,128]{3,2,1,0:T(8,128)(2,1)S(1)}, u32[]{:S(2)}, u32[]{:S(2)}) collective-permute-start(f16[2,13,32,128]{3,2,1,0:T(8,128)(2,1)S(1)} %multiply_convert_fusion.4), channel_id=1, source_target_pairs={{0,16},{8,24},{16,0},{24,8},{1,17},{9,25},{17,1},{25,9},{2,18},{10... | collective-permute-start | bytes 638984 | tf_op jit(solution)/shard_map/ppermute | solution.py:263
  17.4 0.7 %multiply_convert_fusion.3 = f16[2,13,32,128]{3,2,1,0:T(8,128)(2,1)} fusion(f32[2,13,32,128]{3,2,1,0:T(8,128)S(1)} %get-tuple-element.20), kind=kLoop, calls=%fused_computation.5 | loop fusion | flops 212992 | bytes 638976 | tf_op jit(solution)/shard_map/convert_element_type | solution.py:306
  18.3 0.1 copy.10
  18.5 0.2 collective-permute-start.2
  18.7 0.5 %collective-permute-done.7 = f16[2,13,32,128]{3,2,1,0:T(8,128)(2,1)S(1)} collective-permute-done((f16[2,13,32,128]{3,2,1,0:T(8,128)(2,1)S(1)}, f16[2,13,32,128]{3,2,1,0:T(8,128)(2,1)S(1)}, u32[]{:S(2)}, u32[]{:S(2)}) %collective-permute-start.7) | collective-permute-done | bytes 213024 | tf_op jit(solution)/shard_map/ppermute | solution.py:263
  19.3 0.5 %collective-permute-done.8 = f16[2,13,32,128]{3,2,1,0:T(8,128)(2,1)S(1)} collective-permute-done((f16[2,13,32,128]{3,2,1,0:T(8,128)(2,1)S(1)}, f16[2,13,32,128]{3,2,1,0:T(8,128)(2,1)S(1)}, u32[]{:S(2)}, u32[]{:S(2)}) %collective-permute-start.8) | collective-permute-done | bytes 213024 | tf_op jit(solution)/shard_map/ppermute | solution.py:263
  19.8 0.1 add_convert_fusion
  19.9 2.7 %collective-permute-start.9 = (bf16[2,7,32,128]{3,2,1,0:T(8,128)(2,1)S(1)}, bf16[2,7,32,128]{3,2,1,0:T(8,128)(2,1)S(1)}, u32[]{:S(2)}, u32[]{:S(2)}) collective-permute-start(bf16[2,7,32,128]{3,2,1,0:T(8,128)(2,1)S(1)} %get-tuple-element.30), channel_id=1, source_target_pairs={{0,4},{1,5},{2,6},{3,7},{4,0},{5,1},{6,2},{7,3},{8,12},{9,13},{10,... | collective-permute-start | bytes 344072 | tf_op jit(solution)/shard_map/ppermute | solution.py:263
  22.6 1.3 %collective-permute-start.11 = (bf16[2,7,32,128]{3,2,1,0:T(8,128)(2,1)S(1)}, bf16[2,7,32,128]{3,2,1,0:T(8,128)(2,1)S(1)}, u32[]{:S(2)}, u32[]{:S(2)}) collective-permute-start(bf16[2,7,32,128]{3,2,1,0:T(8,128)(2,1)S(1)} %get-tuple-element.29), channel_id=1, source_target_pairs={{0,6},{1,7},{2,4},{3,5},{4,2},{5,3},{6,0},{7,1},{8,14},{9,15},{10,... | collective-permute-start | bytes 344072 | tf_op jit(solution)/shard_map/ppermute | solution.py:263
  24.0 3.5 %collective-permute-done.1 = f16[2,13,32,128]{3,2,1,0:T(8,128)(2,1)S(1)} collective-permute-done((f16[2,13,32,128]{3,2,1,0:T(8,128)(2,1)S(1)}, f16[2,13,32,128]{3,2,1,0:T(8,128)(2,1)S(1)}, u32[]{:S(2)}, u32[]{:S(2)}) %collective-permute-start.1) | collective-permute-done | bytes 213024 | tf_op jit(solution)/shard_map/ppermute | solution.py:263
  27.5 0.3 collective-permute-done.2
  27.8 0.1 add_convert_fusion.1
  28.0 1.7 %collective-permute-start.4 = (bf16[2,7,32,128]{3,2,1,0:T(8,128)(2,1)S(1)}, bf16[2,7,32,128]{3,2,1,0:T(8,128)(2,1)S(1)}, u32[]{:S(2)}, u32[]{:S(2)}) collective-permute-start(bf16[2,7,32,128]{3,2,1,0:T(8,128)(2,1)S(1)} %get-tuple-element.31), channel_id=1, source_target_pairs={{0,2},{1,3},{2,0},{3,1},{4,6},{5,7},{6,4},{7,5},{8,10},{9,11},{10,... | collective-permute-start | bytes 344072 | tf_op jit(solution)/shard_map/ppermute | solution.py:263
  29.8 2.0 %collective-permute-done.9.refs_4_ = bf16[2,7,32,128]{3,2,1,0:T(8,128)(2,1)S(1)} collective-permute-done((bf16[2,7,32,128]{3,2,1,0:T(8,128)(2,1)S(1)}, bf16[2,7,32,128]{3,2,1,0:T(8,128)(2,1)S(1)}, u32[]{:S(2)}, u32[]{:S(2)}) %collective-permute-start.9) | collective-permute-done | bytes 114720 | tf_op jit(solution)/shard_map/ppermute | solution.py:263
  31.8 0.5 %collective-permute-start.12 = (bf16[2,7,32,128]{3,2,1,0:T(8,128)(2,1)S(1)}, bf16[2,7,32,128]{3,2,1,0:T(8,128)(2,1)S(1)}, u32[]{:S(2)}, u32[]{:S(2)}) collective-permute-start(bf16[2,7,32,128]{3,2,1,0:T(8,128)(2,1)S(1)} %collective-permute-done.11.refs_6_), channel_id=1, source_target_pairs={{0,1},{1,0},{2,3},{3,2},{4,5},{5,4},{6,7},{7,6},{8,9},{9,8},{10,11... | collective-permute-start | bytes 344072 | tf_op jit(solution)/shard_map/ppermute | solution.py:263
  32.3 1.2 %collective-permute-done.4.refs_2_ = bf16[2,7,32,128]{3,2,1,0:T(8,128)(2,1)S(1)} collective-permute-done((bf16[2,7,32,128]{3,2,1,0:T(8,128)(2,1)S(1)}, bf16[2,7,32,128]{3,2,1,0:T(8,128)(2,1)S(1)}, u32[]{:S(2)}, u32[]{:S(2)}) %collective-permute-start.4) | collective-permute-done | bytes 114720 | tf_op jit(solution)/shard_map/ppermute | solution.py:263
  33.5 1.3 %collective-permute-done.5.refs_3_ = bf16[2,7,32,128]{3,2,1,0:T(8,128)(2,1)S(1)} collective-permute-done((bf16[2,7,32,128]{3,2,1,0:T(8,128)(2,1)S(1)}, bf16[2,7,32,128]{3,2,1,0:T(8,128)(2,1)S(1)}, u32[]{:S(2)}, u32[]{:S(2)}) %collective-permute-start.5) | collective-permute-done | bytes 114720 | tf_op jit(solution)/shard_map/ppermute | solution.py:263
  34.8 2.8 %lag_profiles.1 = (bf16[4,2,16,128]{3,2,1,0:T(8,128)(2,1)S(1)}, bf16[4,2,16,128]{3,2,1,0:T(8,128)(2,1)S(1)}, bf16[4,2,16,128]{3,2,1,0:T(8,128)(2,1)S(1)}, bf16[4,2,16,128]{3,2,1,0:T(8,128)(2,1)S(1)}) custom-call(s32[1]{0:T(128)} %bitcast.chip_ref, s32[1]{0:T(128)} %bitcast.1.core_ref, f32[2,32,128]{2,1,0:T(8,128)S(1)} %bitcast.16, ...), custom_call_target="tpu_custom_call" | custom-call | tf_op jit(solution)/shard_map/lag_profiles/pallas_call | solution.py:206
  37.6 1.0 %collective-permute-start.14 = (bf16[4,2,16,128]{3,2,1,0:T(8,128)(2,1)S(1)}, bf16[4,2,16,128]{3,2,1,0:T(8,128)(2,1)S(1)}, u32[]{:S(2)}, u32[]{:S(2)}) collective-permute-start(bf16[4,2,16,128]{3,2,1,0:T(8,128)(2,1)S(1)} %get-tuple-element.26), channel_id=1, source_target_pairs={{0,2},{1,3},{2,0},{3,1},{4,6},{5,7},{6,4},{7,5},{8,10},{9,11},{10,... | collective-permute-start | bytes 98312 | tf_op jit(solution)/shard_map/ppermute | solution.py:263
  38.6 2.7 %collective-permute-start.16 = (bf16[4,2,16,128]{3,2,1,0:T(8,128)(2,1)S(1)}, bf16[4,2,16,128]{3,2,1,0:T(8,128)(2,1)S(1)}, u32[]{:S(2)}, u32[]{:S(2)}) collective-permute-start(bf16[4,2,16,128]{3,2,1,0:T(8,128)(2,1)S(1)} %get-tuple-element.27), channel_id=1, source_target_pairs={{0,4},{1,5},{2,6},{3,7},{4,0},{5,1},{6,2},{7,3},{8,12},{9,13},{10,... | collective-permute-start | bytes 98312 | tf_op jit(solution)/shard_map/ppermute | solution.py:263
  41.4 0.7 %collective-permute-start.18 = (bf16[4,2,16,128]{3,2,1,0:T(8,128)(2,1)S(1)}, bf16[4,2,16,128]{3,2,1,0:T(8,128)(2,1)S(1)}, u32[]{:S(2)}, u32[]{:S(2)}) collective-permute-start(bf16[4,2,16,128]{3,2,1,0:T(8,128)(2,1)S(1)} %get-tuple-element.28), channel_id=1, source_target_pairs={{0,6},{1,7},{2,4},{3,5},{4,2},{5,3},{6,0},{7,1},{8,14},{9,15},{10,... | collective-permute-start | bytes 98312 | tf_op jit(solution)/shard_map/ppermute | solution.py:263
  42.1 0.5 %collective-permute-start.15 = (bf16[4,2,16,128]{3,2,1,0:T(8,128)(2,1)S(1)}, bf16[4,2,16,128]{3,2,1,0:T(8,128)(2,1)S(1)}, u32[]{:S(2)}, u32[]{:S(2)}) collective-permute-start(bf16[4,2,16,128]{3,2,1,0:T(8,128)(2,1)S(1)} %collective-permute-done.14.refs_2_), channel_id=1, source_target_pairs={{0,1},{1,0},{2,3},{3,2},{4,5},{5,4},{6,7},{7,6},{8,9},{9,8},{10,11... | collective-permute-start | bytes 98312 | tf_op jit(solution)/shard_map/ppermute | solution.py:263
  42.6 0.9 %collective-permute-done.16.refs_4_ = bf16[4,2,16,128]{3,2,1,0:T(8,128)(2,1)S(1)} collective-permute-done((bf16[4,2,16,128]{3,2,1,0:T(8,128)(2,1)S(1)}, bf16[4,2,16,128]{3,2,1,0:T(8,128)(2,1)S(1)}, u32[]{:S(2)}, u32[]{:S(2)}) %collective-permute-start.16) | collective-permute-done | bytes 32800 | tf_op jit(solution)/shard_map/ppermute | solution.py:263
  43.5 3.6 %collective-permute-done.18.refs_6_ = bf16[4,2,16,128]{3,2,1,0:T(8,128)(2,1)S(1)} collective-permute-done((bf16[4,2,16,128]{3,2,1,0:T(8,128)(2,1)S(1)}, bf16[4,2,16,128]{3,2,1,0:T(8,128)(2,1)S(1)}, u32[]{:S(2)}, u32[]{:S(2)}) %collective-permute-start.18) | collective-permute-done | bytes 32800 | tf_op jit(solution)/shard_map/ppermute | solution.py:263
  47.1 1.2 %collective-permute-done.19.refs_7_ = bf16[4,2,16,128]{3,2,1,0:T(8,128)(2,1)S(1)} collective-permute-done((bf16[4,2,16,128]{3,2,1,0:T(8,128)(2,1)S(1)}, bf16[4,2,16,128]{3,2,1,0:T(8,128)(2,1)S(1)}, u32[]{:S(2)}, u32[]{:S(2)}) %collective-permute-start.19) | collective-permute-done | bytes 32800 | tf_op jit(solution)/shard_map/ppermute | solution.py:263
  48.3 0.7 %gather_beams.1 = f32[25,16,128]{2,1,0:T(8,128)} custom-call(s32[1]{0:T(128)} %bitcast.chip_ref, s32[1]{0:T(128)} %bitcast.1.core_ref, bf16[4,2,16,128]{3,2,1,0:T(8,128)(2,1)S(1)} %get-tuple-element.25.refs_0_, bf16[4,2,16,128]{3,2,1,0:T(8,128)(2,1)S(1)} %collective-permute-done.13.refs_1_, bf16[4,2,16,128]{3,2,1,0:T(8,128)(2,1)S(1)} %collective-permute-done.14.refs_2_, ...), custom_call_target="tpu_custom_call" | custom-call | tf_op jit(solution)/shard_map/gather_beams/pallas_call | solution.py:239
  (37 shorter events, 0.7 us)
Async XLA Ops:
  0.0 18.2 %copy-start.1 = (s32[256]{0:T(256)S(1)}, s32[256]{0:T(256)}, u32[]{:S(2)}) copy-start(s32[256]{0:T(256)} %param.7) | copy-start | bytes 3076
  4.5 14.0 %copy-start = (s32[32,16]{0,1:T(8,128)S(1)}, s32[32,16]{0,1:T(8,128)}, u32[]{:S(2)}) copy-start(s32[32,16]{0,1:T(8,128)} %param.6) | copy-start | bytes 6148
  4.5 13.9 %collective-permute-start.6 = (f16[2,13,32,128]{3,2,1,0:T(8,128)(2,1)S(1)}, f16[2,13,32,128]{3,2,1,0:T(8,128)(2,1)S(1)}, u32[]{:S(2)}, u32[]{:S(2)}) collective-permute-start(f16[2,13,32,128]{3,2,1,0:T(8,128)(2,1)S(1)} %multiply_convert_fusion.2), channel_id=1, source_target_pairs={{0,24},{8,16},{16,8},{24,0},{1,25},{9,17},{17,9},{25,1},{2,26},{10... | collective-permute-start | bytes 638984 | tf_op jit(solution)/shard_map/ppermute | solution.py:263
  8.6 10.7 %collective-permute-start.7 = (f16[2,13,32,128]{3,2,1,0:T(8,128)(2,1)S(1)}, f16[2,13,32,128]{3,2,1,0:T(8,128)(2,1)S(1)}, u32[]{:S(2)}, u32[]{:S(2)}) collective-permute-start(f16[2,13,32,128]{3,2,1,0:T(8,128)(2,1)S(1)} %multiply_convert_fusion.1), channel_id=1, source_target_pairs={{0,16},{8,24},{16,0},{24,8},{1,17},{9,25},{17,1},{25,9},{2,18},{10... | collective-permute-start | bytes 638984 | tf_op jit(solution)/shard_map/ppermute | solution.py:263
  9.2 10.6 %collective-permute-start.8 = (f16[2,13,32,128]{3,2,1,0:T(8,128)(2,1)S(1)}, f16[2,13,32,128]{3,2,1,0:T(8,128)(2,1)S(1)}, u32[]{:S(2)}, u32[]{:S(2)}) collective-permute-start(f16[2,13,32,128]{3,2,1,0:T(8,128)(2,1)S(1)} %multiply_convert_fusion), channel_id=1, source_target_pairs={{0,8},{8,0},{16,24},{24,16},{1,9},{9,1},{17,25},{25,17},{2,10},{10... | collective-permute-start | bytes 638984 | tf_op jit(solution)/shard_map/ppermute | solution.py:263
  13.8 10.1 %collective-permute-start = (f16[2,13,32,128]{3,2,1,0:T(8,128)(2,1)S(1)}, f16[2,13,32,128]{3,2,1,0:T(8,128)(2,1)S(1)}, u32[]{:S(2)}, u32[]{:S(2)}) collective-permute-start(f16[2,13,32,128]{3,2,1,0:T(8,128)(2,1)S(1)} %multiply_convert_fusion.5), channel_id=1, source_target_pairs={{0,24},{8,16},{16,8},{24,0},{1,25},{9,17},{17,9},{25,1},{2,26},{10... | collective-permute-start | bytes 638984 | tf_op jit(solution)/shard_map/ppermute | solution.py:263
  16.9 10.6 %collective-permute-start.1 = (f16[2,13,32,128]{3,2,1,0:T(8,128)(2,1)S(1)}, f16[2,13,32,128]{3,2,1,0:T(8,128)(2,1)S(1)}, u32[]{:S(2)}, u32[]{:S(2)}) collective-permute-start(f16[2,13,32,128]{3,2,1,0:T(8,128)(2,1)S(1)} %multiply_convert_fusion.4), channel_id=1, source_target_pairs={{0,16},{8,24},{16,0},{24,8},{1,17},{9,25},{17,1},{25,9},{2,18},{10... | collective-permute-start | bytes 638984 | tf_op jit(solution)/shard_map/ppermute | solution.py:263
  18.5 9.3 %collective-permute-start.2 = (f16[2,13,32,128]{3,2,1,0:T(8,128)(2,1)}, f16[2,13,32,128]{3,2,1,0:T(8,128)(2,1)S(1)}, u32[]{:S(2)}, u32[]{:S(2)}) collective-permute-start(f16[2,13,32,128]{3,2,1,0:T(8,128)(2,1)} %multiply_convert_fusion.3), channel_id=1, source_target_pairs={{0,8},{8,0},{16,24},{24,16},{1,9},{9,1},{17,25},{25,17},{2,10},{10... | collective-permute-start | bytes 638984 | tf_op jit(solution)/shard_map/ppermute | solution.py:263
  19.9 11.8 %collective-permute-start.9 = (bf16[2,7,32,128]{3,2,1,0:T(8,128)(2,1)S(1)}, bf16[2,7,32,128]{3,2,1,0:T(8,128)(2,1)S(1)}, u32[]{:S(2)}, u32[]{:S(2)}) collective-permute-start(bf16[2,7,32,128]{3,2,1,0:T(8,128)(2,1)S(1)} %get-tuple-element.30), channel_id=1, source_target_pairs={{0,4},{1,5},{2,6},{3,7},{4,0},{5,1},{6,2},{7,3},{8,12},{9,13},{10,... | collective-permute-start | bytes 344072 | tf_op jit(solution)/shard_map/ppermute | solution.py:263
  22.6 9.2 %collective-permute-start.11 = (bf16[2,7,32,128]{3,2,1,0:T(8,128)(2,1)S(1)}, bf16[2,7,32,128]{3,2,1,0:T(8,128)(2,1)S(1)}, u32[]{:S(2)}, u32[]{:S(2)}) collective-permute-start(bf16[2,7,32,128]{3,2,1,0:T(8,128)(2,1)S(1)} %get-tuple-element.29), channel_id=1, source_target_pairs={{0,6},{1,7},{2,4},{3,5},{4,2},{5,3},{6,0},{7,1},{8,14},{9,15},{10,... | collective-permute-start | bytes 344072 | tf_op jit(solution)/shard_map/ppermute | solution.py:263
  28.0 5.5 %collective-permute-start.4 = (bf16[2,7,32,128]{3,2,1,0:T(8,128)(2,1)S(1)}, bf16[2,7,32,128]{3,2,1,0:T(8,128)(2,1)S(1)}, u32[]{:S(2)}, u32[]{:S(2)}) collective-permute-start(bf16[2,7,32,128]{3,2,1,0:T(8,128)(2,1)S(1)} %get-tuple-element.31), channel_id=1, source_target_pairs={{0,2},{1,3},{2,0},{3,1},{4,6},{5,7},{6,4},{7,5},{8,10},{9,11},{10,... | collective-permute-start | bytes 344072 | tf_op jit(solution)/shard_map/ppermute | solution.py:263
  29.7 3.8 %collective-permute-start.3 = (bf16[2,7,32,128]{3,2,1,0:T(8,128)(2,1)S(1)}, bf16[2,7,32,128]{3,2,1,0:T(8,128)(2,1)S(1)}, u32[]{:S(2)}, u32[]{:S(2)}) collective-permute-start(bf16[2,7,32,128]{3,2,1,0:T(8,128)(2,1)S(1)} %get-tuple-element.32.refs_0_), channel_id=1, source_target_pairs={{0,1},{1,0},{2,3},{3,2},{4,5},{5,4},{6,7},{7,6},{8,9},{9,8},{10,11... | collective-permute-start | bytes 344072 | tf_op jit(solution)/shard_map/ppermute | solution.py:263
  31.8 1.7 %collective-permute-start.10 = (bf16[2,7,32,128]{3,2,1,0:T(8,128)(2,1)S(1)}, bf16[2,7,32,128]{3,2,1,0:T(8,128)(2,1)S(1)}, u32[]{:S(2)}, u32[]{:S(2)}) collective-permute-start(bf16[2,7,32,128]{3,2,1,0:T(8,128)(2,1)S(1)} %collective-permute-done.9.refs_4_), channel_id=1, source_target_pairs={{0,1},{1,0},{2,3},{3,2},{4,5},{5,4},{6,7},{7,6},{8,9},{9,8},{10,11... | collective-permute-start | bytes 344072 | tf_op jit(solution)/shard_map/ppermute | solution.py:263
  31.8 1.7 %collective-permute-start.12 = (bf16[2,7,32,128]{3,2,1,0:T(8,128)(2,1)S(1)}, bf16[2,7,32,128]{3,2,1,0:T(8,128)(2,1)S(1)}, u32[]{:S(2)}, u32[]{:S(2)}) collective-permute-start(bf16[2,7,32,128]{3,2,1,0:T(8,128)(2,1)S(1)} %collective-permute-done.11.refs_6_), channel_id=1, source_target_pairs={{0,1},{1,0},{2,3},{3,2},{4,5},{5,4},{6,7},{7,6},{8,9},{9,8},{10,11... | collective-permute-start | bytes 344072 | tf_op jit(solution)/shard_map/ppermute | solution.py:263
  33.5 1.3 %collective-permute-start.5 = (bf16[2,7,32,128]{3,2,1,0:T(8,128)(2,1)S(1)}, bf16[2,7,32,128]{3,2,1,0:T(8,128)(2,1)S(1)}, u32[]{:S(2)}, u32[]{:S(2)}) collective-permute-start(bf16[2,7,32,128]{3,2,1,0:T(8,128)(2,1)S(1)} %collective-permute-done.4.refs_2_), channel_id=1, source_target_pairs={{0,1},{1,0},{2,3},{3,2},{4,5},{5,4},{6,7},{7,6},{8,9},{9,8},{10,11... | collective-permute-start | bytes 344072 | tf_op jit(solution)/shard_map/ppermute | solution.py:263
  37.6 4.5 %collective-permute-start.14 = (bf16[4,2,16,128]{3,2,1,0:T(8,128)(2,1)S(1)}, bf16[4,2,16,128]{3,2,1,0:T(8,128)(2,1)S(1)}, u32[]{:S(2)}, u32[]{:S(2)}) collective-permute-start(bf16[4,2,16,128]{3,2,1,0:T(8,128)(2,1)S(1)} %get-tuple-element.26), channel_id=1, source_target_pairs={{0,2},{1,3},{2,0},{3,1},{4,6},{5,7},{6,4},{7,5},{8,10},{9,11},{10,... | collective-permute-start | bytes 98312 | tf_op jit(solution)/shard_map/ppermute | solution.py:263
  38.6 4.9 %collective-permute-start.16 = (bf16[4,2,16,128]{3,2,1,0:T(8,128)(2,1)S(1)}, bf16[4,2,16,128]{3,2,1,0:T(8,128)(2,1)S(1)}, u32[]{:S(2)}, u32[]{:S(2)}) collective-permute-start(bf16[4,2,16,128]{3,2,1,0:T(8,128)(2,1)S(1)} %get-tuple-element.27), channel_id=1, source_target_pairs={{0,4},{1,5},{2,6},{3,7},{4,0},{5,1},{6,2},{7,3},{8,12},{9,13},{10,... | collective-permute-start | bytes 98312 | tf_op jit(solution)/shard_map/ppermute | solution.py:263
  41.4 5.7 %collective-permute-start.18 = (bf16[4,2,16,128]{3,2,1,0:T(8,128)(2,1)S(1)}, bf16[4,2,16,128]{3,2,1,0:T(8,128)(2,1)S(1)}, u32[]{:S(2)}, u32[]{:S(2)}) collective-permute-start(bf16[4,2,16,128]{3,2,1,0:T(8,128)(2,1)S(1)} %get-tuple-element.28), channel_id=1, source_target_pairs={{0,6},{1,7},{2,4},{3,5},{4,2},{5,3},{6,0},{7,1},{8,14},{9,15},{10,... | collective-permute-start | bytes 98312 | tf_op jit(solution)/shard_map/ppermute | solution.py:263
  42.1 5.0 %collective-permute-start.13 = (bf16[4,2,16,128]{3,2,1,0:T(8,128)(2,1)S(1)}, bf16[4,2,16,128]{3,2,1,0:T(8,128)(2,1)S(1)}, u32[]{:S(2)}, u32[]{:S(2)}) collective-permute-start(bf16[4,2,16,128]{3,2,1,0:T(8,128)(2,1)S(1)} %get-tuple-element.25.refs_0_), channel_id=1, source_target_pairs={{0,1},{1,0},{2,3},{3,2},{4,5},{5,4},{6,7},{7,6},{8,9},{9,8},{10,11... | collective-permute-start | bytes 98312 | tf_op jit(solution)/shard_map/ppermute | solution.py:263
  42.1 5.0 %collective-permute-start.15 = (bf16[4,2,16,128]{3,2,1,0:T(8,128)(2,1)S(1)}, bf16[4,2,16,128]{3,2,1,0:T(8,128)(2,1)S(1)}, u32[]{:S(2)}, u32[]{:S(2)}) collective-permute-start(bf16[4,2,16,128]{3,2,1,0:T(8,128)(2,1)S(1)} %collective-permute-done.14.refs_2_), channel_id=1, source_target_pairs={{0,1},{1,0},{2,3},{3,2},{4,5},{5,4},{6,7},{7,6},{8,9},{9,8},{10,11... | collective-permute-start | bytes 98312 | tf_op jit(solution)/shard_map/ppermute | solution.py:263
  43.5 3.6 %collective-permute-start.17 = (bf16[4,2,16,128]{3,2,1,0:T(8,128)(2,1)S(1)}, bf16[4,2,16,128]{3,2,1,0:T(8,128)(2,1)S(1)}, u32[]{:S(2)}, u32[]{:S(2)}) collective-permute-start(bf16[4,2,16,128]{3,2,1,0:T(8,128)(2,1)S(1)} %collective-permute-done.16.refs_4_), channel_id=1, source_target_pairs={{0,1},{1,0},{2,3},{3,2},{4,5},{5,4},{6,7},{7,6},{8,9},{9,8},{10,11... | collective-permute-start | bytes 98312 | tf_op jit(solution)/shard_map/ppermute | solution.py:263
  47.1 1.2 %collective-permute-start.19 = (bf16[4,2,16,128]{3,2,1,0:T(8,128)(2,1)S(1)}, bf16[4,2,16,128]{3,2,1,0:T(8,128)(2,1)S(1)}, u32[]{:S(2)}, u32[]{:S(2)}) collective-permute-start(bf16[4,2,16,128]{3,2,1,0:T(8,128)(2,1)S(1)} %collective-permute-done.18.refs_6_), channel_id=1, source_target_pairs={{0,1},{1,0},{2,3},{3,2},{4,5},{5,4},{6,7},{7,6},{8,9},{9,8},{10,11... | collective-permute-start | bytes 98312 | tf_op jit(solution)/shard_map/ppermute | solution.py:263

commit v7 on v6

--- a/solution.py
+++ b/solution.py
@@ -227,7 +227,7 @@
     slots = pieces_in[0].shape[0]
     chip = chip_ref[0]
     core = core_ref[0]
-    for index, ref in enumerate(pieces_in):
+    for index, ref in enumerate(reversed(pieces_in)):
         first = (chip ^ (index // 2)) * (beams - width) // (chips - 1)
         first += (core ^ (index % 2)) * (width - slots)
         out_ref[pl.ds(first, slots)] = ref[:, core].astype(F32)
@@ -243,7 +243,7 @@
         out_shape=jax.ShapeDtypeStruct((beams, gates, LANES), F32),
         compiler_params=pltpu.CompilerParams(vmem_limit_bytes=VMEM),
         name="gather_beams",
-    )(*place, *pieces)
+    )(*place, *reversed(pieces))
 
 
 def sign_rows(code_signs, periods, row_groups):

time: 49.1 us -> 47.8 us (0.974)
  waiting for transfers between devices: 15 us -> 13.7 us
    ppermute x20, waiting for transfers between devices: 15 us -> 13.7 us  [exchanged(): lax.ppermute(block, axis, [(i, i ^ step) for i in range(lax.axis_size(axi...]
  transfers between devices with their start and end apart: 20 -> 20, of which waited for: 10 -> 11; matrix products, arithmetic and copies ran while one was open for 3% -> 3% of each run, Pallas kernels for 9% -> 9%
where the time goes in v7:
time: 47.8 us; the launch traced here: 47.7 us
  starting transfers between devices  19.7 us (41%)
  waiting for transfers between devices  13.7 us (29%)
  Pallas kernels  12.4 us (26%)
  other arithmetic  1.29 us (3%)
    ppermute x20, starting transfers between devices, exchanged(): lax.ppermute(block, axis, [(i, i ^ step) for i in range(lax.axis_size(axi...  19.7 us
    ppermute x20, waiting for transfers between devices, exchanged(): lax.ppermute(block, axis, [(i, i ^ step) for i in range(lax.axis_size(axi...  13.7 us
    pallas_call x2, Pallas kernels, partial_beams(): pl.pallas_call(beam_kernel, in_specs=[pl.BlockSpec(memory_space=pltpu.SME...  8.92 us
    pallas_call x1, Pallas kernels, lag_profiles(): pl.pallas_call(functools.partial(lag_kernel, scale, len(pieces)), in_spec...  2.81 us
    convert_element_type x6, other arithmetic, body(): came = exchanged((partial[step] * gain).astype(jnp.float16), 'sub', step)  0.97 us
  transfers between devices with their start and end apart: 20, of which 11 were waited for; matrix products, arithmetic and copies ran while one was open for 3% of the time, Pallas kernels for 9%

profile of v7, /device:TPU:0, one launch (start us, length us, event | category | flops | bytes accessed | tf_op | source)
XLA Modules:
  0.0 47.7 jit_solution(3439216337487421083)
XLA Ops:
  0.0 4.5 %partial_beams.3 = (f32[2,13,32,128]{3,2,1,0:T(8,128)S(1)}, f32[2,13,32,128]{3,2,1,0:T(8,128)S(1)}, f32[2,13,32,128]{3,2,1,0:T(8,128)S(1)}, f32[2,13,32,128]{3,2,1,0:T(8,128)S(1)}) custom-call(s32[1]{0:T(128)} %bitcast.7.here_ref, s32[1]{0:T(128)} %bitcast.11.start_ref, bf16[100,2,540]{2,1,0:T(2,128)(2,1)} %bitcast.19, bf16[540,2,4096]{2,1,0:T(2,128)(2,1)} %bitcast.17), custom_call_target="tpu_custom_call" | custom-call | flops 920125440 | bytes 10551296 | tf_op jit(solution)/shard_map/partial_beams/pallas_call | solution.py:91
  4.5 4.0 %collective-permute-start.6 = (f16[2,13,32,128]{3,2,1,0:T(8,128)(2,1)S(1)}, f16[2,13,32,128]{3,2,1,0:T(8,128)(2,1)S(1)}, u32[]{:S(2)}, u32[]{:S(2)}) collective-permute-start(f16[2,13,32,128]{3,2,1,0:T(8,128)(2,1)S(1)} %multiply_convert_fusion.2), channel_id=1, source_target_pairs={{0,24},{8,16},{16,8},{24,0},{1,25},{9,17},{17,9},{25,1},{2,26},{10... | collective-permute-start | bytes 638984 | tf_op jit(solution)/shard_map/ppermute | solution.py:263
  8.6 0.6 %collective-permute-start.7 = (f16[2,13,32,128]{3,2,1,0:T(8,128)(2,1)S(1)}, f16[2,13,32,128]{3,2,1,0:T(8,128)(2,1)S(1)}, u32[]{:S(2)}, u32[]{:S(2)}) collective-permute-start(f16[2,13,32,128]{3,2,1,0:T(8,128)(2,1)S(1)} %multiply_convert_fusion.1), channel_id=1, source_target_pairs={{0,16},{8,24},{16,0},{24,8},{1,17},{9,25},{17,1},{25,9},{2,18},{10... | collective-permute-start | bytes 638984 | tf_op jit(solution)/shard_map/ppermute | solution.py:263
  9.2 0.1 collective-permute-start.8
  9.3 4.5 %partial_beams.2 = (f32[2,13,32,128]{3,2,1,0:T(8,128)S(1)}, f32[2,13,32,128]{3,2,1,0:T(8,128)S(1)}, f32[2,13,32,128]{3,2,1,0:T(8,128)S(1)}, f32[2,13,32,128]{3,2,1,0:T(8,128)S(1)}) custom-call(s32[1]{0:T(128)} %bitcast.7.here_ref, s32[1]{0:T(128)} %bitcast.8.start_ref, bf16[100,2,540]{2,1,0:T(2,128)(2,1)} %bitcast.20, bf16[540,2,4096]{2,1,0:T(2,128)(2,1)} %bitcast.18), custom_call_target="tpu_custom_call" | custom-call | flops 920125440 | bytes 10551296 | tf_op jit(solution)/shard_map/partial_beams/pallas_call | solution.py:91
  13.8 3.0 %collective-permute-start = (f16[2,13,32,128]{3,2,1,0:T(8,128)(2,1)S(1)}, f16[2,13,32,128]{3,2,1,0:T(8,128)(2,1)S(1)}, u32[]{:S(2)}, u32[]{:S(2)}) collective-permute-start(f16[2,13,32,128]{3,2,1,0:T(8,128)(2,1)S(1)} %multiply_convert_fusion.5), channel_id=1, source_target_pairs={{0,24},{8,16},{16,8},{24,0},{1,25},{9,17},{17,9},{25,1},{2,26},{10... | collective-permute-start | bytes 638984 | tf_op jit(solution)/shard_map/ppermute | solution.py:263
  16.9 0.6 %collective-permute-start.1 = (f16[2,13,32,128]{3,2,1,0:T(8,128)(2,1)S(1)}, f16[2,13,32,128]{3,2,1,0:T(8,128)(2,1)S(1)}, u32[]{:S(2)}, u32[]{:S(2)}) collective-permute-start(f16[2,13,32,128]{3,2,1,0:T(8,128)(2,1)S(1)} %multiply_convert_fusion.4), channel_id=1, source_target_pairs={{0,16},{8,24},{16,0},{24,8},{1,17},{9,25},{17,1},{25,9},{2,18},{10... | collective-permute-start | bytes 638984 | tf_op jit(solution)/shard_map/ppermute | solution.py:263
  17.4 0.7 %multiply_convert_fusion.3 = f16[2,13,32,128]{3,2,1,0:T(8,128)(2,1)} fusion(f32[2,13,32,128]{3,2,1,0:T(8,128)S(1)} %get-tuple-element.20), kind=kLoop, calls=%fused_computation.5 | loop fusion | flops 212992 | bytes 638976 | tf_op jit(solution)/shard_map/convert_element_type | solution.py:306
  18.3 0.1 copy.10
  18.5 0.2 collective-permute-start.2
  18.7 0.5 %collective-permute-done.7 = f16[2,13,32,128]{3,2,1,0:T(8,128)(2,1)S(1)} collective-permute-done((f16[2,13,32,128]{3,2,1,0:T(8,128)(2,1)S(1)}, f16[2,13,32,128]{3,2,1,0:T(8,128)(2,1)S(1)}, u32[]{:S(2)}, u32[]{:S(2)}) %collective-permute-start.7) | collective-permute-done | bytes 213024 | tf_op jit(solution)/shard_map/ppermute | solution.py:263
  19.3 0.5 %collective-permute-done.8 = f16[2,13,32,128]{3,2,1,0:T(8,128)(2,1)S(1)} collective-permute-done((f16[2,13,32,128]{3,2,1,0:T(8,128)(2,1)S(1)}, f16[2,13,32,128]{3,2,1,0:T(8,128)(2,1)S(1)}, u32[]{:S(2)}, u32[]{:S(2)}) %collective-permute-start.8) | collective-permute-done | bytes 213024 | tf_op jit(solution)/shard_map/ppermute | solution.py:263
  19.8 0.1 add_convert_fusion
  19.9 2.7 %collective-permute-start.9 = (bf16[2,7,32,128]{3,2,1,0:T(8,128)(2,1)S(1)}, bf16[2,7,32,128]{3,2,1,0:T(8,128)(2,1)S(1)}, u32[]{:S(2)}, u32[]{:S(2)}) collective-permute-start(bf16[2,7,32,128]{3,2,1,0:T(8,128)(2,1)S(1)} %get-tuple-element.30), channel_id=1, source_target_pairs={{0,4},{1,5},{2,6},{3,7},{4,0},{5,1},{6,2},{7,3},{8,12},{9,13},{10,... | collective-permute-start | bytes 344072 | tf_op jit(solution)/shard_map/ppermute | solution.py:263
  22.6 1.3 %collective-permute-start.11 = (bf16[2,7,32,128]{3,2,1,0:T(8,128)(2,1)S(1)}, bf16[2,7,32,128]{3,2,1,0:T(8,128)(2,1)S(1)}, u32[]{:S(2)}, u32[]{:S(2)}) collective-permute-start(bf16[2,7,32,128]{3,2,1,0:T(8,128)(2,1)S(1)} %get-tuple-element.29), channel_id=1, source_target_pairs={{0,6},{1,7},{2,4},{3,5},{4,2},{5,3},{6,0},{7,1},{8,14},{9,15},{10,... | collective-permute-start | bytes 344072 | tf_op jit(solution)/shard_map/ppermute | solution.py:263
  24.0 3.5 %collective-permute-done.1 = f16[2,13,32,128]{3,2,1,0:T(8,128)(2,1)S(1)} collective-permute-done((f16[2,13,32,128]{3,2,1,0:T(8,128)(2,1)S(1)}, f16[2,13,32,128]{3,2,1,0:T(8,128)(2,1)S(1)}, u32[]{:S(2)}, u32[]{:S(2)}) %collective-permute-start.1) | collective-permute-done | bytes 213024 | tf_op jit(solution)/shard_map/ppermute | solution.py:263
  27.5 0.3 collective-permute-done.2
  27.8 0.1 add_convert_fusion.1
  28.0 1.7 %collective-permute-start.4 = (bf16[2,7,32,128]{3,2,1,0:T(8,128)(2,1)S(1)}, bf16[2,7,32,128]{3,2,1,0:T(8,128)(2,1)S(1)}, u32[]{:S(2)}, u32[]{:S(2)}) collective-permute-start(bf16[2,7,32,128]{3,2,1,0:T(8,128)(2,1)S(1)} %get-tuple-element.31), channel_id=1, source_target_pairs={{0,2},{1,3},{2,0},{3,1},{4,6},{5,7},{6,4},{7,5},{8,10},{9,11},{10,... | collective-permute-start | bytes 344072 | tf_op jit(solution)/shard_map/ppermute | solution.py:263
  29.8 2.0 %collective-permute-done.9.refs_4_ = bf16[2,7,32,128]{3,2,1,0:T(8,128)(2,1)S(1)} collective-permute-done((bf16[2,7,32,128]{3,2,1,0:T(8,128)(2,1)S(1)}, bf16[2,7,32,128]{3,2,1,0:T(8,128)(2,1)S(1)}, u32[]{:S(2)}, u32[]{:S(2)}) %collective-permute-start.9) | collective-permute-done | bytes 114720 | tf_op jit(solution)/shard_map/ppermute | solution.py:263
  31.8 0.5 %collective-permute-start.12 = (bf16[2,7,32,128]{3,2,1,0:T(8,128)(2,1)S(1)}, bf16[2,7,32,128]{3,2,1,0:T(8,128)(2,1)S(1)}, u32[]{:S(2)}, u32[]{:S(2)}) collective-permute-start(bf16[2,7,32,128]{3,2,1,0:T(8,128)(2,1)S(1)} %collective-permute-done.11.refs_6_), channel_id=1, source_target_pairs={{0,1},{1,0},{2,3},{3,2},{4,5},{5,4},{6,7},{7,6},{8,9},{9,8},{10,11... | collective-permute-start | bytes 344072 | tf_op jit(solution)/shard_map/ppermute | solution.py:263
  32.3 1.2 %collective-permute-done.4.refs_2_ = bf16[2,7,32,128]{3,2,1,0:T(8,128)(2,1)S(1)} collective-permute-done((bf16[2,7,32,128]{3,2,1,0:T(8,128)(2,1)S(1)}, bf16[2,7,32,128]{3,2,1,0:T(8,128)(2,1)S(1)}, u32[]{:S(2)}, u32[]{:S(2)}) %collective-permute-start.4) | collective-permute-done | bytes 114720 | tf_op jit(solution)/shard_map/ppermute | solution.py:263
  33.5 1.3 %collective-permute-done.5.refs_3_ = bf16[2,7,32,128]{3,2,1,0:T(8,128)(2,1)S(1)} collective-permute-done((bf16[2,7,32,128]{3,2,1,0:T(8,128)(2,1)S(1)}, bf16[2,7,32,128]{3,2,1,0:T(8,128)(2,1)S(1)}, u32[]{:S(2)}, u32[]{:S(2)}) %collective-permute-start.5) | collective-permute-done | bytes 114720 | tf_op jit(solution)/shard_map/ppermute | solution.py:263
  34.8 2.8 %lag_profiles.1 = (bf16[4,2,16,128]{3,2,1,0:T(8,128)(2,1)S(1)}, bf16[4,2,16,128]{3,2,1,0:T(8,128)(2,1)S(1)}, bf16[4,2,16,128]{3,2,1,0:T(8,128)(2,1)S(1)}, bf16[4,2,16,128]{3,2,1,0:T(8,128)(2,1)S(1)}) custom-call(s32[1]{0:T(128)} %bitcast.chip_ref, s32[1]{0:T(128)} %bitcast.1.core_ref, f32[2,32,128]{2,1,0:T(8,128)S(1)} %bitcast.16, ...), custom_call_target="tpu_custom_call" | custom-call | tf_op jit(solution)/shard_map/lag_profiles/pallas_call | solution.py:206
  37.6 3.2 %collective-permute-start.13 = (bf16[4,2,16,128]{3,2,1,0:T(8,128)(2,1)S(1)}, bf16[4,2,16,128]{3,2,1,0:T(8,128)(2,1)S(1)}, u32[]{:S(2)}, u32[]{:S(2)}) collective-permute-start(bf16[4,2,16,128]{3,2,1,0:T(8,128)(2,1)S(1)} %get-tuple-element.25), channel_id=1, source_target_pairs={{0,6},{1,7},{2,4},{3,5},{4,2},{5,3},{6,0},{7,1},{8,14},{9,15},{10,... | collective-permute-start | bytes 98312 | tf_op jit(solution)/shard_map/ppermute | solution.py:263
  40.8 1.3 %collective-permute-start.17 = (bf16[4,2,16,128]{3,2,1,0:T(8,128)(2,1)S(1)}, bf16[4,2,16,128]{3,2,1,0:T(8,128)(2,1)S(1)}, u32[]{:S(2)}, u32[]{:S(2)}) collective-permute-start(bf16[4,2,16,128]{3,2,1,0:T(8,128)(2,1)S(1)} %get-tuple-element.27), channel_id=1, source_target_pairs={{0,2},{1,3},{2,0},{3,1},{4,6},{5,7},{6,4},{7,5},{8,10},{9,11},{10,... | collective-permute-start | bytes 98312 | tf_op jit(solution)/shard_map/ppermute | solution.py:263
  42.1 1.3 %collective-permute-done.13.refs_1_ = bf16[4,2,16,128]{3,2,1,0:T(8,128)(2,1)S(1)} collective-permute-done((bf16[4,2,16,128]{3,2,1,0:T(8,128)(2,1)S(1)}, bf16[4,2,16,128]{3,2,1,0:T(8,128)(2,1)S(1)}, u32[]{:S(2)}, u32[]{:S(2)}) %collective-permute-start.13) | collective-permute-done | bytes 32800 | tf_op jit(solution)/shard_map/ppermute | solution.py:263
  43.4 2.2 %collective-permute-done.15.refs_3_ = bf16[4,2,16,128]{3,2,1,0:T(8,128)(2,1)S(1)} collective-permute-done((bf16[4,2,16,128]{3,2,1,0:T(8,128)(2,1)S(1)}, bf16[4,2,16,128]{3,2,1,0:T(8,128)(2,1)S(1)}, u32[]{:S(2)}, u32[]{:S(2)}) %collective-permute-start.15) | collective-permute-done | bytes 32800 | tf_op jit(solution)/shard_map/ppermute | solution.py:263
  45.6 0.5 %collective-permute-start.18 = (bf16[4,2,16,128]{3,2,1,0:T(8,128)(2,1)S(1)}, bf16[4,2,16,128]{3,2,1,0:T(8,128)(2,1)S(1)}, u32[]{:S(2)}, u32[]{:S(2)}) collective-permute-start(bf16[4,2,16,128]{3,2,1,0:T(8,128)(2,1)S(1)} %collective-permute-done.17.refs_5_), channel_id=1, source_target_pairs={{0,1},{1,0},{2,3},{3,2},{4,5},{5,4},{6,7},{7,6},{8,9},{9,8},{10,11... | collective-permute-start | bytes 98312 | tf_op jit(solution)/shard_map/ppermute | solution.py:263
  46.1 0.7 %collective-permute-done.16.refs_2_ = bf16[4,2,16,128]{3,2,1,0:T(8,128)(2,1)S(1)} collective-permute-done((bf16[4,2,16,128]{3,2,1,0:T(8,128)(2,1)S(1)}, bf16[4,2,16,128]{3,2,1,0:T(8,128)(2,1)S(1)}, u32[]{:S(2)}, u32[]{:S(2)}) %collective-permute-start.16) | collective-permute-done | bytes 32800 | tf_op jit(solution)/shard_map/ppermute | solution.py:263
  46.8 0.2 collective-permute-done.18.refs_4_
  47.0 0.7 %gather_beams.1 = f32[25,16,128]{2,1,0:T(8,128)} custom-call(s32[1]{0:T(128)} %bitcast.chip_ref, s32[1]{0:T(128)} %bitcast.1.core_ref, bf16[4,2,16,128]{3,2,1,0:T(8,128)(2,1)S(1)} %collective-permute-done.14.refs_0_, bf16[4,2,16,128]{3,2,1,0:T(8,128)(2,1)S(1)} %collective-permute-done.13.refs_1_, ...), custom_call_target="tpu_custom_call" | custom-call | tf_op jit(solution)/shard_map/gather_beams/pallas_call | solution.py:239
  (37 shorter events, 0.7 us)
Async XLA Ops:
  0.0 18.2 %copy-start.1 = (s32[256]{0:T(256)S(1)}, s32[256]{0:T(256)}, u32[]{:S(2)}) copy-start(s32[256]{0:T(256)} %param.7) | copy-start | bytes 3076
  4.5 14.0 %copy-start = (s32[32,16]{0,1:T(8,128)S(1)}, s32[32,16]{0,1:T(8,128)}, u32[]{:S(2)}) copy-start(s32[32,16]{0,1:T(8,128)} %param.6) | copy-start | bytes 6148
  4.5 13.9 %collective-permute-start.6 = (f16[2,13,32,128]{3,2,1,0:T(8,128)(2,1)S(1)}, f16[2,13,32,128]{3,2,1,0:T(8,128)(2,1)S(1)}, u32[]{:S(2)}, u32[]{:S(2)}) collective-permute-start(f16[2,13,32,128]{3,2,1,0:T(8,128)(2,1)S(1)} %multiply_convert_fusion.2), channel_id=1, source_target_pairs={{0,24},{8,16},{16,8},{24,0},{1,25},{9,17},{17,9},{25,1},{2,26},{10... | collective-permute-start | bytes 638984 | tf_op jit(solution)/shard_map/ppermute | solution.py:263
  8.6 10.7 %collective-permute-start.7 = (f16[2,13,32,128]{3,2,1,0:T(8,128)(2,1)S(1)}, f16[2,13,32,128]{3,2,1,0:T(8,128)(2,1)S(1)}, u32[]{:S(2)}, u32[]{:S(2)}) collective-permute-start(f16[2,13,32,128]{3,2,1,0:T(8,128)(2,1)S(1)} %multiply_convert_fusion.1), channel_id=1, source_target_pairs={{0,16},{8,24},{16,0},{24,8},{1,17},{9,25},{17,1},{25,9},{2,18},{10... | collective-permute-start | bytes 638984 | tf_op jit(solution)/shard_map/ppermute | solution.py:263
  9.2 10.6 %collective-permute-start.8 = (f16[2,13,32,128]{3,2,1,0:T(8,128)(2,1)S(1)}, f16[2,13,32,128]{3,2,1,0:T(8,128)(2,1)S(1)}, u32[]{:S(2)}, u32[]{:S(2)}) collective-permute-start(f16[2,13,32,128]{3,2,1,0:T(8,128)(2,1)S(1)} %multiply_convert_fusion), channel_id=1, source_target_pairs={{0,8},{8,0},{16,24},{24,16},{1,9},{9,1},{17,25},{25,17},{2,10},{10... | collective-permute-start | bytes 638984 | tf_op jit(solution)/shard_map/ppermute | solution.py:263
  13.8 10.1 %collective-permute-start = (f16[2,13,32,128]{3,2,1,0:T(8,128)(2,1)S(1)}, f16[2,13,32,128]{3,2,1,0:T(8,128)(2,1)S(1)}, u32[]{:S(2)}, u32[]{:S(2)}) collective-permute-start(f16[2,13,32,128]{3,2,1,0:T(8,128)(2,1)S(1)} %multiply_convert_fusion.5), channel_id=1, source_target_pairs={{0,24},{8,16},{16,8},{24,0},{1,25},{9,17},{17,9},{25,1},{2,26},{10... | collective-permute-start | bytes 638984 | tf_op jit(solution)/shard_map/ppermute | solution.py:263
  16.9 10.6 %collective-permute-start.1 = (f16[2,13,32,128]{3,2,1,0:T(8,128)(2,1)S(1)}, f16[2,13,32,128]{3,2,1,0:T(8,128)(2,1)S(1)}, u32[]{:S(2)}, u32[]{:S(2)}) collective-permute-start(f16[2,13,32,128]{3,2,1,0:T(8,128)(2,1)S(1)} %multiply_convert_fusion.4), channel_id=1, source_target_pairs={{0,16},{8,24},{16,0},{24,8},{1,17},{9,25},{17,1},{25,9},{2,18},{10... | collective-permute-start | bytes 638984 | tf_op jit(solution)/shard_map/ppermute | solution.py:263
  18.5 9.3 %collective-permute-start.2 = (f16[2,13,32,128]{3,2,1,0:T(8,128)(2,1)}, f16[2,13,32,128]{3,2,1,0:T(8,128)(2,1)S(1)}, u32[]{:S(2)}, u32[]{:S(2)}) collective-permute-start(f16[2,13,32,128]{3,2,1,0:T(8,128)(2,1)} %multiply_convert_fusion.3), channel_id=1, source_target_pairs={{0,8},{8,0},{16,24},{24,16},{1,9},{9,1},{17,25},{25,17},{2,10},{10... | collective-permute-start | bytes 638984 | tf_op jit(solution)/shard_map/ppermute | solution.py:263
  19.9 11.8 %collective-permute-start.9 = (bf16[2,7,32,128]{3,2,1,0:T(8,128)(2,1)S(1)}, bf16[2,7,32,128]{3,2,1,0:T(8,128)(2,1)S(1)}, u32[]{:S(2)}, u32[]{:S(2)}) collective-permute-start(bf16[2,7,32,128]{3,2,1,0:T(8,128)(2,1)S(1)} %get-tuple-element.30), channel_id=1, source_target_pairs={{0,4},{1,5},{2,6},{3,7},{4,0},{5,1},{6,2},{7,3},{8,12},{9,13},{10,... | collective-permute-start | bytes 344072 | tf_op jit(solution)/shard_map/ppermute | solution.py:263
  22.6 9.2 %collective-permute-start.11 = (bf16[2,7,32,128]{3,2,1,0:T(8,128)(2,1)S(1)}, bf16[2,7,32,128]{3,2,1,0:T(8,128)(2,1)S(1)}, u32[]{:S(2)}, u32[]{:S(2)}) collective-permute-start(bf16[2,7,32,128]{3,2,1,0:T(8,128)(2,1)S(1)} %get-tuple-element.29), channel_id=1, source_target_pairs={{0,6},{1,7},{2,4},{3,5},{4,2},{5,3},{6,0},{7,1},{8,14},{9,15},{10,... | collective-permute-start | bytes 344072 | tf_op jit(solution)/shard_map/ppermute | solution.py:263
  28.0 5.5 %collective-permute-start.4 = (bf16[2,7,32,128]{3,2,1,0:T(8,128)(2,1)S(1)}, bf16[2,7,32,128]{3,2,1,0:T(8,128)(2,1)S(1)}, u32[]{:S(2)}, u32[]{:S(2)}) collective-permute-start(bf16[2,7,32,128]{3,2,1,0:T(8,128)(2,1)S(1)} %get-tuple-element.31), channel_id=1, source_target_pairs={{0,2},{1,3},{2,0},{3,1},{4,6},{5,7},{6,4},{7,5},{8,10},{9,11},{10,... | collective-permute-start | bytes 344072 | tf_op jit(solution)/shard_map/ppermute | solution.py:263
  29.7 3.8 %collective-permute-start.3 = (bf16[2,7,32,128]{3,2,1,0:T(8,128)(2,1)S(1)}, bf16[2,7,32,128]{3,2,1,0:T(8,128)(2,1)S(1)}, u32[]{:S(2)}, u32[]{:S(2)}) collective-permute-start(bf16[2,7,32,128]{3,2,1,0:T(8,128)(2,1)S(1)} %get-tuple-element.32.refs_0_), channel_id=1, source_target_pairs={{0,1},{1,0},{2,3},{3,2},{4,5},{5,4},{6,7},{7,6},{8,9},{9,8},{10,11... | collective-permute-start | bytes 344072 | tf_op jit(solution)/shard_map/ppermute | solution.py:263
  31.8 1.7 %collective-permute-start.10 = (bf16[2,7,32,128]{3,2,1,0:T(8,128)(2,1)S(1)}, bf16[2,7,32,128]{3,2,1,0:T(8,128)(2,1)S(1)}, u32[]{:S(2)}, u32[]{:S(2)}) collective-permute-start(bf16[2,7,32,128]{3,2,1,0:T(8,128)(2,1)S(1)} %collective-permute-done.9.refs_4_), channel_id=1, source_target_pairs={{0,1},{1,0},{2,3},{3,2},{4,5},{5,4},{6,7},{7,6},{8,9},{9,8},{10,11... | collective-permute-start | bytes 344072 | tf_op jit(solution)/shard_map/ppermute | solution.py:263
  31.8 1.7 %collective-permute-start.12 = (bf16[2,7,32,128]{3,2,1,0:T(8,128)(2,1)S(1)}, bf16[2,7,32,128]{3,2,1,0:T(8,128)(2,1)S(1)}, u32[]{:S(2)}, u32[]{:S(2)}) collective-permute-start(bf16[2,7,32,128]{3,2,1,0:T(8,128)(2,1)S(1)} %collective-permute-done.11.refs_6_), channel_id=1, source_target_pairs={{0,1},{1,0},{2,3},{3,2},{4,5},{5,4},{6,7},{7,6},{8,9},{9,8},{10,11... | collective-permute-start | bytes 344072 | tf_op jit(solution)/shard_map/ppermute | solution.py:263
  33.5 1.3 %collective-permute-start.5 = (bf16[2,7,32,128]{3,2,1,0:T(8,128)(2,1)S(1)}, bf16[2,7,32,128]{3,2,1,0:T(8,128)(2,1)S(1)}, u32[]{:S(2)}, u32[]{:S(2)}) collective-permute-start(bf16[2,7,32,128]{3,2,1,0:T(8,128)(2,1)S(1)} %collective-permute-done.4.refs_2_), channel_id=1, source_target_pairs={{0,1},{1,0},{2,3},{3,2},{4,5},{5,4},{6,7},{7,6},{8,9},{9,8},{10,11... | collective-permute-start | bytes 344072 | tf_op jit(solution)/shard_map/ppermute | solution.py:263
  37.6 5.8 %collective-permute-start.13 = (bf16[4,2,16,128]{3,2,1,0:T(8,128)(2,1)S(1)}, bf16[4,2,16,128]{3,2,1,0:T(8,128)(2,1)S(1)}, u32[]{:S(2)}, u32[]{:S(2)}) collective-permute-start(bf16[4,2,16,128]{3,2,1,0:T(8,128)(2,1)S(1)} %get-tuple-element.25), channel_id=1, source_target_pairs={{0,6},{1,7},{2,4},{3,5},{4,2},{5,3},{6,0},{7,1},{8,14},{9,15},{10,... | collective-permute-start | bytes 98312 | tf_op jit(solution)/shard_map/ppermute | solution.py:263
  40.8 4.8 %collective-permute-start.15 = (bf16[4,2,16,128]{3,2,1,0:T(8,128)(2,1)S(1)}, bf16[4,2,16,128]{3,2,1,0:T(8,128)(2,1)S(1)}, u32[]{:S(2)}, u32[]{:S(2)}) collective-permute-start(bf16[4,2,16,128]{3,2,1,0:T(8,128)(2,1)S(1)} %get-tuple-element.26), channel_id=1, source_target_pairs={{0,4},{1,5},{2,6},{3,7},{4,0},{5,1},{6,2},{7,3},{8,12},{9,13},{10,... | collective-permute-start | bytes 98312 | tf_op jit(solution)/shard_map/ppermute | solution.py:263
  40.8 4.8 %collective-permute-start.17 = (bf16[4,2,16,128]{3,2,1,0:T(8,128)(2,1)S(1)}, bf16[4,2,16,128]{3,2,1,0:T(8,128)(2,1)S(1)}, u32[]{:S(2)}, u32[]{:S(2)}) collective-permute-start(bf16[4,2,16,128]{3,2,1,0:T(8,128)(2,1)S(1)} %get-tuple-element.27), channel_id=1, source_target_pairs={{0,2},{1,3},{2,0},{3,1},{4,6},{5,7},{6,4},{7,5},{8,10},{9,11},{10,... | collective-permute-start | bytes 98312 | tf_op jit(solution)/shard_map/ppermute | solution.py:263
  42.1 4.1 %collective-permute-start.19 = (bf16[4,2,16,128]{3,2,1,0:T(8,128)(2,1)S(1)}, bf16[4,2,16,128]{3,2,1,0:T(8,128)(2,1)S(1)}, u32[]{:S(2)}, u32[]{:S(2)}) collective-permute-start(bf16[4,2,16,128]{3,2,1,0:T(8,128)(2,1)S(1)} %get-tuple-element.28.refs_7_), channel_id=1, source_target_pairs={{0,1},{1,0},{2,3},{3,2},{4,5},{5,4},{6,7},{7,6},{8,9},{9,8},{10,11... | collective-permute-start | bytes 98312 | tf_op jit(solution)/shard_map/ppermute | solution.py:263
  43.4 2.7 %collective-permute-start.14 = (bf16[4,2,16,128]{3,2,1,0:T(8,128)(2,1)S(1)}, bf16[4,2,16,128]{3,2,1,0:T(8,128)(2,1)S(1)}, u32[]{:S(2)}, u32[]{:S(2)}) collective-permute-start(bf16[4,2,16,128]{3,2,1,0:T(8,128)(2,1)S(1)} %collective-permute-done.13.refs_1_), channel_id=1, source_target_pairs={{0,1},{1,0},{2,3},{3,2},{4,5},{5,4},{6,7},{7,6},{8,9},{9,8},{10,11... | collective-permute-start | bytes 98312 | tf_op jit(solution)/shard_map/ppermute | solution.py:263
  45.6 1.2 %collective-permute-start.16 = (bf16[4,2,16,128]{3,2,1,0:T(8,128)(2,1)S(1)}, bf16[4,2,16,128]{3,2,1,0:T(8,128)(2,1)S(1)}, u32[]{:S(2)}, u32[]{:S(2)}) collective-permute-start(bf16[4,2,16,128]{3,2,1,0:T(8,128)(2,1)S(1)} %collective-permute-done.15.refs_3_), channel_id=1, source_target_pairs={{0,1},{1,0},{2,3},{3,2},{4,5},{5,4},{6,7},{7,6},{8,9},{9,8},{10,11... | collective-permute-start | bytes 98312 | tf_op jit(solution)/shard_map/ppermute | solution.py:263
  45.6 1.4 %collective-permute-start.18 = (bf16[4,2,16,128]{3,2,1,0:T(8,128)(2,1)S(1)}, bf16[4,2,16,128]{3,2,1,0:T(8,128)(2,1)S(1)}, u32[]{:S(2)}, u32[]{:S(2)}) collective-permute-start(bf16[4,2,16,128]{3,2,1,0:T(8,128)(2,1)S(1)} %collective-permute-done.17.refs_5_), channel_id=1, source_target_pairs={{0,1},{1,0},{2,3},{3,2},{4,5},{5,4},{6,7},{7,6},{8,9},{9,8},{10,11... | collective-permute-start | bytes 98312 | tf_op jit(solution)/shard_map/ppermute | solution.py:263

commit v8 on v7

--- a/solution.py
+++ b/solution.py
@@ -122,7 +122,10 @@
     taken = pieces_in[0].shape[1] - slots
     for index, ref in enumerate(pieces_in):
         source = 2 * (chip ^ (index // 2)) + (core ^ (index % 2))
-        x_ref[source] = ref[:, pl.ds(core * taken, slots)]
+        if ref.shape[1] == slots:
+            x_ref[source] = ref[...]
+        else:
+            x_ref[source] = ref[:, pl.ds(core * taken, slots)]
     row_groups = sign_ref.shape[0]
     depth = row_groups * rows
     lane = lax.broadcasted_iota(jnp.int32, (rows, LANES), 1)
@@ -283,7 +286,8 @@
     scale = 1.0 / math.sqrt(periods * IPP_LEN / GATES)
     here = lax.axis_index("sub")
     chip = lax.axis_index("tm") // 2
-    place = (chip.reshape(1), (lax.axis_index("tm") % 2).reshape(1))
+    core = lax.axis_index("tm") % 2
+    place = (chip.reshape(1), core.reshape(1))
     signs = sign_rows(code_signs, periods, sources // PER_ROW)
     gate_hot = gate_rows(gate_map)
     weights = pltpu.with_memory_space_constraint(beam_weights.transpose(1, 0, 2), pltpu.HBM)
@@ -297,7 +301,7 @@
     half = chips // 2
     count = max((half - 1) * (beams - width) // (chips - 1) + width, beams - first_of(half))
     low = chip < half
-    blocks = [None] * chips
+    pieces = [None] * sources
     for far in (True, False):
         start = jnp.where(low == far, beams - count, 0).astype(jnp.int32)
         partial = partial_beams(by_channel, weights, here, start, groups, count)
@@ -308,8 +312,16 @@
         total = total.astype(BF16)
         for step in range(half, chips) if far else range(half):
             place_of = first_of(chip ^ step) - start
-            blocks[step] = lax.dynamic_slice_in_dim(total, place_of, width, 1)
-    terms = lag_profiles(place, signs, gate_hot, spread(blocks), sources, slots, scale)
+            if far or not step:
+                block = lax.dynamic_slice_in_dim(total, place_of, width, 1)
+                block = exchanged(block, "tm", 2 * step) if step else block
+                pieces[2 * step : 2 * step + 2] = [block, exchanged(block, "tm", 1)]
+            else:
+                for other in range(2):
+                    first = place_of + (core ^ other) * (width - slots)
+                    block = lax.dynamic_slice_in_dim(total, first, slots, 1)
+                    pieces[2 * step + other] = exchanged(block, "tm", 2 * step + other)
+    terms = lag_profiles(place, signs, gate_hot, pieces, sources, slots, scale)
     return gather_beams(place, spread(terms[::-1]), width, beams).transpose(1, 0, 2)
 
 

time: 47.8 us -> 46.5 us (0.973)
  waiting for transfers between devices: 13.7 us -> 11.8 us
    ppermute x20, waiting for transfers between devices: 13.7 us -> 11.8 us  [exchanged(): lax.ppermute(block, axis, [(i, i ^ step) for i in range(lax.axis_size(axi...]
    ppermute x20, starting transfers between devices: 19.7 us -> 20.1 us  [exchanged(): lax.ppermute(block, axis, [(i, i ^ step) for i in range(lax.axis_size(axi...]
  transfers between devices with their start and end apart: 20 -> 20, of which waited for: 11 -> 11; matrix products, arithmetic and copies ran while one was open for 3% -> 4% of each run, Pallas kernels for 9% -> 10%
where the time goes in v8:
time: 46.5 us; the launch traced here: 46.4 us
  starting transfers between devices  20.1 us (43%)
  Pallas kernels  12.4 us (27%)
  waiting for transfers between devices  11.8 us (25%)
  other arithmetic  1.31 us (3%)
    ppermute x20, starting transfers between devices, exchanged(): lax.ppermute(block, axis, [(i, i ^ step) for i in range(lax.axis_size(axi...  20.1 us
    ppermute x20, waiting for transfers between devices, exchanged(): lax.ppermute(block, axis, [(i, i ^ step) for i in range(lax.axis_size(axi...  11.8 us
    pallas_call x2, Pallas kernels, partial_beams(): pl.pallas_call(beam_kernel, in_specs=[pl.BlockSpec(memory_space=pltpu.SME...  8.92 us
    pallas_call x1, Pallas kernels, lag_profiles(): pl.pallas_call(functools.partial(lag_kernel, scale, len(pieces)), in_spec...  2.82 us
    convert_element_type x6, other arithmetic, body(): came = exchanged((partial[step] * gain).astype(jnp.float16), 'sub', step)  0.97 us
  transfers between devices with their start and end apart: 20, of which 11 were waited for; matrix products, arithmetic and copies ran while one was open for 4% of the time, Pallas kernels for 10%

profile of v8, /device:TPU:0, one launch (start us, length us, event | category | flops | bytes accessed | tf_op | source)
XLA Modules:
  0.0 46.4 jit_solution(2181092181397365160)
XLA Ops:
  0.0 4.5 %partial_beams.3 = (f32[2,13,32,128]{3,2,1,0:T(8,128)S(1)}, f32[2,13,32,128]{3,2,1,0:T(8,128)S(1)}, f32[2,13,32,128]{3,2,1,0:T(8,128)S(1)}, f32[2,13,32,128]{3,2,1,0:T(8,128)S(1)}) custom-call(s32[1]{0:T(128)} %bitcast.7.here_ref, s32[1]{0:T(128)} %bitcast.11.start_ref, bf16[100,2,540]{2,1,0:T(2,128)(2,1)} %bitcast.19, bf16[540,2,4096]{2,1,0:T(2,128)(2,1)} %bitcast.17), custom_call_target="tpu_custom_call" | custom-call | flops 920125440 | bytes 10551296 | tf_op jit(solution)/shard_map/partial_beams/pallas_call | solution.py:91
  4.5 4.0 %collective-permute-start.6 = (f16[2,13,32,128]{3,2,1,0:T(8,128)(2,1)S(1)}, f16[2,13,32,128]{3,2,1,0:T(8,128)(2,1)S(1)}, u32[]{:S(2)}, u32[]{:S(2)}) collective-permute-start(f16[2,13,32,128]{3,2,1,0:T(8,128)(2,1)S(1)} %multiply_convert_fusion.2), channel_id=1, source_target_pairs={{0,24},{8,16},{16,8},{24,0},{1,25},{9,17},{17,9},{25,1},{2,26},{10... | collective-permute-start | bytes 638984 | tf_op jit(solution)/shard_map/ppermute | solution.py:266
  8.6 0.6 %collective-permute-start.7 = (f16[2,13,32,128]{3,2,1,0:T(8,128)(2,1)S(1)}, f16[2,13,32,128]{3,2,1,0:T(8,128)(2,1)S(1)}, u32[]{:S(2)}, u32[]{:S(2)}) collective-permute-start(f16[2,13,32,128]{3,2,1,0:T(8,128)(2,1)S(1)} %multiply_convert_fusion.1), channel_id=1, source_target_pairs={{0,16},{8,24},{16,0},{24,8},{1,17},{9,25},{17,1},{25,9},{2,18},{10... | collective-permute-start | bytes 638984 | tf_op jit(solution)/shard_map/ppermute | solution.py:266
  9.2 0.1 collective-permute-start.8
  9.3 4.5 %partial_beams.2 = (f32[2,13,32,128]{3,2,1,0:T(8,128)S(1)}, f32[2,13,32,128]{3,2,1,0:T(8,128)S(1)}, f32[2,13,32,128]{3,2,1,0:T(8,128)S(1)}, f32[2,13,32,128]{3,2,1,0:T(8,128)S(1)}) custom-call(s32[1]{0:T(128)} %bitcast.7.here_ref, s32[1]{0:T(128)} %bitcast.8.start_ref, bf16[100,2,540]{2,1,0:T(2,128)(2,1)} %bitcast.20, bf16[540,2,4096]{2,1,0:T(2,128)(2,1)} %bitcast.18), custom_call_target="tpu_custom_call" | custom-call | flops 920125440 | bytes 10551296 | tf_op jit(solution)/shard_map/partial_beams/pallas_call | solution.py:91
  13.8 3.0 %collective-permute-start = (f16[2,13,32,128]{3,2,1,0:T(8,128)(2,1)S(1)}, f16[2,13,32,128]{3,2,1,0:T(8,128)(2,1)S(1)}, u32[]{:S(2)}, u32[]{:S(2)}) collective-permute-start(f16[2,13,32,128]{3,2,1,0:T(8,128)(2,1)S(1)} %multiply_convert_fusion.5), channel_id=1, source_target_pairs={{0,24},{8,16},{16,8},{24,0},{1,25},{9,17},{17,9},{25,1},{2,26},{10... | collective-permute-start | bytes 638984 | tf_op jit(solution)/shard_map/ppermute | solution.py:266
  16.9 0.6 %collective-permute-start.1 = (f16[2,13,32,128]{3,2,1,0:T(8,128)(2,1)S(1)}, f16[2,13,32,128]{3,2,1,0:T(8,128)(2,1)S(1)}, u32[]{:S(2)}, u32[]{:S(2)}) collective-permute-start(f16[2,13,32,128]{3,2,1,0:T(8,128)(2,1)S(1)} %multiply_convert_fusion.4), channel_id=1, source_target_pairs={{0,16},{8,24},{16,0},{24,8},{1,17},{9,25},{17,1},{25,9},{2,18},{10... | collective-permute-start | bytes 638984 | tf_op jit(solution)/shard_map/ppermute | solution.py:266
  17.4 0.7 %multiply_convert_fusion.3 = f16[2,13,32,128]{3,2,1,0:T(8,128)(2,1)} fusion(f32[2,13,32,128]{3,2,1,0:T(8,128)S(1)} %get-tuple-element.20), kind=kLoop, calls=%fused_computation.5 | loop fusion | flops 212992 | bytes 638976 | tf_op jit(solution)/shard_map/convert_element_type | solution.py:310
  18.6 0.2 collective-permute-start.2
  18.8 0.4 collective-permute-done.7
  19.3 0.5 %collective-permute-done.8 = f16[2,13,32,128]{3,2,1,0:T(8,128)(2,1)S(1)} collective-permute-done((f16[2,13,32,128]{3,2,1,0:T(8,128)(2,1)S(1)}, f16[2,13,32,128]{3,2,1,0:T(8,128)(2,1)S(1)}, u32[]{:S(2)}, u32[]{:S(2)}) %collective-permute-start.8) | collective-permute-done | bytes 213024 | tf_op jit(solution)/shard_map/ppermute | solution.py:266
  19.8 0.1 add_convert_fusion
  19.9 2.7 %collective-permute-start.9 = (bf16[2,7,32,128]{3,2,1,0:T(8,128)(2,1)S(1)}, bf16[2,7,32,128]{3,2,1,0:T(8,128)(2,1)S(1)}, u32[]{:S(2)}, u32[]{:S(2)}) collective-permute-start(bf16[2,7,32,128]{3,2,1,0:T(8,128)(2,1)S(1)} %get-tuple-element.30), channel_id=1, source_target_pairs={{0,4},{1,5},{2,6},{3,7},{4,0},{5,1},{6,2},{7,3},{8,12},{9,13},{10,... | collective-permute-start | bytes 344072 | tf_op jit(solution)/shard_map/ppermute | solution.py:266
  22.6 1.3 %collective-permute-start.11 = (bf16[2,7,32,128]{3,2,1,0:T(8,128)(2,1)S(1)}, bf16[2,7,32,128]{3,2,1,0:T(8,128)(2,1)S(1)}, u32[]{:S(2)}, u32[]{:S(2)}) collective-permute-start(bf16[2,7,32,128]{3,2,1,0:T(8,128)(2,1)S(1)} %get-tuple-element.29), channel_id=1, source_target_pairs={{0,6},{1,7},{2,4},{3,5},{4,2},{5,3},{6,0},{7,1},{8,14},{9,15},{10,... | collective-permute-start | bytes 344072 | tf_op jit(solution)/shard_map/ppermute | solution.py:266
  24.0 3.5 %collective-permute-done.1 = f16[2,13,32,128]{3,2,1,0:T(8,128)(2,1)S(1)} collective-permute-done((f16[2,13,32,128]{3,2,1,0:T(8,128)(2,1)S(1)}, f16[2,13,32,128]{3,2,1,0:T(8,128)(2,1)S(1)}, u32[]{:S(2)}, u32[]{:S(2)}) %collective-permute-start.1) | collective-permute-done | bytes 213024 | tf_op jit(solution)/shard_map/ppermute | solution.py:266
  27.5 0.3 collective-permute-done.2
  27.8 0.1 add_convert_fusion.1
  28.0 1.7 %collective-permute-start.4 = (bf16[2,4,32,128]{3,2,1,0:T(8,128)(2,1)S(1)}, bf16[2,4,32,128]{3,2,1,0:T(8,128)(2,1)S(1)}, u32[]{:S(2)}, u32[]{:S(2)}) collective-permute-start(bf16[2,4,32,128]{3,2,1,0:T(8,128)(2,1)S(1)} %get-tuple-element.32), channel_id=1, source_target_pairs={{0,2},{1,3},{2,0},{3,1},{4,6},{5,7},{6,4},{7,5},{8,10},{9,11},{10,... | collective-permute-start | bytes 196616 | tf_op jit(solution)/shard_map/ppermute | solution.py:266
  29.6 0.6 %collective-permute-start.3 = (bf16[2,7,32,128]{3,2,1,0:T(8,128)(2,1)S(1)}, bf16[2,7,32,128]{3,2,1,0:T(8,128)(2,1)S(1)}, u32[]{:S(2)}, u32[]{:S(2)}) collective-permute-start(bf16[2,7,32,128]{3,2,1,0:T(8,128)(2,1)S(1)} %constant_dynamic-slice_fusion.4.refs_0_), channel_id=1, source_target_pairs={{0,1},{1,0},{2,3},{3,2},{4,5},{5,4},{6,7},{7,6},{8,9},{9,8},{10,11... | collective-permute-start | bytes 344072 | tf_op jit(solution)/shard_map/ppermute | solution.py:266
  30.2 1.6 %collective-permute-done.9.refs_4_ = bf16[2,7,32,128]{3,2,1,0:T(8,128)(2,1)S(1)} collective-permute-done((bf16[2,7,32,128]{3,2,1,0:T(8,128)(2,1)S(1)}, bf16[2,7,32,128]{3,2,1,0:T(8,128)(2,1)S(1)}, u32[]{:S(2)}, u32[]{:S(2)}) %collective-permute-start.9) | collective-permute-done | bytes 114720 | tf_op jit(solution)/shard_map/ppermute | solution.py:266
  31.8 0.5 %collective-permute-start.12 = (bf16[2,7,32,128]{3,2,1,0:T(8,128)(2,1)S(1)}, bf16[2,7,32,128]{3,2,1,0:T(8,128)(2,1)S(1)}, u32[]{:S(2)}, u32[]{:S(2)}) collective-permute-start(bf16[2,7,32,128]{3,2,1,0:T(8,128)(2,1)S(1)} %collective-permute-done.11.refs_6_), channel_id=1, source_target_pairs={{0,1},{1,0},{2,3},{3,2},{4,5},{5,4},{6,7},{7,6},{8,9},{9,8},{10,11... | collective-permute-start | bytes 344072 | tf_op jit(solution)/shard_map/ppermute | solution.py:266
  32.4 1.4 %collective-permute-done.5.refs_3_ = bf16[2,4,32,128]{3,2,1,0:T(8,128)(2,1)S(1)} collective-permute-done((bf16[2,4,32,128]{3,2,1,0:T(8,128)(2,1)S(1)}, bf16[2,4,32,128]{3,2,1,0:T(8,128)(2,1)S(1)}, u32[]{:S(2)}, u32[]{:S(2)}) %collective-permute-start.5) | collective-permute-done | bytes 65568 | tf_op jit(solution)/shard_map/ppermute | solution.py:266
  33.8 2.8 %lag_profiles.1 = (bf16[4,2,16,128]{3,2,1,0:T(8,128)(2,1)S(1)}, bf16[4,2,16,128]{3,2,1,0:T(8,128)(2,1)S(1)}, bf16[4,2,16,128]{3,2,1,0:T(8,128)(2,1)S(1)}, bf16[4,2,16,128]{3,2,1,0:T(8,128)(2,1)S(1)}) custom-call(s32[1]{0:T(128)} %bitcast.chip_ref, s32[1]{0:T(128)} %bitcast.1.core_ref, f32[2,32,128]{2,1,0:T(8,128)S(1)} %bitcast.16, ...), custom_call_target="tpu_custom_call" | custom-call | tf_op jit(solution)/shard_map/lag_profiles/pallas_call | solution.py:209
  36.7 2.7 %collective-permute-start.13 = (bf16[4,2,16,128]{3,2,1,0:T(8,128)(2,1)S(1)}, bf16[4,2,16,128]{3,2,1,0:T(8,128)(2,1)S(1)}, u32[]{:S(2)}, u32[]{:S(2)}) collective-permute-start(bf16[4,2,16,128]{3,2,1,0:T(8,128)(2,1)S(1)} %get-tuple-element.25), channel_id=1, source_target_pairs={{0,6},{1,7},{2,4},{3,5},{4,2},{5,3},{6,0},{7,1},{8,14},{9,15},{10,... | collective-permute-start | bytes 98312 | tf_op jit(solution)/shard_map/ppermute | solution.py:266
  39.4 0.6 %collective-permute-start.15 = (bf16[4,2,16,128]{3,2,1,0:T(8,128)(2,1)S(1)}, bf16[4,2,16,128]{3,2,1,0:T(8,128)(2,1)S(1)}, u32[]{:S(2)}, u32[]{:S(2)}) collective-permute-start(bf16[4,2,16,128]{3,2,1,0:T(8,128)(2,1)S(1)} %get-tuple-element.26), channel_id=1, source_target_pairs={{0,4},{1,5},{2,6},{3,7},{4,0},{5,1},{6,2},{7,3},{8,12},{9,13},{10,... | collective-permute-start | bytes 98312 | tf_op jit(solution)/shard_map/ppermute | solution.py:266
  40.0 1.1 %collective-permute-start.17 = (bf16[4,2,16,128]{3,2,1,0:T(8,128)(2,1)S(1)}, bf16[4,2,16,128]{3,2,1,0:T(8,128)(2,1)S(1)}, u32[]{:S(2)}, u32[]{:S(2)}) collective-permute-start(bf16[4,2,16,128]{3,2,1,0:T(8,128)(2,1)S(1)} %get-tuple-element.27), channel_id=1, source_target_pairs={{0,2},{1,3},{2,0},{3,1},{4,6},{5,7},{6,4},{7,5},{8,10},{9,11},{10,... | collective-permute-start | bytes 98312 | tf_op jit(solution)/shard_map/ppermute | solution.py:266
  41.1 1.3 %collective-permute-done.13.refs_1_ = bf16[4,2,16,128]{3,2,1,0:T(8,128)(2,1)S(1)} collective-permute-done((bf16[4,2,16,128]{3,2,1,0:T(8,128)(2,1)S(1)}, bf16[4,2,16,128]{3,2,1,0:T(8,128)(2,1)S(1)}, u32[]{:S(2)}, u32[]{:S(2)}) %collective-permute-start.13) | collective-permute-done | bytes 32800 | tf_op jit(solution)/shard_map/ppermute | solution.py:266
  42.4 1.8 %collective-permute-done.15.refs_3_ = bf16[4,2,16,128]{3,2,1,0:T(8,128)(2,1)S(1)} collective-permute-done((bf16[4,2,16,128]{3,2,1,0:T(8,128)(2,1)S(1)}, bf16[4,2,16,128]{3,2,1,0:T(8,128)(2,1)S(1)}, u32[]{:S(2)}, u32[]{:S(2)}) %collective-permute-start.15) | collective-permute-done | bytes 32800 | tf_op jit(solution)/shard_map/ppermute | solution.py:266
  44.3 0.4 collective-permute-start.18
  44.8 0.7 %collective-permute-done.16.refs_2_ = bf16[4,2,16,128]{3,2,1,0:T(8,128)(2,1)S(1)} collective-permute-done((bf16[4,2,16,128]{3,2,1,0:T(8,128)(2,1)S(1)}, bf16[4,2,16,128]{3,2,1,0:T(8,128)(2,1)S(1)}, u32[]{:S(2)}, u32[]{:S(2)}) %collective-permute-start.16) | collective-permute-done | bytes 32800 | tf_op jit(solution)/shard_map/ppermute | solution.py:266
  45.5 0.2 collective-permute-done.18.refs_4_
  45.7 0.7 %gather_beams.1 = f32[25,16,128]{2,1,0:T(8,128)} custom-call(s32[1]{0:T(128)} %bitcast.chip_ref, s32[1]{0:T(128)} %bitcast.1.core_ref, bf16[4,2,16,128]{3,2,1,0:T(8,128)(2,1)S(1)} %collective-permute-done.14.refs_0_, bf16[4,2,16,128]{3,2,1,0:T(8,128)(2,1)S(1)} %collective-permute-done.13.refs_1_, ...), custom_call_target="tpu_custom_call" | custom-call | tf_op jit(solution)/shard_map/gather_beams/pallas_call | solution.py:242
  (38 shorter events, 0.8 us)
Async XLA Ops:
  0.0 18.2 %copy-start.1 = (s32[256]{0:T(256)S(1)}, s32[256]{0:T(256)}, u32[]{:S(2)}) copy-start(s32[256]{0:T(256)} %param.7) | copy-start | bytes 3076
  4.5 14.1 %copy-start = (s32[32,16]{0,1:T(8,128)S(1)}, s32[32,16]{0,1:T(8,128)}, u32[]{:S(2)}) copy-start(s32[32,16]{0,1:T(8,128)} %param.6) | copy-start | bytes 6148
  4.5 14.0 %collective-permute-start.6 = (f16[2,13,32,128]{3,2,1,0:T(8,128)(2,1)S(1)}, f16[2,13,32,128]{3,2,1,0:T(8,128)(2,1)S(1)}, u32[]{:S(2)}, u32[]{:S(2)}) collective-permute-start(f16[2,13,32,128]{3,2,1,0:T(8,128)(2,1)S(1)} %multiply_convert_fusion.2), channel_id=1, source_target_pairs={{0,24},{8,16},{16,8},{24,0},{1,25},{9,17},{17,9},{25,1},{2,26},{10... | collective-permute-start | bytes 638984 | tf_op jit(solution)/shard_map/ppermute | solution.py:266
  8.6 10.7 %collective-permute-start.7 = (f16[2,13,32,128]{3,2,1,0:T(8,128)(2,1)S(1)}, f16[2,13,32,128]{3,2,1,0:T(8,128)(2,1)S(1)}, u32[]{:S(2)}, u32[]{:S(2)}) collective-permute-start(f16[2,13,32,128]{3,2,1,0:T(8,128)(2,1)S(1)} %multiply_convert_fusion.1), channel_id=1, source_target_pairs={{0,16},{8,24},{16,0},{24,8},{1,17},{9,25},{17,1},{25,9},{2,18},{10... | collective-permute-start | bytes 638984 | tf_op jit(solution)/shard_map/ppermute | solution.py:266
  9.2 10.6 %collective-permute-start.8 = (f16[2,13,32,128]{3,2,1,0:T(8,128)(2,1)S(1)}, f16[2,13,32,128]{3,2,1,0:T(8,128)(2,1)S(1)}, u32[]{:S(2)}, u32[]{:S(2)}) collective-permute-start(f16[2,13,32,128]{3,2,1,0:T(8,128)(2,1)S(1)} %multiply_convert_fusion), channel_id=1, source_target_pairs={{0,8},{8,0},{16,24},{24,16},{1,9},{9,1},{17,25},{25,17},{2,10},{10... | collective-permute-start | bytes 638984 | tf_op jit(solution)/shard_map/ppermute | solution.py:266
  13.8 10.1 %collective-permute-start = (f16[2,13,32,128]{3,2,1,0:T(8,128)(2,1)S(1)}, f16[2,13,32,128]{3,2,1,0:T(8,128)(2,1)S(1)}, u32[]{:S(2)}, u32[]{:S(2)}) collective-permute-start(f16[2,13,32,128]{3,2,1,0:T(8,128)(2,1)S(1)} %multiply_convert_fusion.5), channel_id=1, source_target_pairs={{0,24},{8,16},{16,8},{24,0},{1,25},{9,17},{17,9},{25,1},{2,26},{10... | collective-permute-start | bytes 638984 | tf_op jit(solution)/shard_map/ppermute | solution.py:266
  16.9 10.6 %collective-permute-start.1 = (f16[2,13,32,128]{3,2,1,0:T(8,128)(2,1)S(1)}, f16[2,13,32,128]{3,2,1,0:T(8,128)(2,1)S(1)}, u32[]{:S(2)}, u32[]{:S(2)}) collective-permute-start(f16[2,13,32,128]{3,2,1,0:T(8,128)(2,1)S(1)} %multiply_convert_fusion.4), channel_id=1, source_target_pairs={{0,16},{8,24},{16,0},{24,8},{1,17},{9,25},{17,1},{25,9},{2,18},{10... | collective-permute-start | bytes 638984 | tf_op jit(solution)/shard_map/ppermute | solution.py:266
  18.6 9.2 %collective-permute-start.2 = (f16[2,13,32,128]{3,2,1,0:T(8,128)(2,1)}, f16[2,13,32,128]{3,2,1,0:T(8,128)(2,1)S(1)}, u32[]{:S(2)}, u32[]{:S(2)}) collective-permute-start(f16[2,13,32,128]{3,2,1,0:T(8,128)(2,1)} %multiply_convert_fusion.3), channel_id=1, source_target_pairs={{0,8},{8,0},{16,24},{24,16},{1,9},{9,1},{17,25},{25,17},{2,10},{10... | collective-permute-start | bytes 638984 | tf_op jit(solution)/shard_map/ppermute | solution.py:266
  19.9 11.8 %collective-permute-start.9 = (bf16[2,7,32,128]{3,2,1,0:T(8,128)(2,1)S(1)}, bf16[2,7,32,128]{3,2,1,0:T(8,128)(2,1)S(1)}, u32[]{:S(2)}, u32[]{:S(2)}) collective-permute-start(bf16[2,7,32,128]{3,2,1,0:T(8,128)(2,1)S(1)} %get-tuple-element.30), channel_id=1, source_target_pairs={{0,4},{1,5},{2,6},{3,7},{4,0},{5,1},{6,2},{7,3},{8,12},{9,13},{10,... | collective-permute-start | bytes 344072 | tf_op jit(solution)/shard_map/ppermute | solution.py:266
  22.6 9.2 %collective-permute-start.11 = (bf16[2,7,32,128]{3,2,1,0:T(8,128)(2,1)S(1)}, bf16[2,7,32,128]{3,2,1,0:T(8,128)(2,1)S(1)}, u32[]{:S(2)}, u32[]{:S(2)}) collective-permute-start(bf16[2,7,32,128]{3,2,1,0:T(8,128)(2,1)S(1)} %get-tuple-element.29), channel_id=1, source_target_pairs={{0,6},{1,7},{2,4},{3,5},{4,2},{5,3},{6,0},{7,1},{8,14},{9,15},{10,... | collective-permute-start | bytes 344072 | tf_op jit(solution)/shard_map/ppermute | solution.py:266
  28.0 4.5 %collective-permute-start.4 = (bf16[2,4,32,128]{3,2,1,0:T(8,128)(2,1)S(1)}, bf16[2,4,32,128]{3,2,1,0:T(8,128)(2,1)S(1)}, u32[]{:S(2)}, u32[]{:S(2)}) collective-permute-start(bf16[2,4,32,128]{3,2,1,0:T(8,128)(2,1)S(1)} %get-tuple-element.32), channel_id=1, source_target_pairs={{0,2},{1,3},{2,0},{3,1},{4,6},{5,7},{6,4},{7,5},{8,10},{9,11},{10,... | collective-permute-start | bytes 196616 | tf_op jit(solution)/shard_map/ppermute | solution.py:266
  29.6 4.2 %collective-permute-start.5 = (bf16[2,4,32,128]{3,2,1,0:T(8,128)(2,1)S(1)}, bf16[2,4,32,128]{3,2,1,0:T(8,128)(2,1)S(1)}, u32[]{:S(2)}, u32[]{:S(2)}) collective-permute-start(bf16[2,4,32,128]{3,2,1,0:T(8,128)(2,1)S(1)} %get-tuple-element.31), channel_id=1, source_target_pairs={{0,3},{1,2},{2,1},{3,0},{4,7},{5,6},{6,5},{7,4},{8,11},{9,10},{10,... | collective-permute-start | bytes 196616 | tf_op jit(solution)/shard_map/ppermute | solution.py:266
  29.6 4.2 %collective-permute-start.3 = (bf16[2,7,32,128]{3,2,1,0:T(8,128)(2,1)S(1)}, bf16[2,7,32,128]{3,2,1,0:T(8,128)(2,1)S(1)}, u32[]{:S(2)}, u32[]{:S(2)}) collective-permute-start(bf16[2,7,32,128]{3,2,1,0:T(8,128)(2,1)S(1)} %constant_dynamic-slice_fusion.4.refs_0_), channel_id=1, source_target_pairs={{0,1},{1,0},{2,3},{3,2},{4,5},{5,4},{6,7},{7,6},{8,9},{9,8},{10,11... | collective-permute-start | bytes 344072 | tf_op jit(solution)/shard_map/ppermute | solution.py:266
  31.8 2.0 %collective-permute-start.10 = (bf16[2,7,32,128]{3,2,1,0:T(8,128)(2,1)S(1)}, bf16[2,7,32,128]{3,2,1,0:T(8,128)(2,1)S(1)}, u32[]{:S(2)}, u32[]{:S(2)}) collective-permute-start(bf16[2,7,32,128]{3,2,1,0:T(8,128)(2,1)S(1)} %collective-permute-done.9.refs_4_), channel_id=1, source_target_pairs={{0,1},{1,0},{2,3},{3,2},{4,5},{5,4},{6,7},{7,6},{8,9},{9,8},{10,11... | collective-permute-start | bytes 344072 | tf_op jit(solution)/shard_map/ppermute | solution.py:266
  31.8 2.0 %collective-permute-start.12 = (bf16[2,7,32,128]{3,2,1,0:T(8,128)(2,1)S(1)}, bf16[2,7,32,128]{3,2,1,0:T(8,128)(2,1)S(1)}, u32[]{:S(2)}, u32[]{:S(2)}) collective-permute-start(bf16[2,7,32,128]{3,2,1,0:T(8,128)(2,1)S(1)} %collective-permute-done.11.refs_6_), channel_id=1, source_target_pairs={{0,1},{1,0},{2,3},{3,2},{4,5},{5,4},{6,7},{7,6},{8,9},{9,8},{10,11... | collective-permute-start | bytes 344072 | tf_op jit(solution)/shard_map/ppermute | solution.py:266
  36.7 5.8 %collective-permute-start.13 = (bf16[4,2,16,128]{3,2,1,0:T(8,128)(2,1)S(1)}, bf16[4,2,16,128]{3,2,1,0:T(8,128)(2,1)S(1)}, u32[]{:S(2)}, u32[]{:S(2)}) collective-permute-start(bf16[4,2,16,128]{3,2,1,0:T(8,128)(2,1)S(1)} %get-tuple-element.25), channel_id=1, source_target_pairs={{0,6},{1,7},{2,4},{3,5},{4,2},{5,3},{6,0},{7,1},{8,14},{9,15},{10,... | collective-permute-start | bytes 98312 | tf_op jit(solution)/shard_map/ppermute | solution.py:266
  39.4 4.9 %collective-permute-start.15 = (bf16[4,2,16,128]{3,2,1,0:T(8,128)(2,1)S(1)}, bf16[4,2,16,128]{3,2,1,0:T(8,128)(2,1)S(1)}, u32[]{:S(2)}, u32[]{:S(2)}) collective-permute-start(bf16[4,2,16,128]{3,2,1,0:T(8,128)(2,1)S(1)} %get-tuple-element.26), channel_id=1, source_target_pairs={{0,4},{1,5},{2,6},{3,7},{4,0},{5,1},{6,2},{7,3},{8,12},{9,13},{10,... | collective-permute-start | bytes 98312 | tf_op jit(solution)/shard_map/ppermute | solution.py:266
  40.0 4.4 %collective-permute-start.17 = (bf16[4,2,16,128]{3,2,1,0:T(8,128)(2,1)S(1)}, bf16[4,2,16,128]{3,2,1,0:T(8,128)(2,1)S(1)}, u32[]{:S(2)}, u32[]{:S(2)}) collective-permute-start(bf16[4,2,16,128]{3,2,1,0:T(8,128)(2,1)S(1)} %get-tuple-element.27), channel_id=1, source_target_pairs={{0,2},{1,3},{2,0},{3,1},{4,6},{5,7},{6,4},{7,5},{8,10},{9,11},{10,... | collective-permute-start | bytes 98312 | tf_op jit(solution)/shard_map/ppermute | solution.py:266
  41.1 3.7 %collective-permute-start.19 = (bf16[4,2,16,128]{3,2,1,0:T(8,128)(2,1)S(1)}, bf16[4,2,16,128]{3,2,1,0:T(8,128)(2,1)S(1)}, u32[]{:S(2)}, u32[]{:S(2)}) collective-permute-start(bf16[4,2,16,128]{3,2,1,0:T(8,128)(2,1)S(1)} %get-tuple-element.28.refs_7_), channel_id=1, source_target_pairs={{0,1},{1,0},{2,3},{3,2},{4,5},{5,4},{6,7},{7,6},{8,9},{9,8},{10,11... | collective-permute-start | bytes 98312 | tf_op jit(solution)/shard_map/ppermute | solution.py:266
  42.4 2.4 %collective-permute-start.14 = (bf16[4,2,16,128]{3,2,1,0:T(8,128)(2,1)S(1)}, bf16[4,2,16,128]{3,2,1,0:T(8,128)(2,1)S(1)}, u32[]{:S(2)}, u32[]{:S(2)}) collective-permute-start(bf16[4,2,16,128]{3,2,1,0:T(8,128)(2,1)S(1)} %collective-permute-done.13.refs_1_), channel_id=1, source_target_pairs={{0,1},{1,0},{2,3},{3,2},{4,5},{5,4},{6,7},{7,6},{8,9},{9,8},{10,11... | collective-permute-start | bytes 98312 | tf_op jit(solution)/shard_map/ppermute | solution.py:266
  44.3 1.2 %collective-permute-start.16 = (bf16[4,2,16,128]{3,2,1,0:T(8,128)(2,1)S(1)}, bf16[4,2,16,128]{3,2,1,0:T(8,128)(2,1)S(1)}, u32[]{:S(2)}, u32[]{:S(2)}) collective-permute-start(bf16[4,2,16,128]{3,2,1,0:T(8,128)(2,1)S(1)} %collective-permute-done.15.refs_3_), channel_id=1, source_target_pairs={{0,1},{1,0},{2,3},{3,2},{4,5},{5,4},{6,7},{7,6},{8,9},{9,8},{10,11... | collective-permute-start | bytes 98312 | tf_op jit(solution)/shard_map/ppermute | solution.py:266
  44.3 1.3 %collective-permute-start.18 = (bf16[4,2,16,128]{3,2,1,0:T(8,128)(2,1)S(1)}, bf16[4,2,16,128]{3,2,1,0:T(8,128)(2,1)S(1)}, u32[]{:S(2)}, u32[]{:S(2)}) collective-permute-start(bf16[4,2,16,128]{3,2,1,0:T(8,128)(2,1)S(1)} %collective-permute-done.17.refs_5_), channel_id=1, source_target_pairs={{0,1},{1,0},{2,3},{3,2},{4,5},{5,4},{6,7},{7,6},{8,9},{9,8},{10,11... | collective-permute-start | bytes 98312 | tf_op jit(solution)/shard_map/ppermute | solution.py:266

commit v9 on v8

--- a/solution.py
+++ b/solution.py
@@ -114,8 +114,8 @@
 
 def lag_kernel(scale, count, chip_ref, core_ref, sign_ref, gate_ref, *refs):
     pieces_in = refs[:count]
-    out_refs = refs[count:-4]
-    x_ref, both_ref, lag_ref, sum_ref = refs[-4:]
+    out_refs = refs[count:-5]
+    x_ref, both_ref, back_ref, lag_ref, sum_ref = refs[-5:]
     sources, _, slots, rows, _ = x_ref.shape
     chip = chip_ref[0]
     core = core_ref[0]
@@ -136,7 +136,6 @@
         == LANES - 1
     ).astype(F32).astype(BF16)
     real_lane = lax.broadcasted_iota(jnp.int32, (LANES, LANES), 1) < LAGS
-    real_depth = lax.broadcasted_iota(jnp.int32, (LANES, 2 * depth), 1) < depth
 
     def assemble(slot, part):
         loaded = [x_ref[d, part, slot].astype(F32) for d in range(sources)]
@@ -166,25 +165,27 @@
         assemble(slot, 0)
         assemble(slot, 1)
     for slot in range(slots):
+        for block in range(BLOCKS + 1):
+            columns = slice(block * LANES, (block + 1) * LANES)
+            back = slice((BLOCKS - block) * LANES, (BLOCKS - block + 1) * LANES)
+            turned = jnp.dot(both_ref[slot, :, columns], flip, preferred_element_type=F32)
+            back_ref[slot, :, back] = turned.astype(BF16)
+    for slot in range(slots):
         held = slice(slot * LANES, (slot + 1) * LANES)
         for block in range(BLOCKS):
             columns = slice(block * LANES, (block + 1) * LANES)
-            base = lax.dot_general(
-                flip,
-                both_ref[slot, :, columns],
-                (((1,), (1,)), ((), ())),
+            base = both_ref[slot, :, columns]
+            turned = jnp.concatenate([-base[depth:], base[:depth]], 0)
+            first = (BLOCKS - 1 - block) * LANES
+            gram = lax.dot_general(
+                jnp.concatenate([base, turned], 1),
+                back_ref[slot, :, first : first + 2 * LANES],
+                (((0,), (0,)), ((), ())),
                 preferred_element_type=F32,
             )
-            swapped = pltpu.roll(base, depth, 1)
-            turned = jnp.where(real_depth, -swapped, swapped)
-            gram = jnp.dot(
-                jnp.concatenate([base, turned], 0).astype(BF16),
-                both_ref[slot, :, block * LANES : (block + 2) * LANES],
-                preferred_element_type=F32,
-            )
-            real_lags = pltpu.roll(gram[:LANES], LANES, 1, stride=1, stride_axis=0)
-            imag_lags = pltpu.roll(gram[LANES:], LANES + LAGS, 1, stride=1, stride_axis=0)
-            lags = jnp.where(real_lane, real_lags[:, :LANES], imag_lags[:, :LANES])
+            real_lags = pltpu.roll(gram[:LANES], LANES + 1, 1, stride=1, stride_axis=0)
+            imag_lags = pltpu.roll(gram[LANES:], LAGS + 1, 1, stride=1, stride_axis=0)
+            lags = jnp.where(real_lane, imag_lags[:, :LANES], real_lags[:, :LANES])
             high = lags.astype(BF16)
             low = (lags - high.astype(F32)).astype(BF16)
             top = 2 * block * LANES
@@ -194,7 +195,8 @@
     gates = jnp.concatenate([gate for gate in gates for _ in range(2)], 1)
     sums = jnp.dot(gates, lag_ref[...], preferred_element_type=F32)
     for slot in range(slots):
-        sum_ref[slot] = sums[:, slot * LANES : (slot + 1) * LANES] * scale
+        rows_of = (sums[:, slot * LANES : (slot + 1) * LANES] * scale).astype(BF16)
+        sum_ref[slot] = jnp.dot(rows_of, flip, preferred_element_type=F32)
     for step, out_ref in enumerate(reversed(out_refs)):
         gates = out_ref.shape[1] * out_ref.shape[2]
         first = pl.multiple_of((chip ^ step) * gates, gates)
@@ -214,6 +216,7 @@
         scratch_shapes=[
             pltpu.VMEM((sources, 2, slots, rows, LANES), BF16),
             pltpu.VMEM((slots, 2 * row_groups * rows, (BLOCKS + 1) * LANES), BF16),
+            pltpu.VMEM((slots, 2 * row_groups * rows, (BLOCKS + 1) * LANES), BF16),
             pltpu.VMEM((2 * IPP_LEN, slots * LANES), BF16),
             pltpu.VMEM((slots, GATES, LANES), F32),
         ],
@@ -256,9 +259,7 @@
 
 
 def gate_rows(gate_map):
-    position = jnp.arange(IPP_LEN)
-    position = position // LANES * LANES + (LANES - 1 - position % LANES)
-    gates = jnp.repeat(gate_map, SEC_LEN).reshape(BLOCKS, LANES)[:, ::-1].reshape(IPP_LEN)
+    gates = jnp.repeat(gate_map, SEC_LEN)
     return (jnp.arange(GATES)[:, None] == gates[None, :]).astype(BF16)
 
 

time: 46.5 us -> 46.2 us (level)
  no operation moved by 1% of the time
where the time goes in v9:
time: 46.2 us; the launch traced here: 46 us
  starting transfers between devices  20.2 us (44%)
  Pallas kernels  12.1 us (26%)
  waiting for transfers between devices  11.9 us (26%)
  other arithmetic  1.3 us (3%)
    ppermute x20, starting transfers between devices, exchanged(): lax.ppermute(block, axis, [(i, i ^ step) for i in range(lax.axis_size(axi...  20.2 us
    ppermute x20, waiting for transfers between devices, exchanged(): lax.ppermute(block, axis, [(i, i ^ step) for i in range(lax.axis_size(axi...  11.9 us
    pallas_call x2, Pallas kernels, partial_beams(): pl.pallas_call(beam_kernel, in_specs=[pl.BlockSpec(memory_space=pltpu.SME...  8.92 us
    pallas_call x1, Pallas kernels, lag_profiles(): pl.pallas_call(functools.partial(lag_kernel, scale, len(pieces)), in_spec...  2.49 us
    convert_element_type x6, other arithmetic, body(): came = exchanged((partial[step] * gain).astype(jnp.float16), 'sub', step)  0.97 us
  transfers between devices with their start and end apart: 20, of which 11 were waited for; matrix products, arithmetic and copies ran while one was open for 4% of the time, Pallas kernels for 10%

profile of v9, /device:TPU:0, one launch (start us, length us, event | category | flops | bytes accessed | tf_op | source)
XLA Modules:
  0.0 46.0 jit_solution(12812947974886153045)
XLA Ops:
  0.0 4.5 %partial_beams.3 = (f32[2,13,32,128]{3,2,1,0:T(8,128)S(1)}, f32[2,13,32,128]{3,2,1,0:T(8,128)S(1)}, f32[2,13,32,128]{3,2,1,0:T(8,128)S(1)}, f32[2,13,32,128]{3,2,1,0:T(8,128)S(1)}) custom-call(s32[1]{0:T(128)} %bitcast.5.here_ref, s32[1]{0:T(128)} %bitcast.9.start_ref, bf16[100,2,540]{2,1,0:T(2,128)(2,1)} %bitcast.17, bf16[540,2,4096]{2,1,0:T(2,128)(2,1)} %bitcast.15), custom_call_target="tpu_custom_call" | custom-call | flops 920125440 | bytes 10551296 | tf_op jit(solution)/shard_map/partial_beams/pallas_call | solution.py:91
  4.5 4.0 %collective-permute-start.6 = (f16[2,13,32,128]{3,2,1,0:T(8,128)(2,1)S(1)}, f16[2,13,32,128]{3,2,1,0:T(8,128)(2,1)S(1)}, u32[]{:S(2)}, u32[]{:S(2)}) collective-permute-start(f16[2,13,32,128]{3,2,1,0:T(8,128)(2,1)S(1)} %multiply_convert_fusion.2), channel_id=1, source_target_pairs={{0,24},{8,16},{16,8},{24,0},{1,25},{9,17},{17,9},{25,1},{2,26},{10... | collective-permute-start | bytes 638984 | tf_op jit(solution)/shard_map/ppermute | solution.py:267
  8.6 0.6 %collective-permute-start.7 = (f16[2,13,32,128]{3,2,1,0:T(8,128)(2,1)S(1)}, f16[2,13,32,128]{3,2,1,0:T(8,128)(2,1)S(1)}, u32[]{:S(2)}, u32[]{:S(2)}) collective-permute-start(f16[2,13,32,128]{3,2,1,0:T(8,128)(2,1)S(1)} %multiply_convert_fusion.1), channel_id=1, source_target_pairs={{0,16},{8,24},{16,0},{24,8},{1,17},{9,25},{17,1},{25,9},{2,18},{10... | collective-permute-start | bytes 638984 | tf_op jit(solution)/shard_map/ppermute | solution.py:267
  9.3 4.5 %partial_beams.2 = (f32[2,13,32,128]{3,2,1,0:T(8,128)S(1)}, f32[2,13,32,128]{3,2,1,0:T(8,128)S(1)}, f32[2,13,32,128]{3,2,1,0:T(8,128)S(1)}, f32[2,13,32,128]{3,2,1,0:T(8,128)S(1)}) custom-call(s32[1]{0:T(128)} %bitcast.5.here_ref, s32[1]{0:T(128)} %bitcast.6.start_ref, bf16[100,2,540]{2,1,0:T(2,128)(2,1)} %bitcast.18, bf16[540,2,4096]{2,1,0:T(2,128)(2,1)} %bitcast.16), custom_call_target="tpu_custom_call" | custom-call | flops 920125440 | bytes 10551296 | tf_op jit(solution)/shard_map/partial_beams/pallas_call | solution.py:91
  13.8 3.0 %collective-permute-start = (f16[2,13,32,128]{3,2,1,0:T(8,128)(2,1)S(1)}, f16[2,13,32,128]{3,2,1,0:T(8,128)(2,1)S(1)}, u32[]{:S(2)}, u32[]{:S(2)}) collective-permute-start(f16[2,13,32,128]{3,2,1,0:T(8,128)(2,1)S(1)} %multiply_convert_fusion.5), channel_id=1, source_target_pairs={{0,24},{8,16},{16,8},{24,0},{1,25},{9,17},{17,9},{25,1},{2,26},{10... | collective-permute-start | bytes 638984 | tf_op jit(solution)/shard_map/ppermute | solution.py:267
  16.9 0.6 %collective-permute-start.1 = (f16[2,13,32,128]{3,2,1,0:T(8,128)(2,1)S(1)}, f16[2,13,32,128]{3,2,1,0:T(8,128)(2,1)S(1)}, u32[]{:S(2)}, u32[]{:S(2)}) collective-permute-start(f16[2,13,32,128]{3,2,1,0:T(8,128)(2,1)S(1)} %multiply_convert_fusion.4), channel_id=1, source_target_pairs={{0,16},{8,24},{16,0},{24,8},{1,17},{9,25},{17,1},{25,9},{2,18},{10... | collective-permute-start | bytes 638984 | tf_op jit(solution)/shard_map/ppermute | solution.py:267
  17.4 0.7 %multiply_convert_fusion.3 = f16[2,13,32,128]{3,2,1,0:T(8,128)(2,1)} fusion(f32[2,13,32,128]{3,2,1,0:T(8,128)S(1)} %get-tuple-element.20), kind=kLoop, calls=%fused_computation.5 | loop fusion | flops 212992 | bytes 638976 | tf_op jit(solution)/shard_map/convert_element_type | solution.py:311
  18.3 0.1 eq.21
  18.5 0.2 collective-permute-start.2
  18.8 0.5 %collective-permute-done.7 = f16[2,13,32,128]{3,2,1,0:T(8,128)(2,1)S(1)} collective-permute-done((f16[2,13,32,128]{3,2,1,0:T(8,128)(2,1)S(1)}, f16[2,13,32,128]{3,2,1,0:T(8,128)(2,1)S(1)}, u32[]{:S(2)}, u32[]{:S(2)}) %collective-permute-start.7) | collective-permute-done | bytes 213024 | tf_op jit(solution)/shard_map/ppermute | solution.py:267
  19.3 0.5 %collective-permute-done.8 = f16[2,13,32,128]{3,2,1,0:T(8,128)(2,1)S(1)} collective-permute-done((f16[2,13,32,128]{3,2,1,0:T(8,128)(2,1)S(1)}, f16[2,13,32,128]{3,2,1,0:T(8,128)(2,1)S(1)}, u32[]{:S(2)}, u32[]{:S(2)}) %collective-permute-start.8) | collective-permute-done | bytes 213024 | tf_op jit(solution)/shard_map/ppermute | solution.py:267
  19.8 0.1 add_convert_fusion
  19.9 2.7 %collective-permute-start.9 = (bf16[2,7,32,128]{3,2,1,0:T(8,128)(2,1)S(1)}, bf16[2,7,32,128]{3,2,1,0:T(8,128)(2,1)S(1)}, u32[]{:S(2)}, u32[]{:S(2)}) collective-permute-start(bf16[2,7,32,128]{3,2,1,0:T(8,128)(2,1)S(1)} %get-tuple-element.30), channel_id=1, source_target_pairs={{0,4},{1,5},{2,6},{3,7},{4,0},{5,1},{6,2},{7,3},{8,12},{9,13},{10,... | collective-permute-start | bytes 344072 | tf_op jit(solution)/shard_map/ppermute | solution.py:267
  22.6 1.3 %collective-permute-start.11 = (bf16[2,7,32,128]{3,2,1,0:T(8,128)(2,1)S(1)}, bf16[2,7,32,128]{3,2,1,0:T(8,128)(2,1)S(1)}, u32[]{:S(2)}, u32[]{:S(2)}) collective-permute-start(bf16[2,7,32,128]{3,2,1,0:T(8,128)(2,1)S(1)} %get-tuple-element.29), channel_id=1, source_target_pairs={{0,6},{1,7},{2,4},{3,5},{4,2},{5,3},{6,0},{7,1},{8,14},{9,15},{10,... | collective-permute-start | bytes 344072 | tf_op jit(solution)/shard_map/ppermute | solution.py:267
  24.0 3.5 %collective-permute-done.1 = f16[2,13,32,128]{3,2,1,0:T(8,128)(2,1)S(1)} collective-permute-done((f16[2,13,32,128]{3,2,1,0:T(8,128)(2,1)S(1)}, f16[2,13,32,128]{3,2,1,0:T(8,128)(2,1)S(1)}, u32[]{:S(2)}, u32[]{:S(2)}) %collective-permute-start.1) | collective-permute-done | bytes 213024 | tf_op jit(solution)/shard_map/ppermute | solution.py:267
  27.5 0.3 collective-permute-done.2
  27.8 0.1 add_convert_fusion.1
  28.0 1.7 %collective-permute-start.4 = (bf16[2,4,32,128]{3,2,1,0:T(8,128)(2,1)S(1)}, bf16[2,4,32,128]{3,2,1,0:T(8,128)(2,1)S(1)}, u32[]{:S(2)}, u32[]{:S(2)}) collective-permute-start(bf16[2,4,32,128]{3,2,1,0:T(8,128)(2,1)S(1)} %get-tuple-element.32), channel_id=1, source_target_pairs={{0,2},{1,3},{2,0},{3,1},{4,6},{5,7},{6,4},{7,5},{8,10},{9,11},{10,... | collective-permute-start | bytes 196616 | tf_op jit(solution)/shard_map/ppermute | solution.py:267
  29.6 0.6 %collective-permute-start.3 = (bf16[2,7,32,128]{3,2,1,0:T(8,128)(2,1)S(1)}, bf16[2,7,32,128]{3,2,1,0:T(8,128)(2,1)S(1)}, u32[]{:S(2)}, u32[]{:S(2)}) collective-permute-start(bf16[2,7,32,128]{3,2,1,0:T(8,128)(2,1)S(1)} %constant_dynamic-slice_fusion.4.refs_0_), channel_id=1, source_target_pairs={{0,1},{1,0},{2,3},{3,2},{4,5},{5,4},{6,7},{7,6},{8,9},{9,8},{10,11... | collective-permute-start | bytes 344072 | tf_op jit(solution)/shard_map/ppermute | solution.py:267
  30.2 1.6 %collective-permute-done.9.refs_4_ = bf16[2,7,32,128]{3,2,1,0:T(8,128)(2,1)S(1)} collective-permute-done((bf16[2,7,32,128]{3,2,1,0:T(8,128)(2,1)S(1)}, bf16[2,7,32,128]{3,2,1,0:T(8,128)(2,1)S(1)}, u32[]{:S(2)}, u32[]{:S(2)}) %collective-permute-start.9) | collective-permute-done | bytes 114720 | tf_op jit(solution)/shard_map/ppermute | solution.py:267
  31.8 0.5 %collective-permute-start.12 = (bf16[2,7,32,128]{3,2,1,0:T(8,128)(2,1)S(1)}, bf16[2,7,32,128]{3,2,1,0:T(8,128)(2,1)S(1)}, u32[]{:S(2)}, u32[]{:S(2)}) collective-permute-start(bf16[2,7,32,128]{3,2,1,0:T(8,128)(2,1)S(1)} %collective-permute-done.11.refs_6_), channel_id=1, source_target_pairs={{0,1},{1,0},{2,3},{3,2},{4,5},{5,4},{6,7},{7,6},{8,9},{9,8},{10,11... | collective-permute-start | bytes 344072 | tf_op jit(solution)/shard_map/ppermute | solution.py:267
  32.4 1.4 %collective-permute-done.5.refs_3_ = bf16[2,4,32,128]{3,2,1,0:T(8,128)(2,1)S(1)} collective-permute-done((bf16[2,4,32,128]{3,2,1,0:T(8,128)(2,1)S(1)}, bf16[2,4,32,128]{3,2,1,0:T(8,128)(2,1)S(1)}, u32[]{:S(2)}, u32[]{:S(2)}) %collective-permute-start.5) | collective-permute-done | bytes 65568 | tf_op jit(solution)/shard_map/ppermute | solution.py:267
  33.8 2.5 %lag_profiles.1 = (bf16[4,2,16,128]{3,2,1,0:T(8,128)(2,1)S(1)}, bf16[4,2,16,128]{3,2,1,0:T(8,128)(2,1)S(1)}, bf16[4,2,16,128]{3,2,1,0:T(8,128)(2,1)S(1)}, bf16[4,2,16,128]{3,2,1,0:T(8,128)(2,1)S(1)}) custom-call(s32[1]{0:T(128)} %bitcast.chip_ref, s32[1]{0:T(128)} %bitcast.1.core_ref, f32[2,32,128]{2,1,0:T(8,128)S(1)} %bitcast.14, ...), custom_call_target="tpu_custom_call" | custom-call | tf_op jit(solution)/shard_map/lag_profiles/pallas_call | solution.py:211
  36.3 2.7 %collective-permute-start.13 = (bf16[4,2,16,128]{3,2,1,0:T(8,128)(2,1)S(1)}, bf16[4,2,16,128]{3,2,1,0:T(8,128)(2,1)S(1)}, u32[]{:S(2)}, u32[]{:S(2)}) collective-permute-start(bf16[4,2,16,128]{3,2,1,0:T(8,128)(2,1)S(1)} %get-tuple-element.25), channel_id=1, source_target_pairs={{0,6},{1,7},{2,4},{3,5},{4,2},{5,3},{6,0},{7,1},{8,14},{9,15},{10,... | collective-permute-start | bytes 98312 | tf_op jit(solution)/shard_map/ppermute | solution.py:267
  39.1 0.6 %collective-permute-start.15 = (bf16[4,2,16,128]{3,2,1,0:T(8,128)(2,1)S(1)}, bf16[4,2,16,128]{3,2,1,0:T(8,128)(2,1)S(1)}, u32[]{:S(2)}, u32[]{:S(2)}) collective-permute-start(bf16[4,2,16,128]{3,2,1,0:T(8,128)(2,1)S(1)} %get-tuple-element.26), channel_id=1, source_target_pairs={{0,4},{1,5},{2,6},{3,7},{4,0},{5,1},{6,2},{7,3},{8,12},{9,13},{10,... | collective-permute-start | bytes 98312 | tf_op jit(solution)/shard_map/ppermute | solution.py:267
  39.6 1.1 %collective-permute-start.17 = (bf16[4,2,16,128]{3,2,1,0:T(8,128)(2,1)S(1)}, bf16[4,2,16,128]{3,2,1,0:T(8,128)(2,1)S(1)}, u32[]{:S(2)}, u32[]{:S(2)}) collective-permute-start(bf16[4,2,16,128]{3,2,1,0:T(8,128)(2,1)S(1)} %get-tuple-element.27), channel_id=1, source_target_pairs={{0,2},{1,3},{2,0},{3,1},{4,6},{5,7},{6,4},{7,5},{8,10},{9,11},{10,... | collective-permute-start | bytes 98312 | tf_op jit(solution)/shard_map/ppermute | solution.py:267
  40.8 1.3 %collective-permute-done.13.refs_1_ = bf16[4,2,16,128]{3,2,1,0:T(8,128)(2,1)S(1)} collective-permute-done((bf16[4,2,16,128]{3,2,1,0:T(8,128)(2,1)S(1)}, bf16[4,2,16,128]{3,2,1,0:T(8,128)(2,1)S(1)}, u32[]{:S(2)}, u32[]{:S(2)}) %collective-permute-start.13) | collective-permute-done | bytes 32800 | tf_op jit(solution)/shard_map/ppermute | solution.py:267
  42.1 1.8 %collective-permute-done.15.refs_3_ = bf16[4,2,16,128]{3,2,1,0:T(8,128)(2,1)S(1)} collective-permute-done((bf16[4,2,16,128]{3,2,1,0:T(8,128)(2,1)S(1)}, bf16[4,2,16,128]{3,2,1,0:T(8,128)(2,1)S(1)}, u32[]{:S(2)}, u32[]{:S(2)}) %collective-permute-start.15) | collective-permute-done | bytes 32800 | tf_op jit(solution)/shard_map/ppermute | solution.py:267
  44.0 0.4 collective-permute-start.18
  44.5 0.7 %collective-permute-done.16.refs_2_ = bf16[4,2,16,128]{3,2,1,0:T(8,128)(2,1)S(1)} collective-permute-done((bf16[4,2,16,128]{3,2,1,0:T(8,128)(2,1)S(1)}, bf16[4,2,16,128]{3,2,1,0:T(8,128)(2,1)S(1)}, u32[]{:S(2)}, u32[]{:S(2)}) %collective-permute-start.16) | collective-permute-done | bytes 32800 | tf_op jit(solution)/shard_map/ppermute | solution.py:267
  45.2 0.2 collective-permute-done.18.refs_4_
  45.3 0.7 %gather_beams.1 = f32[25,16,128]{2,1,0:T(8,128)} custom-call(s32[1]{0:T(128)} %bitcast.chip_ref, s32[1]{0:T(128)} %bitcast.1.core_ref, bf16[4,2,16,128]{3,2,1,0:T(8,128)(2,1)S(1)} %collective-permute-done.14.refs_0_, bf16[4,2,16,128]{3,2,1,0:T(8,128)(2,1)S(1)} %collective-permute-done.13.refs_1_, ...), custom_call_target="tpu_custom_call" | custom-call | tf_op jit(solution)/shard_map/gather_beams/pallas_call | solution.py:245
  (35 shorter events, 0.8 us)
Async XLA Ops:
  0.0 18.2 %copy-start.1 = (s32[256]{0:T(256)S(1)}, s32[256]{0:T(256)}, u32[]{:S(2)}) copy-start(s32[256]{0:T(256)} %param.7) | copy-start | bytes 3076
  4.5 14.0 %copy-start = (s32[32,16]{0,1:T(8,128)S(1)}, s32[32,16]{0,1:T(8,128)}, u32[]{:S(2)}) copy-start(s32[32,16]{0,1:T(8,128)} %param.6) | copy-start | bytes 6148
  4.5 14.0 %collective-permute-start.6 = (f16[2,13,32,128]{3,2,1,0:T(8,128)(2,1)S(1)}, f16[2,13,32,128]{3,2,1,0:T(8,128)(2,1)S(1)}, u32[]{:S(2)}, u32[]{:S(2)}) collective-permute-start(f16[2,13,32,128]{3,2,1,0:T(8,128)(2,1)S(1)} %multiply_convert_fusion.2), channel_id=1, source_target_pairs={{0,24},{8,16},{16,8},{24,0},{1,25},{9,17},{17,9},{25,1},{2,26},{10... | collective-permute-start | bytes 638984 | tf_op jit(solution)/shard_map/ppermute | solution.py:267
  8.6 10.7 %collective-permute-start.7 = (f16[2,13,32,128]{3,2,1,0:T(8,128)(2,1)S(1)}, f16[2,13,32,128]{3,2,1,0:T(8,128)(2,1)S(1)}, u32[]{:S(2)}, u32[]{:S(2)}) collective-permute-start(f16[2,13,32,128]{3,2,1,0:T(8,128)(2,1)S(1)} %multiply_convert_fusion.1), channel_id=1, source_target_pairs={{0,16},{8,24},{16,0},{24,8},{1,17},{9,25},{17,1},{25,9},{2,18},{10... | collective-permute-start | bytes 638984 | tf_op jit(solution)/shard_map/ppermute | solution.py:267
  9.2 10.6 %collective-permute-start.8 = (f16[2,13,32,128]{3,2,1,0:T(8,128)(2,1)S(1)}, f16[2,13,32,128]{3,2,1,0:T(8,128)(2,1)S(1)}, u32[]{:S(2)}, u32[]{:S(2)}) collective-permute-start(f16[2,13,32,128]{3,2,1,0:T(8,128)(2,1)S(1)} %multiply_convert_fusion), channel_id=1, source_target_pairs={{0,8},{8,0},{16,24},{24,16},{1,9},{9,1},{17,25},{25,17},{2,10},{10... | collective-permute-start | bytes 638984 | tf_op jit(solution)/shard_map/ppermute | solution.py:267
  13.8 10.1 %collective-permute-start = (f16[2,13,32,128]{3,2,1,0:T(8,128)(2,1)S(1)}, f16[2,13,32,128]{3,2,1,0:T(8,128)(2,1)S(1)}, u32[]{:S(2)}, u32[]{:S(2)}) collective-permute-start(f16[2,13,32,128]{3,2,1,0:T(8,128)(2,1)S(1)} %multiply_convert_fusion.5), channel_id=1, source_target_pairs={{0,24},{8,16},{16,8},{24,0},{1,25},{9,17},{17,9},{25,1},{2,26},{10... | collective-permute-start | bytes 638984 | tf_op jit(solution)/shard_map/ppermute | solution.py:267
  16.9 10.6 %collective-permute-start.1 = (f16[2,13,32,128]{3,2,1,0:T(8,128)(2,1)S(1)}, f16[2,13,32,128]{3,2,1,0:T(8,128)(2,1)S(1)}, u32[]{:S(2)}, u32[]{:S(2)}) collective-permute-start(f16[2,13,32,128]{3,2,1,0:T(8,128)(2,1)S(1)} %multiply_convert_fusion.4), channel_id=1, source_target_pairs={{0,16},{8,24},{16,0},{24,8},{1,17},{9,25},{17,1},{25,9},{2,18},{10... | collective-permute-start | bytes 638984 | tf_op jit(solution)/shard_map/ppermute | solution.py:267
  18.5 9.3 %collective-permute-start.2 = (f16[2,13,32,128]{3,2,1,0:T(8,128)(2,1)}, f16[2,13,32,128]{3,2,1,0:T(8,128)(2,1)S(1)}, u32[]{:S(2)}, u32[]{:S(2)}) collective-permute-start(f16[2,13,32,128]{3,2,1,0:T(8,128)(2,1)} %multiply_convert_fusion.3), channel_id=1, source_target_pairs={{0,8},{8,0},{16,24},{24,16},{1,9},{9,1},{17,25},{25,17},{2,10},{10... | collective-permute-start | bytes 638984 | tf_op jit(solution)/shard_map/ppermute | solution.py:267
  19.9 11.8 %collective-permute-start.9 = (bf16[2,7,32,128]{3,2,1,0:T(8,128)(2,1)S(1)}, bf16[2,7,32,128]{3,2,1,0:T(8,128)(2,1)S(1)}, u32[]{:S(2)}, u32[]{:S(2)}) collective-permute-start(bf16[2,7,32,128]{3,2,1,0:T(8,128)(2,1)S(1)} %get-tuple-element.30), channel_id=1, source_target_pairs={{0,4},{1,5},{2,6},{3,7},{4,0},{5,1},{6,2},{7,3},{8,12},{9,13},{10,... | collective-permute-start | bytes 344072 | tf_op jit(solution)/shard_map/ppermute | solution.py:267
  22.6 9.2 %collective-permute-start.11 = (bf16[2,7,32,128]{3,2,1,0:T(8,128)(2,1)S(1)}, bf16[2,7,32,128]{3,2,1,0:T(8,128)(2,1)S(1)}, u32[]{:S(2)}, u32[]{:S(2)}) collective-permute-start(bf16[2,7,32,128]{3,2,1,0:T(8,128)(2,1)S(1)} %get-tuple-element.29), channel_id=1, source_target_pairs={{0,6},{1,7},{2,4},{3,5},{4,2},{5,3},{6,0},{7,1},{8,14},{9,15},{10,... | collective-permute-start | bytes 344072 | tf_op jit(solution)/shard_map/ppermute | solution.py:267
  28.0 4.5 %collective-permute-start.4 = (bf16[2,4,32,128]{3,2,1,0:T(8,128)(2,1)S(1)}, bf16[2,4,32,128]{3,2,1,0:T(8,128)(2,1)S(1)}, u32[]{:S(2)}, u32[]{:S(2)}) collective-permute-start(bf16[2,4,32,128]{3,2,1,0:T(8,128)(2,1)S(1)} %get-tuple-element.32), channel_id=1, source_target_pairs={{0,2},{1,3},{2,0},{3,1},{4,6},{5,7},{6,4},{7,5},{8,10},{9,11},{10,... | collective-permute-start | bytes 196616 | tf_op jit(solution)/shard_map/ppermute | solution.py:267
  29.6 4.2 %collective-permute-start.5 = (bf16[2,4,32,128]{3,2,1,0:T(8,128)(2,1)S(1)}, bf16[2,4,32,128]{3,2,1,0:T(8,128)(2,1)S(1)}, u32[]{:S(2)}, u32[]{:S(2)}) collective-permute-start(bf16[2,4,32,128]{3,2,1,0:T(8,128)(2,1)S(1)} %get-tuple-element.31), channel_id=1, source_target_pairs={{0,3},{1,2},{2,1},{3,0},{4,7},{5,6},{6,5},{7,4},{8,11},{9,10},{10,... | collective-permute-start | bytes 196616 | tf_op jit(solution)/shard_map/ppermute | solution.py:267
  29.6 4.2 %collective-permute-start.3 = (bf16[2,7,32,128]{3,2,1,0:T(8,128)(2,1)S(1)}, bf16[2,7,32,128]{3,2,1,0:T(8,128)(2,1)S(1)}, u32[]{:S(2)}, u32[]{:S(2)}) collective-permute-start(bf16[2,7,32,128]{3,2,1,0:T(8,128)(2,1)S(1)} %constant_dynamic-slice_fusion.4.refs_0_), channel_id=1, source_target_pairs={{0,1},{1,0},{2,3},{3,2},{4,5},{5,4},{6,7},{7,6},{8,9},{9,8},{10,11... | collective-permute-start | bytes 344072 | tf_op jit(solution)/shard_map/ppermute | solution.py:267
  31.8 2.0 %collective-permute-start.10 = (bf16[2,7,32,128]{3,2,1,0:T(8,128)(2,1)S(1)}, bf16[2,7,32,128]{3,2,1,0:T(8,128)(2,1)S(1)}, u32[]{:S(2)}, u32[]{:S(2)}) collective-permute-start(bf16[2,7,32,128]{3,2,1,0:T(8,128)(2,1)S(1)} %collective-permute-done.9.refs_4_), channel_id=1, source_target_pairs={{0,1},{1,0},{2,3},{3,2},{4,5},{5,4},{6,7},{7,6},{8,9},{9,8},{10,11... | collective-permute-start | bytes 344072 | tf_op jit(solution)/shard_map/ppermute | solution.py:267
  31.8 2.0 %collective-permute-start.12 = (bf16[2,7,32,128]{3,2,1,0:T(8,128)(2,1)S(1)}, bf16[2,7,32,128]{3,2,1,0:T(8,128)(2,1)S(1)}, u32[]{:S(2)}, u32[]{:S(2)}) collective-permute-start(bf16[2,7,32,128]{3,2,1,0:T(8,128)(2,1)S(1)} %collective-permute-done.11.refs_6_), channel_id=1, source_target_pairs={{0,1},{1,0},{2,3},{3,2},{4,5},{5,4},{6,7},{7,6},{8,9},{9,8},{10,11... | collective-permute-start | bytes 344072 | tf_op jit(solution)/shard_map/ppermute | solution.py:267
  36.3 5.8 %collective-permute-start.13 = (bf16[4,2,16,128]{3,2,1,0:T(8,128)(2,1)S(1)}, bf16[4,2,16,128]{3,2,1,0:T(8,128)(2,1)S(1)}, u32[]{:S(2)}, u32[]{:S(2)}) collective-permute-start(bf16[4,2,16,128]{3,2,1,0:T(8,128)(2,1)S(1)} %get-tuple-element.25), channel_id=1, source_target_pairs={{0,6},{1,7},{2,4},{3,5},{4,2},{5,3},{6,0},{7,1},{8,14},{9,15},{10,... | collective-permute-start | bytes 98312 | tf_op jit(solution)/shard_map/ppermute | solution.py:267
  39.1 4.9 %collective-permute-start.15 = (bf16[4,2,16,128]{3,2,1,0:T(8,128)(2,1)S(1)}, bf16[4,2,16,128]{3,2,1,0:T(8,128)(2,1)S(1)}, u32[]{:S(2)}, u32[]{:S(2)}) collective-permute-start(bf16[4,2,16,128]{3,2,1,0:T(8,128)(2,1)S(1)} %get-tuple-element.26), channel_id=1, source_target_pairs={{0,4},{1,5},{2,6},{3,7},{4,0},{5,1},{6,2},{7,3},{8,12},{9,13},{10,... | collective-permute-start | bytes 98312 | tf_op jit(solution)/shard_map/ppermute | solution.py:267
  39.6 4.4 %collective-permute-start.17 = (bf16[4,2,16,128]{3,2,1,0:T(8,128)(2,1)S(1)}, bf16[4,2,16,128]{3,2,1,0:T(8,128)(2,1)S(1)}, u32[]{:S(2)}, u32[]{:S(2)}) collective-permute-start(bf16[4,2,16,128]{3,2,1,0:T(8,128)(2,1)S(1)} %get-tuple-element.27), channel_id=1, source_target_pairs={{0,2},{1,3},{2,0},{3,1},{4,6},{5,7},{6,4},{7,5},{8,10},{9,11},{10,... | collective-permute-start | bytes 98312 | tf_op jit(solution)/shard_map/ppermute | solution.py:267
  40.8 3.7 %collective-permute-start.19 = (bf16[4,2,16,128]{3,2,1,0:T(8,128)(2,1)S(1)}, bf16[4,2,16,128]{3,2,1,0:T(8,128)(2,1)S(1)}, u32[]{:S(2)}, u32[]{:S(2)}) collective-permute-start(bf16[4,2,16,128]{3,2,1,0:T(8,128)(2,1)S(1)} %get-tuple-element.28.refs_7_), channel_id=1, source_target_pairs={{0,1},{1,0},{2,3},{3,2},{4,5},{5,4},{6,7},{7,6},{8,9},{9,8},{10,11... | collective-permute-start | bytes 98312 | tf_op jit(solution)/shard_map/ppermute | solution.py:267
  42.1 2.4 %collective-permute-start.14 = (bf16[4,2,16,128]{3,2,1,0:T(8,128)(2,1)S(1)}, bf16[4,2,16,128]{3,2,1,0:T(8,128)(2,1)S(1)}, u32[]{:S(2)}, u32[]{:S(2)}) collective-permute-start(bf16[4,2,16,128]{3,2,1,0:T(8,128)(2,1)S(1)} %collective-permute-done.13.refs_1_), channel_id=1, source_target_pairs={{0,1},{1,0},{2,3},{3,2},{4,5},{5,4},{6,7},{7,6},{8,9},{9,8},{10,11... | collective-permute-start | bytes 98312 | tf_op jit(solution)/shard_map/ppermute | solution.py:267
  43.9 1.2 %collective-permute-start.16 = (bf16[4,2,16,128]{3,2,1,0:T(8,128)(2,1)S(1)}, bf16[4,2,16,128]{3,2,1,0:T(8,128)(2,1)S(1)}, u32[]{:S(2)}, u32[]{:S(2)}) collective-permute-start(bf16[4,2,16,128]{3,2,1,0:T(8,128)(2,1)S(1)} %collective-permute-done.15.refs_3_), channel_id=1, source_target_pairs={{0,1},{1,0},{2,3},{3,2},{4,5},{5,4},{6,7},{7,6},{8,9},{9,8},{10,11... | collective-permute-start | bytes 98312 | tf_op jit(solution)/shard_map/ppermute | solution.py:267
  44.0 1.3 %collective-permute-start.18 = (bf16[4,2,16,128]{3,2,1,0:T(8,128)(2,1)S(1)}, bf16[4,2,16,128]{3,2,1,0:T(8,128)(2,1)S(1)}, u32[]{:S(2)}, u32[]{:S(2)}) collective-permute-start(bf16[4,2,16,128]{3,2,1,0:T(8,128)(2,1)S(1)} %collective-permute-done.17.refs_5_), channel_id=1, source_target_pairs={{0,1},{1,0},{2,3},{3,2},{4,5},{5,4},{6,7},{7,6},{8,9},{9,8},{10,11... | collective-permute-start | bytes 98312 | tf_op jit(solution)/shard_map/ppermute | solution.py:267

commit v10 on v9

--- a/solution.py
+++ b/solution.py
@@ -164,12 +164,12 @@
     for slot in range(slots):
         assemble(slot, 0)
         assemble(slot, 1)
-    for slot in range(slots):
-        for block in range(BLOCKS + 1):
-            columns = slice(block * LANES, (block + 1) * LANES)
-            back = slice((BLOCKS - block) * LANES, (BLOCKS - block + 1) * LANES)
-            turned = jnp.dot(both_ref[slot, :, columns], flip, preferred_element_type=F32)
-            back_ref[slot, :, back] = turned.astype(BF16)
+    for block in range(BLOCKS + 1):
+        columns = slice(block * LANES, (block + 1) * LANES)
+        back = slice((BLOCKS - block) * LANES, (BLOCKS - block + 1) * LANES)
+        ahead = both_ref[:, :, columns].reshape(slots * 2 * depth, LANES)
+        turned = jnp.dot(ahead, flip, preferred_element_type=F32).astype(BF16)
+        back_ref[:, :, back] = turned.reshape(slots, 2 * depth, LANES)
     for slot in range(slots):
         held = slice(slot * LANES, (slot + 1) * LANES)
         for block in range(BLOCKS):

time: 46.2 us -> 46.2 us (level)
  no operation moved by 1% of the time
where the time goes in v10:
time: 46.2 us; the launch traced here: 46 us
  starting transfers between devices  20.1 us (44%)
  Pallas kernels  12.1 us (26%)
  waiting for transfers between devices  11.9 us (26%)
  other arithmetic  1.3 us (3%)
    ppermute x20, starting transfers between devices, exchanged(): lax.ppermute(block, axis, [(i, i ^ step) for i in range(lax.axis_size(axi...  20.1 us
    ppermute x20, waiting for transfers between devices, exchanged(): lax.ppermute(block, axis, [(i, i ^ step) for i in range(lax.axis_size(axi...  11.9 us
    pallas_call x2, Pallas kernels, partial_beams(): pl.pallas_call(beam_kernel, in_specs=[pl.BlockSpec(memory_space=pltpu.SME...  8.92 us
    pallas_call x1, Pallas kernels, lag_profiles(): pl.pallas_call(functools.partial(lag_kernel, scale, len(pieces)), in_spec...  2.47 us
    convert_element_type x6, other arithmetic, body(): came = exchanged((partial[step] * gain).astype(jnp.float16), 'sub', step)  0.97 us
  transfers between devices with their start and end apart: 20, of which 11 were waited for; matrix products, arithmetic and copies ran while one was open for 4% of the time, Pallas kernels for 10%

profile of v10, /device:TPU:0, one launch (start us, length us, event | category | flops | bytes accessed | tf_op | source)
XLA Modules:
  0.0 46.0 jit_solution(11544857379504333041)
XLA Ops:
  0.0 4.5 %partial_beams.3 = (f32[2,13,32,128]{3,2,1,0:T(8,128)S(1)}, f32[2,13,32,128]{3,2,1,0:T(8,128)S(1)}, f32[2,13,32,128]{3,2,1,0:T(8,128)S(1)}, f32[2,13,32,128]{3,2,1,0:T(8,128)S(1)}) custom-call(s32[1]{0:T(128)} %bitcast.5.here_ref, s32[1]{0:T(128)} %bitcast.9.start_ref, bf16[100,2,540]{2,1,0:T(2,128)(2,1)} %bitcast.17, bf16[540,2,4096]{2,1,0:T(2,128)(2,1)} %bitcast.15), custom_call_target="tpu_custom_call" | custom-call | flops 920125440 | bytes 10551296 | tf_op jit(solution)/shard_map/partial_beams/pallas_call | solution.py:91
  4.5 4.0 %collective-permute-start.6 = (f16[2,13,32,128]{3,2,1,0:T(8,128)(2,1)S(1)}, f16[2,13,32,128]{3,2,1,0:T(8,128)(2,1)S(1)}, u32[]{:S(2)}, u32[]{:S(2)}) collective-permute-start(f16[2,13,32,128]{3,2,1,0:T(8,128)(2,1)S(1)} %multiply_convert_fusion.2), channel_id=1, source_target_pairs={{0,24},{8,16},{16,8},{24,0},{1,25},{9,17},{17,9},{25,1},{2,26},{10... | collective-permute-start | bytes 638984 | tf_op jit(solution)/shard_map/ppermute | solution.py:267
  8.6 0.6 %collective-permute-start.7 = (f16[2,13,32,128]{3,2,1,0:T(8,128)(2,1)S(1)}, f16[2,13,32,128]{3,2,1,0:T(8,128)(2,1)S(1)}, u32[]{:S(2)}, u32[]{:S(2)}) collective-permute-start(f16[2,13,32,128]{3,2,1,0:T(8,128)(2,1)S(1)} %multiply_convert_fusion.1), channel_id=1, source_target_pairs={{0,16},{8,24},{16,0},{24,8},{1,17},{9,25},{17,1},{25,9},{2,18},{10... | collective-permute-start | bytes 638984 | tf_op jit(solution)/shard_map/ppermute | solution.py:267
  9.3 4.5 %partial_beams.2 = (f32[2,13,32,128]{3,2,1,0:T(8,128)S(1)}, f32[2,13,32,128]{3,2,1,0:T(8,128)S(1)}, f32[2,13,32,128]{3,2,1,0:T(8,128)S(1)}, f32[2,13,32,128]{3,2,1,0:T(8,128)S(1)}) custom-call(s32[1]{0:T(128)} %bitcast.5.here_ref, s32[1]{0:T(128)} %bitcast.6.start_ref, bf16[100,2,540]{2,1,0:T(2,128)(2,1)} %bitcast.18, bf16[540,2,4096]{2,1,0:T(2,128)(2,1)} %bitcast.16), custom_call_target="tpu_custom_call" | custom-call | flops 920125440 | bytes 10551296 | tf_op jit(solution)/shard_map/partial_beams/pallas_call | solution.py:91
  13.8 3.0 %collective-permute-start = (f16[2,13,32,128]{3,2,1,0:T(8,128)(2,1)S(1)}, f16[2,13,32,128]{3,2,1,0:T(8,128)(2,1)S(1)}, u32[]{:S(2)}, u32[]{:S(2)}) collective-permute-start(f16[2,13,32,128]{3,2,1,0:T(8,128)(2,1)S(1)} %multiply_convert_fusion.5), channel_id=1, source_target_pairs={{0,24},{8,16},{16,8},{24,0},{1,25},{9,17},{17,9},{25,1},{2,26},{10... | collective-permute-start | bytes 638984 | tf_op jit(solution)/shard_map/ppermute | solution.py:267
  16.9 0.6 %collective-permute-start.1 = (f16[2,13,32,128]{3,2,1,0:T(8,128)(2,1)S(1)}, f16[2,13,32,128]{3,2,1,0:T(8,128)(2,1)S(1)}, u32[]{:S(2)}, u32[]{:S(2)}) collective-permute-start(f16[2,13,32,128]{3,2,1,0:T(8,128)(2,1)S(1)} %multiply_convert_fusion.4), channel_id=1, source_target_pairs={{0,16},{8,24},{16,0},{24,8},{1,17},{9,25},{17,1},{25,9},{2,18},{10... | collective-permute-start | bytes 638984 | tf_op jit(solution)/shard_map/ppermute | solution.py:267
  17.4 0.7 %multiply_convert_fusion.3 = f16[2,13,32,128]{3,2,1,0:T(8,128)(2,1)} fusion(f32[2,13,32,128]{3,2,1,0:T(8,128)S(1)} %get-tuple-element.20), kind=kLoop, calls=%fused_computation.5 | loop fusion | flops 212992 | bytes 638976 | tf_op jit(solution)/shard_map/convert_element_type | solution.py:311
  18.3 0.1 eq.21
  18.5 0.2 collective-permute-start.2
  18.8 0.5 %collective-permute-done.7 = f16[2,13,32,128]{3,2,1,0:T(8,128)(2,1)S(1)} collective-permute-done((f16[2,13,32,128]{3,2,1,0:T(8,128)(2,1)S(1)}, f16[2,13,32,128]{3,2,1,0:T(8,128)(2,1)S(1)}, u32[]{:S(2)}, u32[]{:S(2)}) %collective-permute-start.7) | collective-permute-done | bytes 213024 | tf_op jit(solution)/shard_map/ppermute | solution.py:267
  19.3 0.5 %collective-permute-done.8 = f16[2,13,32,128]{3,2,1,0:T(8,128)(2,1)S(1)} collective-permute-done((f16[2,13,32,128]{3,2,1,0:T(8,128)(2,1)S(1)}, f16[2,13,32,128]{3,2,1,0:T(8,128)(2,1)S(1)}, u32[]{:S(2)}, u32[]{:S(2)}) %collective-permute-start.8) | collective-permute-done | bytes 213024 | tf_op jit(solution)/shard_map/ppermute | solution.py:267
  19.8 0.1 add_convert_fusion
  19.9 2.7 %collective-permute-start.9 = (bf16[2,7,32,128]{3,2,1,0:T(8,128)(2,1)S(1)}, bf16[2,7,32,128]{3,2,1,0:T(8,128)(2,1)S(1)}, u32[]{:S(2)}, u32[]{:S(2)}) collective-permute-start(bf16[2,7,32,128]{3,2,1,0:T(8,128)(2,1)S(1)} %get-tuple-element.30), channel_id=1, source_target_pairs={{0,4},{1,5},{2,6},{3,7},{4,0},{5,1},{6,2},{7,3},{8,12},{9,13},{10,... | collective-permute-start | bytes 344072 | tf_op jit(solution)/shard_map/ppermute | solution.py:267
  22.6 1.3 %collective-permute-start.11 = (bf16[2,7,32,128]{3,2,1,0:T(8,128)(2,1)S(1)}, bf16[2,7,32,128]{3,2,1,0:T(8,128)(2,1)S(1)}, u32[]{:S(2)}, u32[]{:S(2)}) collective-permute-start(bf16[2,7,32,128]{3,2,1,0:T(8,128)(2,1)S(1)} %get-tuple-element.29), channel_id=1, source_target_pairs={{0,6},{1,7},{2,4},{3,5},{4,2},{5,3},{6,0},{7,1},{8,14},{9,15},{10,... | collective-permute-start | bytes 344072 | tf_op jit(solution)/shard_map/ppermute | solution.py:267
  24.0 3.5 %collective-permute-done.1 = f16[2,13,32,128]{3,2,1,0:T(8,128)(2,1)S(1)} collective-permute-done((f16[2,13,32,128]{3,2,1,0:T(8,128)(2,1)S(1)}, f16[2,13,32,128]{3,2,1,0:T(8,128)(2,1)S(1)}, u32[]{:S(2)}, u32[]{:S(2)}) %collective-permute-start.1) | collective-permute-done | bytes 213024 | tf_op jit(solution)/shard_map/ppermute | solution.py:267
  27.5 0.3 collective-permute-done.2
  27.8 0.1 add_convert_fusion.1
  28.0 1.7 %collective-permute-start.4 = (bf16[2,4,32,128]{3,2,1,0:T(8,128)(2,1)S(1)}, bf16[2,4,32,128]{3,2,1,0:T(8,128)(2,1)S(1)}, u32[]{:S(2)}, u32[]{:S(2)}) collective-permute-start(bf16[2,4,32,128]{3,2,1,0:T(8,128)(2,1)S(1)} %get-tuple-element.32), channel_id=1, source_target_pairs={{0,2},{1,3},{2,0},{3,1},{4,6},{5,7},{6,4},{7,5},{8,10},{9,11},{10,... | collective-permute-start | bytes 196616 | tf_op jit(solution)/shard_map/ppermute | solution.py:267
  29.6 0.6 %collective-permute-start.3 = (bf16[2,7,32,128]{3,2,1,0:T(8,128)(2,1)S(1)}, bf16[2,7,32,128]{3,2,1,0:T(8,128)(2,1)S(1)}, u32[]{:S(2)}, u32[]{:S(2)}) collective-permute-start(bf16[2,7,32,128]{3,2,1,0:T(8,128)(2,1)S(1)} %constant_dynamic-slice_fusion.4.refs_0_), channel_id=1, source_target_pairs={{0,1},{1,0},{2,3},{3,2},{4,5},{5,4},{6,7},{7,6},{8,9},{9,8},{10,11... | collective-permute-start | bytes 344072 | tf_op jit(solution)/shard_map/ppermute | solution.py:267
  30.2 1.6 %collective-permute-done.9.refs_4_ = bf16[2,7,32,128]{3,2,1,0:T(8,128)(2,1)S(1)} collective-permute-done((bf16[2,7,32,128]{3,2,1,0:T(8,128)(2,1)S(1)}, bf16[2,7,32,128]{3,2,1,0:T(8,128)(2,1)S(1)}, u32[]{:S(2)}, u32[]{:S(2)}) %collective-permute-start.9) | collective-permute-done | bytes 114720 | tf_op jit(solution)/shard_map/ppermute | solution.py:267
  31.8 0.5 %collective-permute-start.12 = (bf16[2,7,32,128]{3,2,1,0:T(8,128)(2,1)S(1)}, bf16[2,7,32,128]{3,2,1,0:T(8,128)(2,1)S(1)}, u32[]{:S(2)}, u32[]{:S(2)}) collective-permute-start(bf16[2,7,32,128]{3,2,1,0:T(8,128)(2,1)S(1)} %collective-permute-done.11.refs_6_), channel_id=1, source_target_pairs={{0,1},{1,0},{2,3},{3,2},{4,5},{5,4},{6,7},{7,6},{8,9},{9,8},{10,11... | collective-permute-start | bytes 344072 | tf_op jit(solution)/shard_map/ppermute | solution.py:267
  32.4 1.4 %collective-permute-done.5.refs_3_ = bf16[2,4,32,128]{3,2,1,0:T(8,128)(2,1)S(1)} collective-permute-done((bf16[2,4,32,128]{3,2,1,0:T(8,128)(2,1)S(1)}, bf16[2,4,32,128]{3,2,1,0:T(8,128)(2,1)S(1)}, u32[]{:S(2)}, u32[]{:S(2)}) %collective-permute-start.5) | collective-permute-done | bytes 65568 | tf_op jit(solution)/shard_map/ppermute | solution.py:267
  33.8 2.5 %lag_profiles.1 = (bf16[4,2,16,128]{3,2,1,0:T(8,128)(2,1)S(1)}, bf16[4,2,16,128]{3,2,1,0:T(8,128)(2,1)S(1)}, bf16[4,2,16,128]{3,2,1,0:T(8,128)(2,1)S(1)}, bf16[4,2,16,128]{3,2,1,0:T(8,128)(2,1)S(1)}) custom-call(s32[1]{0:T(128)} %bitcast.chip_ref, s32[1]{0:T(128)} %bitcast.1.core_ref, f32[2,32,128]{2,1,0:T(8,128)S(1)} %bitcast.14, ...), custom_call_target="tpu_custom_call" | custom-call | tf_op jit(solution)/shard_map/lag_profiles/pallas_call | solution.py:211
  36.3 2.7 %collective-permute-start.13 = (bf16[4,2,16,128]{3,2,1,0:T(8,128)(2,1)S(1)}, bf16[4,2,16,128]{3,2,1,0:T(8,128)(2,1)S(1)}, u32[]{:S(2)}, u32[]{:S(2)}) collective-permute-start(bf16[4,2,16,128]{3,2,1,0:T(8,128)(2,1)S(1)} %get-tuple-element.25), channel_id=1, source_target_pairs={{0,6},{1,7},{2,4},{3,5},{4,2},{5,3},{6,0},{7,1},{8,14},{9,15},{10,... | collective-permute-start | bytes 98312 | tf_op jit(solution)/shard_map/ppermute | solution.py:267
  39.0 0.6 %collective-permute-start.15 = (bf16[4,2,16,128]{3,2,1,0:T(8,128)(2,1)S(1)}, bf16[4,2,16,128]{3,2,1,0:T(8,128)(2,1)S(1)}, u32[]{:S(2)}, u32[]{:S(2)}) collective-permute-start(bf16[4,2,16,128]{3,2,1,0:T(8,128)(2,1)S(1)} %get-tuple-element.26), channel_id=1, source_target_pairs={{0,4},{1,5},{2,6},{3,7},{4,0},{5,1},{6,2},{7,3},{8,12},{9,13},{10,... | collective-permute-start | bytes 98312 | tf_op jit(solution)/shard_map/ppermute | solution.py:267
  39.6 1.1 %collective-permute-start.17 = (bf16[4,2,16,128]{3,2,1,0:T(8,128)(2,1)S(1)}, bf16[4,2,16,128]{3,2,1,0:T(8,128)(2,1)S(1)}, u32[]{:S(2)}, u32[]{:S(2)}) collective-permute-start(bf16[4,2,16,128]{3,2,1,0:T(8,128)(2,1)S(1)} %get-tuple-element.27), channel_id=1, source_target_pairs={{0,2},{1,3},{2,0},{3,1},{4,6},{5,7},{6,4},{7,5},{8,10},{9,11},{10,... | collective-permute-start | bytes 98312 | tf_op jit(solution)/shard_map/ppermute | solution.py:267
  40.8 1.3 %collective-permute-done.13.refs_1_ = bf16[4,2,16,128]{3,2,1,0:T(8,128)(2,1)S(1)} collective-permute-done((bf16[4,2,16,128]{3,2,1,0:T(8,128)(2,1)S(1)}, bf16[4,2,16,128]{3,2,1,0:T(8,128)(2,1)S(1)}, u32[]{:S(2)}, u32[]{:S(2)}) %collective-permute-start.13) | collective-permute-done | bytes 32800 | tf_op jit(solution)/shard_map/ppermute | solution.py:267
  42.1 1.8 %collective-permute-done.15.refs_3_ = bf16[4,2,16,128]{3,2,1,0:T(8,128)(2,1)S(1)} collective-permute-done((bf16[4,2,16,128]{3,2,1,0:T(8,128)(2,1)S(1)}, bf16[4,2,16,128]{3,2,1,0:T(8,128)(2,1)S(1)}, u32[]{:S(2)}, u32[]{:S(2)}) %collective-permute-start.15) | collective-permute-done | bytes 32800 | tf_op jit(solution)/shard_map/ppermute | solution.py:267
  44.0 0.4 collective-permute-start.18
  44.5 0.7 %collective-permute-done.16.refs_2_ = bf16[4,2,16,128]{3,2,1,0:T(8,128)(2,1)S(1)} collective-permute-done((bf16[4,2,16,128]{3,2,1,0:T(8,128)(2,1)S(1)}, bf16[4,2,16,128]{3,2,1,0:T(8,128)(2,1)S(1)}, u32[]{:S(2)}, u32[]{:S(2)}) %collective-permute-start.16) | collective-permute-done | bytes 32800 | tf_op jit(solution)/shard_map/ppermute | solution.py:267
  45.1 0.2 collective-permute-done.18.refs_4_
  45.3 0.7 %gather_beams.1 = f32[25,16,128]{2,1,0:T(8,128)} custom-call(s32[1]{0:T(128)} %bitcast.chip_ref, s32[1]{0:T(128)} %bitcast.1.core_ref, bf16[4,2,16,128]{3,2,1,0:T(8,128)(2,1)S(1)} %collective-permute-done.14.refs_0_, bf16[4,2,16,128]{3,2,1,0:T(8,128)(2,1)S(1)} %collective-permute-done.13.refs_1_, ...), custom_call_target="tpu_custom_call" | custom-call | tf_op jit(solution)/shard_map/gather_beams/pallas_call | solution.py:245
  (35 shorter events, 0.8 us)
Async XLA Ops:
  0.0 18.2 %copy-start.1 = (s32[256]{0:T(256)S(1)}, s32[256]{0:T(256)}, u32[]{:S(2)}) copy-start(s32[256]{0:T(256)} %param.7) | copy-start | bytes 3076
  4.5 14.0 %copy-start = (s32[32,16]{0,1:T(8,128)S(1)}, s32[32,16]{0,1:T(8,128)}, u32[]{:S(2)}) copy-start(s32[32,16]{0,1:T(8,128)} %param.6) | copy-start | bytes 6148
  4.5 14.0 %collective-permute-start.6 = (f16[2,13,32,128]{3,2,1,0:T(8,128)(2,1)S(1)}, f16[2,13,32,128]{3,2,1,0:T(8,128)(2,1)S(1)}, u32[]{:S(2)}, u32[]{:S(2)}) collective-permute-start(f16[2,13,32,128]{3,2,1,0:T(8,128)(2,1)S(1)} %multiply_convert_fusion.2), channel_id=1, source_target_pairs={{0,24},{8,16},{16,8},{24,0},{1,25},{9,17},{17,9},{25,1},{2,26},{10... | collective-permute-start | bytes 638984 | tf_op jit(solution)/shard_map/ppermute | solution.py:267
  8.6 10.7 %collective-permute-start.7 = (f16[2,13,32,128]{3,2,1,0:T(8,128)(2,1)S(1)}, f16[2,13,32,128]{3,2,1,0:T(8,128)(2,1)S(1)}, u32[]{:S(2)}, u32[]{:S(2)}) collective-permute-start(f16[2,13,32,128]{3,2,1,0:T(8,128)(2,1)S(1)} %multiply_convert_fusion.1), channel_id=1, source_target_pairs={{0,16},{8,24},{16,0},{24,8},{1,17},{9,25},{17,1},{25,9},{2,18},{10... | collective-permute-start | bytes 638984 | tf_op jit(solution)/shard_map/ppermute | solution.py:267
  9.2 10.6 %collective-permute-start.8 = (f16[2,13,32,128]{3,2,1,0:T(8,128)(2,1)S(1)}, f16[2,13,32,128]{3,2,1,0:T(8,128)(2,1)S(1)}, u32[]{:S(2)}, u32[]{:S(2)}) collective-permute-start(f16[2,13,32,128]{3,2,1,0:T(8,128)(2,1)S(1)} %multiply_convert_fusion), channel_id=1, source_target_pairs={{0,8},{8,0},{16,24},{24,16},{1,9},{9,1},{17,25},{25,17},{2,10},{10... | collective-permute-start | bytes 638984 | tf_op jit(solution)/shard_map/ppermute | solution.py:267
  13.8 10.1 %collective-permute-start = (f16[2,13,32,128]{3,2,1,0:T(8,128)(2,1)S(1)}, f16[2,13,32,128]{3,2,1,0:T(8,128)(2,1)S(1)}, u32[]{:S(2)}, u32[]{:S(2)}) collective-permute-start(f16[2,13,32,128]{3,2,1,0:T(8,128)(2,1)S(1)} %multiply_convert_fusion.5), channel_id=1, source_target_pairs={{0,24},{8,16},{16,8},{24,0},{1,25},{9,17},{17,9},{25,1},{2,26},{10... | collective-permute-start | bytes 638984 | tf_op jit(solution)/shard_map/ppermute | solution.py:267
  16.9 10.6 %collective-permute-start.1 = (f16[2,13,32,128]{3,2,1,0:T(8,128)(2,1)S(1)}, f16[2,13,32,128]{3,2,1,0:T(8,128)(2,1)S(1)}, u32[]{:S(2)}, u32[]{:S(2)}) collective-permute-start(f16[2,13,32,128]{3,2,1,0:T(8,128)(2,1)S(1)} %multiply_convert_fusion.4), channel_id=1, source_target_pairs={{0,16},{8,24},{16,0},{24,8},{1,17},{9,25},{17,1},{25,9},{2,18},{10... | collective-permute-start | bytes 638984 | tf_op jit(solution)/shard_map/ppermute | solution.py:267
  18.5 9.3 %collective-permute-start.2 = (f16[2,13,32,128]{3,2,1,0:T(8,128)(2,1)}, f16[2,13,32,128]{3,2,1,0:T(8,128)(2,1)S(1)}, u32[]{:S(2)}, u32[]{:S(2)}) collective-permute-start(f16[2,13,32,128]{3,2,1,0:T(8,128)(2,1)} %multiply_convert_fusion.3), channel_id=1, source_target_pairs={{0,8},{8,0},{16,24},{24,16},{1,9},{9,1},{17,25},{25,17},{2,10},{10... | collective-permute-start | bytes 638984 | tf_op jit(solution)/shard_map/ppermute | solution.py:267
  19.9 11.8 %collective-permute-start.9 = (bf16[2,7,32,128]{3,2,1,0:T(8,128)(2,1)S(1)}, bf16[2,7,32,128]{3,2,1,0:T(8,128)(2,1)S(1)}, u32[]{:S(2)}, u32[]{:S(2)}) collective-permute-start(bf16[2,7,32,128]{3,2,1,0:T(8,128)(2,1)S(1)} %get-tuple-element.30), channel_id=1, source_target_pairs={{0,4},{1,5},{2,6},{3,7},{4,0},{5,1},{6,2},{7,3},{8,12},{9,13},{10,... | collective-permute-start | bytes 344072 | tf_op jit(solution)/shard_map/ppermute | solution.py:267
  22.6 9.2 %collective-permute-start.11 = (bf16[2,7,32,128]{3,2,1,0:T(8,128)(2,1)S(1)}, bf16[2,7,32,128]{3,2,1,0:T(8,128)(2,1)S(1)}, u32[]{:S(2)}, u32[]{:S(2)}) collective-permute-start(bf16[2,7,32,128]{3,2,1,0:T(8,128)(2,1)S(1)} %get-tuple-element.29), channel_id=1, source_target_pairs={{0,6},{1,7},{2,4},{3,5},{4,2},{5,3},{6,0},{7,1},{8,14},{9,15},{10,... | collective-permute-start | bytes 344072 | tf_op jit(solution)/shard_map/ppermute | solution.py:267
  28.0 4.5 %collective-permute-start.4 = (bf16[2,4,32,128]{3,2,1,0:T(8,128)(2,1)S(1)}, bf16[2,4,32,128]{3,2,1,0:T(8,128)(2,1)S(1)}, u32[]{:S(2)}, u32[]{:S(2)}) collective-permute-start(bf16[2,4,32,128]{3,2,1,0:T(8,128)(2,1)S(1)} %get-tuple-element.32), channel_id=1, source_target_pairs={{0,2},{1,3},{2,0},{3,1},{4,6},{5,7},{6,4},{7,5},{8,10},{9,11},{10,... | collective-permute-start | bytes 196616 | tf_op jit(solution)/shard_map/ppermute | solution.py:267
  29.6 4.2 %collective-permute-start.5 = (bf16[2,4,32,128]{3,2,1,0:T(8,128)(2,1)S(1)}, bf16[2,4,32,128]{3,2,1,0:T(8,128)(2,1)S(1)}, u32[]{:S(2)}, u32[]{:S(2)}) collective-permute-start(bf16[2,4,32,128]{3,2,1,0:T(8,128)(2,1)S(1)} %get-tuple-element.31), channel_id=1, source_target_pairs={{0,3},{1,2},{2,1},{3,0},{4,7},{5,6},{6,5},{7,4},{8,11},{9,10},{10,... | collective-permute-start | bytes 196616 | tf_op jit(solution)/shard_map/ppermute | solution.py:267
  29.6 4.2 %collective-permute-start.3 = (bf16[2,7,32,128]{3,2,1,0:T(8,128)(2,1)S(1)}, bf16[2,7,32,128]{3,2,1,0:T(8,128)(2,1)S(1)}, u32[]{:S(2)}, u32[]{:S(2)}) collective-permute-start(bf16[2,7,32,128]{3,2,1,0:T(8,128)(2,1)S(1)} %constant_dynamic-slice_fusion.4.refs_0_), channel_id=1, source_target_pairs={{0,1},{1,0},{2,3},{3,2},{4,5},{5,4},{6,7},{7,6},{8,9},{9,8},{10,11... | collective-permute-start | bytes 344072 | tf_op jit(solution)/shard_map/ppermute | solution.py:267
  31.8 2.0 %collective-permute-start.10 = (bf16[2,7,32,128]{3,2,1,0:T(8,128)(2,1)S(1)}, bf16[2,7,32,128]{3,2,1,0:T(8,128)(2,1)S(1)}, u32[]{:S(2)}, u32[]{:S(2)}) collective-permute-start(bf16[2,7,32,128]{3,2,1,0:T(8,128)(2,1)S(1)} %collective-permute-done.9.refs_4_), channel_id=1, source_target_pairs={{0,1},{1,0},{2,3},{3,2},{4,5},{5,4},{6,7},{7,6},{8,9},{9,8},{10,11... | collective-permute-start | bytes 344072 | tf_op jit(solution)/shard_map/ppermute | solution.py:267
  31.8 2.0 %collective-permute-start.12 = (bf16[2,7,32,128]{3,2,1,0:T(8,128)(2,1)S(1)}, bf16[2,7,32,128]{3,2,1,0:T(8,128)(2,1)S(1)}, u32[]{:S(2)}, u32[]{:S(2)}) collective-permute-start(bf16[2,7,32,128]{3,2,1,0:T(8,128)(2,1)S(1)} %collective-permute-done.11.refs_6_), channel_id=1, source_target_pairs={{0,1},{1,0},{2,3},{3,2},{4,5},{5,4},{6,7},{7,6},{8,9},{9,8},{10,11... | collective-permute-start | bytes 344072 | tf_op jit(solution)/shard_map/ppermute | solution.py:267
  36.3 5.8 %collective-permute-start.13 = (bf16[4,2,16,128]{3,2,1,0:T(8,128)(2,1)S(1)}, bf16[4,2,16,128]{3,2,1,0:T(8,128)(2,1)S(1)}, u32[]{:S(2)}, u32[]{:S(2)}) collective-permute-start(bf16[4,2,16,128]{3,2,1,0:T(8,128)(2,1)S(1)} %get-tuple-element.25), channel_id=1, source_target_pairs={{0,6},{1,7},{2,4},{3,5},{4,2},{5,3},{6,0},{7,1},{8,14},{9,15},{10,... | collective-permute-start | bytes 98312 | tf_op jit(solution)/shard_map/ppermute | solution.py:267
  39.0 4.9 %collective-permute-start.15 = (bf16[4,2,16,128]{3,2,1,0:T(8,128)(2,1)S(1)}, bf16[4,2,16,128]{3,2,1,0:T(8,128)(2,1)S(1)}, u32[]{:S(2)}, u32[]{:S(2)}) collective-permute-start(bf16[4,2,16,128]{3,2,1,0:T(8,128)(2,1)S(1)} %get-tuple-element.26), channel_id=1, source_target_pairs={{0,4},{1,5},{2,6},{3,7},{4,0},{5,1},{6,2},{7,3},{8,12},{9,13},{10,... | collective-permute-start | bytes 98312 | tf_op jit(solution)/shard_map/ppermute | solution.py:267
  39.6 4.4 %collective-permute-start.17 = (bf16[4,2,16,128]{3,2,1,0:T(8,128)(2,1)S(1)}, bf16[4,2,16,128]{3,2,1,0:T(8,128)(2,1)S(1)}, u32[]{:S(2)}, u32[]{:S(2)}) collective-permute-start(bf16[4,2,16,128]{3,2,1,0:T(8,128)(2,1)S(1)} %get-tuple-element.27), channel_id=1, source_target_pairs={{0,2},{1,3},{2,0},{3,1},{4,6},{5,7},{6,4},{7,5},{8,10},{9,11},{10,... | collective-permute-start | bytes 98312 | tf_op jit(solution)/shard_map/ppermute | solution.py:267
  40.8 3.7 %collective-permute-start.19 = (bf16[4,2,16,128]{3,2,1,0:T(8,128)(2,1)S(1)}, bf16[4,2,16,128]{3,2,1,0:T(8,128)(2,1)S(1)}, u32[]{:S(2)}, u32[]{:S(2)}) collective-permute-start(bf16[4,2,16,128]{3,2,1,0:T(8,128)(2,1)S(1)} %get-tuple-element.28.refs_7_), channel_id=1, source_target_pairs={{0,1},{1,0},{2,3},{3,2},{4,5},{5,4},{6,7},{7,6},{8,9},{9,8},{10,11... | collective-permute-start | bytes 98312 | tf_op jit(solution)/shard_map/ppermute | solution.py:267
  42.1 2.4 %collective-permute-start.14 = (bf16[4,2,16,128]{3,2,1,0:T(8,128)(2,1)S(1)}, bf16[4,2,16,128]{3,2,1,0:T(8,128)(2,1)S(1)}, u32[]{:S(2)}, u32[]{:S(2)}) collective-permute-start(bf16[4,2,16,128]{3,2,1,0:T(8,128)(2,1)S(1)} %collective-permute-done.13.refs_1_), channel_id=1, source_target_pairs={{0,1},{1,0},{2,3},{3,2},{4,5},{5,4},{6,7},{7,6},{8,9},{9,8},{10,11... | collective-permute-start | bytes 98312 | tf_op jit(solution)/shard_map/ppermute | solution.py:267
  43.9 1.2 %collective-permute-start.16 = (bf16[4,2,16,128]{3,2,1,0:T(8,128)(2,1)S(1)}, bf16[4,2,16,128]{3,2,1,0:T(8,128)(2,1)S(1)}, u32[]{:S(2)}, u32[]{:S(2)}) collective-permute-start(bf16[4,2,16,128]{3,2,1,0:T(8,128)(2,1)S(1)} %collective-permute-done.15.refs_3_), channel_id=1, source_target_pairs={{0,1},{1,0},{2,3},{3,2},{4,5},{5,4},{6,7},{7,6},{8,9},{9,8},{10,11... | collective-permute-start | bytes 98312 | tf_op jit(solution)/shard_map/ppermute | solution.py:267
  44.0 1.3 %collective-permute-start.18 = (bf16[4,2,16,128]{3,2,1,0:T(8,128)(2,1)S(1)}, bf16[4,2,16,128]{3,2,1,0:T(8,128)(2,1)S(1)}, u32[]{:S(2)}, u32[]{:S(2)}) collective-permute-start(bf16[4,2,16,128]{3,2,1,0:T(8,128)(2,1)S(1)} %collective-permute-done.17.refs_5_), channel_id=1, source_target_pairs={{0,1},{1,0},{2,3},{3,2},{4,5},{5,4},{6,7},{7,6},{8,9},{9,8},{10,11... | collective-permute-start | bytes 98312 | tf_op jit(solution)/shard_map/ppermute | solution.py:267
